TPU v7x, 32 devices: a whole 2x2x4 slice. The times are simulated.
32 devices in a mesh: dp: 4 (over y, x), seq: 8 (over z, core).
Axes of the slice: x: 2, y: 2, z: 4, core: 2. Of those that a mesh axis runs over, the one named last changes fastest.
Arguments:
- tokens: bfloat16 [2, 4096, 1088], P(None, ('dp', 'seq')), may hold values from -6 to 6
- cotangent: bfloat16 [2, 4096, 1088], P(None, ('dp', 'seq')), may hold values from -6 to 6
- w_qkv: bfloat16 [1088, 3264], P('dp', 'seq'), may hold values from -0.1875 to 0.1875
- w_out: bfloat16 [1088, 1088], P('dp', 'seq'), may hold values from -1.5 to 1.5
- w_up: bfloat16 [1088, 4352], P('dp', 'seq'), may hold values from -0.1875 to 0.1875
- w_down: bfloat16 [4352, 1088], P('dp', 'seq'), may hold values from -0.09375 to 0.09375
- gain_one: bfloat16 [1088], P('dp'), may hold values from 0.25 to 1.75
- bias_one: bfloat16 [1088], P('dp'), may hold values from -3 to 3
- gain_two: bfloat16 [1088], P('dp'), may hold values from 0.25 to 1.75
- bias_two: bfloat16 [1088], P('dp'), may hold values from -3 to 3
- lengths: int32 [2, 4, 8], P(None, 'dp'), may hold values from 1 to 896, 1024 in all within a row
- slot_order: int32 [2, 4, 8], P(None, 'dp'), may hold values from 0 to 7, each once within a row
Outputs:
- block_out: bfloat16 [2, 4096, 1088], P(None, ('dp', 'seq'))
- grad_input: bfloat16 [2, 4096, 1088], P(None, ('dp', 'seq'))
- grad_qkv: float32 [1088, 3264], P('dp', 'seq')
- grad_proj: float32 [1088, 1088], P('dp', 'seq')
- grad_up: float32 [1088, 4352], P('dp', 'seq')
- grad_down: float32 [4352, 1088], P('dp', 'seq')
- grad_gain_one: float32 [1088], P('dp')
- grad_bias_one: float32 [1088], P('dp')
- grad_gain_two: float32 [1088], P('dp')
- grad_bias_two: float32 [1088], P('dp')
Inputs may be any that keep to these rules, and one draw needn't show every extreme that they name: For each micro-batch and group the 8 lengths sum to 1024; the largest is exactly 896. `slot_order`: each row over the last dimension holds every number below 8 once.
All inputs are finite; a program needn't handle non-finite values.
Results may differ from a plain program's by a relative error of at most 0.02.
Values may be sent and summed in bfloat16 or wider, within the bound.
A program may use at most 192 MiB of HBM per device.

v0:
```python
import jax
import jax.numpy as jnp
from jax import lax
from jax.sharding import PartitionSpec as P

HEADS = 17


EPS = 1e-05
GELU_C = 0.7978845608028654


def gelu_tanh(values):
    return 0.5 * values * (1.0 + jnp.tanh(GELU_C * (values + 0.044715 * values * values * values)))


def normalize(residual):
    row_mean = jnp.mean(residual, -1, keepdims=True)
    centered = residual - row_mean
    inv_std = lax.rsqrt(jnp.mean(centered * centered, -1, keepdims=True) + EPS)
    return (centered * inv_std, inv_std)


def norm_back(grad_normed, scaled, inv_std, gain_row):
    grad_scaled = grad_normed * gain_row
    return inv_std * (
        grad_scaled
        - jnp.mean(grad_scaled, -1, keepdims=True)
        - scaled * jnp.mean(grad_scaled * scaled, -1, keepdims=True)
    )


def running_total(counts):
    index = jnp.arange(counts.shape[0], dtype=jnp.int32)
    return jnp.sum(jnp.where(index[None, :] <= index[:, None], counts[None, :], 0), 1)


def segment_of(places, doc_ends):
    return jnp.sum((places[:, None] >= doc_ends[None, :]).astype(jnp.int32), 1)


def pair_swap(block):
    route = [(i, i ^ 1) for i in range(lax.axis_size("seq"))]
    return lax.ppermute(block, "seq", route)


def same_core():
    n_seq = lax.axis_size("seq")
    return [list(range(core, n_seq, 2)) for core in range(2)]


def gather_stack(shard):
    chips = lax.all_gather(shard, "seq", axis_index_groups=same_core())
    held = lax.all_gather(chips, "dp")
    other = pair_swap(held)
    first = lax.axis_index("seq") % 2 == 0
    both = jnp.stack([jnp.where(first, held, other), jnp.where(first, other, held)], 2)
    dp, chip_count = held.shape[:2]
    return both.transpose(1, 2, 0, 3, 4).reshape(2 * chip_count, dp, *shard.shape)


def pair_sum(parts):
    pairs = parts.reshape(parts.shape[0] // 2, 2, *parts.shape[1:])
    first = lax.axis_index("seq") % 2 == 0
    mine = jnp.where(first, pairs[:, 0], pairs[:, 1])
    other = jnp.where(first, pairs[:, 1], pairs[:, 0])
    got = pair_swap(other)
    return (mine.astype(jnp.float32) + got.astype(jnp.float32)).astype(jnp.bfloat16)


def scatter_stack(parts, after):
    held = pair_sum(parts).transpose(1, 0, 2, 3).reshape(-1, parts.shape[3])
    if after is not None:
        held, after = lax.optimization_barrier((held, after))
    held = lax.psum_scatter(held, "dp", scatter_dimension=0, tiled=True)
    held = lax.psum_scatter(
        held, "seq", scatter_dimension=0, axis_index_groups=same_core(), tiled=True
    )
    return held, after


def dot(left, right):
    return jnp.dot(left, right, preferred_element_type=jnp.float32)


def dot_right_t(left, right):
    return lax.dot_general(left, right, (((1,), (1,)), ((), ())), preferred_element_type=jnp.float32)


def dot_left_t(left, right):
    return lax.dot_general(left, right, (((0,), (0,)), ((), ())), preferred_element_type=jnp.float32)


def cols_of(rows, count):
    return rows.reshape(rows.shape[0], count, -1).transpose(1, 0, 2)


def apply_cols(rows, cols):
    lifted = jnp.broadcast_to(rows[None], (cols.shape[0],) + rows.shape)
    made = lax.dot_general(
        lifted, cols, (((2,), (1,)), ((0,), (0,))), preferred_element_type=jnp.float32
    )
    return made.transpose(1, 0, 2).reshape(rows.shape[0], -1)


def apply_cols_t(rows, cols):
    lifted = cols_of(rows, cols.shape[0])
    return lax.dot_general(
        lifted, cols, (((0, 2), (0, 2)), ((), ())), preferred_element_type=jnp.float32
    )


def grad_cols(left, right, count):
    lifted = jnp.broadcast_to(left[None], (count,) + left.shape)
    return lax.dot_general(
        lifted, cols_of(right, count), (((1,), (1,)), ((0,), (0,))),
        preferred_element_type=jnp.float32,
    )


def heads_of(rows, micro_count, head_dim):
    return rows.reshape(micro_count, -1, HEADS, head_dim).transpose(0, 2, 1, 3)


def rows_of(heads):
    micro_count, _, slots, head_dim = heads.shape
    return heads.transpose(0, 2, 1, 3).reshape(micro_count * slots, HEADS * head_dim)


def batched(left, right, left_dim, right_dim):
    return lax.dot_general(
        left,
        right,
        (((left_dim,), (right_dim,)), ((0, 1), (0, 1))),
        preferred_element_type=jnp.float32,
    )


def shards(
    tokens,
    cotangent,
    w_qkv,
    w_out,
    w_up,
    w_down,
    gain_one,
    bias_one,
    gain_two,
    bias_two,
    lengths,
    slot_order,
):
    micro_count, tok_dev, width = tokens.shape
    rows = micro_count * tok_dev
    head_dim = width // HEADS
    score_scale = head_dim ** (-0.5)
    n_seq = lax.axis_size("seq")
    my_slot = lax.axis_index("seq")
    bf16 = jnp.bfloat16

    norms = lax.all_gather(
        jnp.stack([gain_one, bias_one, gain_two, bias_two]), "dp", axis=1, tiled=True
    ).astype(jnp.float32)
    g_one, b_one, g_two, b_two = norms[0], norms[1], norms[2], norms[3]
    n_dp = lax.axis_size("dp")
    part, qkv_cols = w_qkv.shape
    out_cols = w_out.shape[1]
    up_cols = w_up.shape[1]
    fold = w_down.shape[0] // up_cols
    attn_stack = gather_stack(jnp.concatenate([w_qkv, w_out], 1))
    down_t = w_down.T
    ffn_stack = gather_stack(
        jnp.concatenate([w_up, *jnp.split(down_t, fold, 1)], 0)
    )
    cols_qkv = attn_stack[..., :qkv_cols].reshape(n_seq, width, qkv_cols)
    full_out = (
        attn_stack[..., qkv_cols:].reshape(n_seq, width, out_cols).transpose(1, 0, 2)
    ).reshape(width, width)
    cols_up = ffn_stack[:, :, :part].reshape(n_seq, width, up_cols)
    full_down_t = (
        ffn_stack[:, :, part:]
        .reshape(n_seq, n_dp, fold, out_cols, up_cols)
        .transpose(0, 3, 1, 2, 4)
        .reshape(width, fold * n_dp * up_cols)
    )

    doc_ends = jax.vmap(running_total)(lengths[:, 0])
    k_place = (
        slot_order[:, 0, :, None] * tok_dev + jnp.arange(tok_dev, dtype=jnp.int32)
    ).reshape(micro_count, n_seq * tok_dev)
    k_segment = jax.vmap(segment_of)(k_place, doc_ends)
    base_slot = lax.dynamic_slice_in_dim(slot_order[:, 0], my_slot, 1, 1)
    q_place = base_slot * tok_dev + jnp.arange(tok_dev, dtype=jnp.int32)
    q_segment = jax.vmap(segment_of)(q_place, doc_ends)
    allowed = (q_segment[:, :, None] == k_segment[:, None, :]) & (
        k_place[:, None, :] <= q_place[:, :, None]
    )

    residual = tokens.astype(jnp.float32).reshape(rows, width)
    scaled_one, inv_one = normalize(residual)
    normed_one = (scaled_one * g_one + b_one).astype(bf16)
    qkv_all = apply_cols(normed_one, cols_qkv).astype(bf16)
    queries = heads_of(qkv_all[:, :width], micro_count, head_dim)
    local_kv = qkv_all[:, width:].reshape(micro_count, tok_dev, 2 * width)
    group_kv = lax.all_gather(local_kv, "seq", axis=1, tiled=True)
    keys = heads_of(group_kv[..., :width], micro_count, head_dim)
    values = heads_of(group_kv[..., width:], micro_count, head_dim)

    scores = batched(queries, keys, 3, 3) * score_scale
    scores = jnp.where(allowed[:, None], scores, -jnp.inf)
    weights = jnp.exp(scores - jnp.max(scores, -1, keepdims=True))
    probs = weights * (1.0 / jnp.sum(weights, -1, keepdims=True))
    probs_low = probs.astype(bf16)
    attended = batched(probs_low, values, 3, 2)
    attn_flat = rows_of(attended.astype(bf16))
    middle = residual + dot(attn_flat, full_out)
    scaled_two, inv_two = normalize(middle)
    normed_two = (scaled_two * g_two + b_two).astype(bf16)
    hidden = apply_cols(normed_two, cols_up)
    activated_full, gelu_back = jax.vjp(gelu_tanh, hidden)
    activated = activated_full.astype(bf16)

    grad_rows = cotangent.reshape(rows, width)
    block_out = (middle + dot_right_t(activated, full_down_t)).astype(bf16)
    grad_hidden = gelu_back(dot(grad_rows, full_down_t))[0].astype(bf16)
    sum_down_t = dot_left_t(grad_rows, activated).astype(bf16)
    sum_down_t = (
        sum_down_t.reshape(n_seq, out_cols, n_dp, fold, up_cols)
        .transpose(0, 2, 3, 1, 4)
        .reshape(n_seq, n_dp, fold * out_cols, up_cols)
    )
    sum_up = grad_cols(normed_two, grad_hidden, n_seq).astype(bf16)
    sum_ffn, _ = scatter_stack(
        jnp.concatenate([sum_up.reshape(n_seq, n_dp, part, up_cols), sum_down_t], 2), None
    )
    grad_normed_two = apply_cols_t(grad_hidden, cols_up)
    grad_middle = grad_rows.astype(jnp.float32) + norm_back(
        grad_normed_two, scaled_two, inv_two, g_two
    )
    grad_branch = grad_middle.astype(bf16)
    sum_proj = grad_cols(attn_flat, grad_branch, n_seq).astype(bf16)
    grad_heads = heads_of(
        dot_right_t(grad_branch, full_out).astype(bf16), micro_count, head_dim
    )

    grad_probs = batched(grad_heads, values, 3, 3)
    row_dot = jnp.sum(probs * grad_probs, -1, keepdims=True)
    grad_scores = (probs * (grad_probs - row_dot)).astype(bf16)
    grad_query = rows_of(batched(grad_scores, keys, 3, 2) * score_scale)
    grad_keys = rows_of(batched(grad_scores, queries, 2, 2) * score_scale)
    grad_values = rows_of(batched(probs_low, grad_heads, 2, 2))
    grad_kv = jnp.concatenate([grad_keys.astype(bf16), grad_values.astype(bf16)], 1)
    grad_kv = grad_kv.reshape(micro_count, n_seq, tok_dev, 2 * width).transpose(1, 0, 2, 3)
    grad_kv = lax.psum_scatter(
        pair_sum(grad_kv), "seq", scatter_dimension=0, axis_index_groups=same_core()
    ).reshape(rows, 2 * width)
    grad_qkv_rows = jnp.concatenate([grad_query.astype(bf16), grad_kv], 1)
    sum_qkv = grad_cols(normed_one, grad_qkv_rows, n_seq).astype(bf16)
    sum_attn, sum_ffn = scatter_stack(
        jnp.concatenate([sum_qkv, sum_proj], 2).reshape(n_seq, n_dp, part, qkv_cols + out_cols),
        sum_ffn,
    )
    sum_attn = sum_attn.astype(jnp.float32)
    sum_ffn = sum_ffn.astype(jnp.float32)
    out_up = sum_ffn[:part]
    out_down = jnp.concatenate(jnp.split(sum_ffn[part:], fold, 0), 1).T
    out_qkv = sum_attn[:, :qkv_cols]
    out_proj = sum_attn[:, qkv_cols:]
    grad_normed_one = apply_cols_t(grad_qkv_rows, cols_qkv)
    grad_input = (
        grad_middle + norm_back(grad_normed_one, scaled_one, inv_one, g_one)
    ).astype(bf16)

    norm_sums = jnp.stack(
        [
            jnp.sum(grad_normed_one * scaled_one, 0),
            jnp.sum(grad_normed_one, 0),
            jnp.sum(grad_normed_two * scaled_two, 0),
            jnp.sum(grad_normed_two, 0),
        ]
    )
    norm_totals = lax.psum(norm_sums, ("dp", "seq"))
    norm_mine = lax.dynamic_slice_in_dim(norm_totals, lax.axis_index("dp") * part, part, 1)
    return (
        block_out.reshape(tokens.shape),
        grad_input.reshape(tokens.shape),
        out_qkv,
        out_proj,
        out_up,
        out_down,
        norm_mine[0],
        norm_mine[1],
        norm_mine[2],
        norm_mine[3],
    )


def solution(mesh):
    return jax.shard_map(
        shards,
        mesh=mesh,
        in_specs=(
            P(None, ("dp", "seq"), None),
            P(None, ("dp", "seq"), None),
            P("dp", "seq"),
            P("dp", "seq"),
            P("dp", "seq"),
            P("dp", "seq"),
            P("dp"),
            P("dp"),
            P("dp"),
            P("dp"),
            P(None, "dp", None),
            P(None, "dp", None),
        ),
        out_specs=(
            P(None, ("dp", "seq"), None),
            P(None, ("dp", "seq"), None),
            P("dp", "seq"),
            P("dp", "seq"),
            P("dp", "seq"),
            P("dp", "seq"),
            P("dp"),
            P("dp"),
            P("dp"),
            P("dp"),
        ),
        check_vma=False,
    )
```

profile of v0, /device:TPU:0, one launch (start us, length us, event | category | flops | bytes accessed | tf_op | source)
XLA Modules:
  0.0 990.3 jit_solution(6537300546122881620)
XLA Ops:
  13.4 33.8 %all-gather.13.cloned.1.call-done = bf16[1088,544]{1,0:T(8,128)(2,1)} async-done(((bf16[272,544]{1,0:T(8,128)(2,1)}), bf16[1088,544]{1,0:T(8,128)(2,1)}) %all-gather.13.cloned.1.call-update) | async-done | bytes 1183760 | tf_op jit(solution)/shard_map/all_gather | solution.py:53
  47.3 58.6 %all-gather.17.cloned.1.call-done = bf16[2176,544]{1,0:T(8,128)(2,1)} async-done(((bf16[544,544]{1,0:T(8,128)(2,1)}), bf16[2176,544]{1,0:T(8,128)(2,1)}) %all-gather.17.cloned.1.call-update) | async-done | bytes 2367504 | tf_op jit(solution)/shard_map/all_gather | solution.py:53
  105.9 64.7 %all-gather.15.cloned.1.call-done = bf16[16,272,544]{2,1,0:T(8,128)(2,1)} async-done(((bf16[4,272,544]{2,1,0:T(8,128)(2,1)}), bf16[16,272,544]{2,1,0:T(8,128)(2,1)}) %all-gather.15.cloned.1.call-update) | async-done | bytes 4734992 | tf_op jit(solution)/shard_map/all_gather | solution.py:54
  170.7 8.1 all-gather.4
  180.0 11.1 %select_bitcast_fusion.3 = (bf16[4,4,1,272,544]{4,3,1,0,2:T(8,128)(2,1)}, bf16[4,4,1,272,544]{4,3,1,0,2:T(8,128)(2,1)}) fusion(bf16[4,4,272,544]{3,2,1,0:T(8,128)(2,1)} %bitcast.351, bf16[4,4,272,544]{3,2,1,0:T(8,128)(2,1)} %collective-permute-done, pred[]{:T(512)S(6)} %eq.33), kind=kLoop, calls=%fused_computation.48 | loop fusion | flops 4734976 | bytes 18939904 | tf_op jit(solution)/shard_map/stack | solution.py:57
  191.1 6.8 maximum_bitcast_fusion.1
  198.0 5.7 copy.210
  203.7 7.7 slice.118
  211.3 6.4 fusion.42
  218.9 63.9 %all-gather.19.cloned.1.call-done = bf16[16,544,544]{2,1,0:T(8,128)(2,1)} async-done(((bf16[4,544,544]{2,1,0:T(8,128)(2,1)}), bf16[16,544,544]{2,1,0:T(8,128)(2,1)}) %all-gather.19.cloned.1.call-update) | async-done | bytes 9469968 | tf_op jit(solution)/shard_map/all_gather | solution.py:54
  284.5 7.0 slice.115
  291.6 6.7 copy.249
  300.3 9.0 select_bitcast_fusion.1
  309.3 10.5 %maximum_bitcast_fusion = bf16[4,2,4,544,544]{4,3,0,2,1:T(8,128)(2,1)} fusion(bf16[4,4,1,544,544]{4,3,1,0,2:T(8,128)(2,1)S(1)} %get-tuple-element.93, bf16[4,4,1,544,544]{4,3,1,0,2:T(8,128)(2,1)S(1)} %get-tuple-element.92), kind=kLoop, calls=%fused_computation.1 | loop fusion | flops 9469952 | bytes 37879808 | tf_op jit(solution)/shard_map/transpose | solution.py:59
  319.8 11.9 %copy.216 = bf16[4,2,4,544,544]{4,3,2,1,0:T(8,128)(2,1)S(1)} copy(bf16[4,2,4,544,544]{4,3,0,2,1:T(8,128)(2,1)} %maximum_bitcast_fusion) | data formatting | bytes 37879808 | tf_op jit(solution)/shard_map/transpose | solution.py:59
  331.8 9.0 fusion.82
  340.8 16.9 %copy.218 = bf16[8,136,4,2,544]{4,3,2,1,0:T(2,128)(2,1)} copy(bf16[8,136,4,2,544]{4,1,3,2,0:T(8,128)(2,1)} %bitcast.326) | data formatting | bytes 18939904 | tf_op jit(solution)/shard_map/transpose | solution.py:183
  357.7 23.4 %reshape.359 = bf16[1088,4352]{1,0:T(8,128)(2,1)} reshape(bf16[8,136,4,2,544]{4,3,2,1,0:T(2,128)(2,1)} %copy.218) | data formatting | bytes 18939904 | tf_op jit(solution)/shard_map/reshape | solution.py:184
  381.1 8.1 fusion.83
  389.2 11.8 %fusion.86 = (f32[2,17,128]{2,1,0:T(8,128)S(1)}, f32[2,17,128,1024]{3,2,1,0:T(8,128)}) fusion(pred[2,128,1024]{2,1,0:T(8,128)(4,1)S(1)} %copy-done.20, bf16[2,17,1024,64]{2,3,1,0:T(8,128)(2,1)} %bitcast.337, bf16[2,128,17,64]{1,0,3,2:T(2,128)(2,1)S(1)} %reshape.349), kind=kOutput, calls=%fused_computation.178 | convolution fusion | flops 588252160 | bytes 23118848 | tf_op jit(solution)/shard_map/sub | solution.py:211
  401.1 9.4 fusion.49
  412.6 11.4 %fusion.24 = (bf16[256,8,544]{0,2,1:T(8,128)(2,1)}, f32[8,256,544]{1,2,0:T(8,128)}) fusion(bf16[8,1088,544]{2,1,0:T(8,128)(2,1)} %bitcast.342, bf16[256,1088]{0,1:T(8,128)(2,1)S(1)} %add_convert_fusion.1), kind=kOutput, calls=%fused_computation.57 | convolution fusion | flops 2434334720 | bytes 16711680 | tf_op jit(solution)/shard_map/dot_general | solution.py:100
  427.6 9.4 fusion.19
  446.1 10.0 %fusion.33 = bf16[2,17,1024,64]{2,3,1,0:T(8,128)(2,1)} fusion(f32[2,17,128,1024]{3,2,1,0:T(8,128)} %get-tuple-element.105, f32[2,17,128]{2,1,0:T(8,128)S(1)} %broadcast_divide_fusion, bf16[2,128,17,64]{1,0,3,2:T(2,128)(2,1)S(1)} %reshape.364), kind=kOutput, calls=%fused_computation.74 | convolution fusion | flops 581566464 | bytes 22856704 | tf_op jit(solution)/shard_map/dot_general | solution.py:131
  456.1 11.2 %multiply_reduce_fusion = (f32[2,17,128]{2,1,0:T(8,128)S(1)}, f32[2,17,128,1024]{3,2,1,0:T(8,128)}) fusion(f32[2,17,128,1024]{3,2,1,0:T(8,128)} %get-tuple-element.105, f32[2,17,128]{2,1,0:T(8,128)S(1)} %broadcast_divide_fusion, bf16[2,17,1024,64]{2,3,1,0:T(8,128)(2,1)S(1)} %bitcast.331, bf16[2,128,17,64]{1,0,3,2:T(2,128)(2,1)S(1)} %reshape.364), kind=kOutput, calls=%fused_computation.9 | convolution fusion | flops 583790336 | bytes 40699904 | tf_op jit(solution)/shard_map/dot_general | solution.py:131
  472.7 6.8 copy.224
  479.5 12.1 %multiply_convert_fusion = bf16[2,17,128,1024]{3,2,1,0:T(8,128)(2,1)S(1)} fusion(f32[2,17,128,1024]{3,2,1,0:T(8,128)} %get-tuple-element.112, f32[2,17,128,1024]{3,2,1,0:T(8,128)} %get-tuple-element.105, f32[2,17,128]{2,1,0:T(8,128)S(1)} %get-tuple-element.111, f32[2,17,128]{2,1,0:T(8,128)S(1)} %broadcast_divide_fusion), kind=kLoop, calls=%fused_computation.8 | loop fusion | flops 17825792 | bytes 44599296 | tf_op jit(solution)/shard_map/convert_element_type | solution.py:248
  498.3 6.9 copy.223
  505.2 6.6 pad_maximum_fusion.2
  522.1 29.8 %reshape.370 = bf16[8,136,4,2,544]{4,3,2,1,0:T(2,128)(2,1)} reshape(bf16[1088,4352]{1,0:T(8,128)(2,1)} %fusion.2) | data formatting | bytes 18939904 | tf_op jit(solution)/shard_map/reshape | solution.py:228
  552.0 11.5 %copy.234 = bf16[8,136,4,2,544]{4,1,3,2,0:T(8,128)(2,1)} copy(bf16[8,136,4,2,544]{4,3,2,1,0:T(2,128)(2,1)} %reshape.370) | data formatting | bytes 18939904 | tf_op jit(solution)/shard_map/reshape | solution.py:228
  569.1 14.3 %copy.233 = bf16[8,1088,544]{2,1,0:T(8,128)(2,1)} copy(bf16[8,1088,544]{1,2,0:T(8,128)(2,1)} %convolution_convert_fusion.2) | data formatting | bytes 18939904 | tf_op jit(solution)/shard_map/convert_element_type | solution.py:232
  583.4 16.0 %fusion.4 = bf16[4,4,544,544]{3,2,1,0:T(8,128)(2,1)} fusion(pred[]{:T(512)S(6)} %eq.33, bf16[4,2,4,272,544]{4,3,2,1,0:T(8,128)(2,1)} %bitcast.317, bf16[4,2,4,272,544]{4,3,2,1,0:T(8,128)(2,1)} %bitcast.313), kind=kLoop, calls=%fused_computation.17 | loop fusion | flops 42614784 | bytes 28409856 | tf_op jit(solution)/shard_map/jit(_where)/select_n | solution.py:66
  604.7 12.2 %collective-permute-done.4 = bf16[4,4,544,544]{3,2,1,0:T(8,128)(2,1)} collective-permute-done((bf16[4,4,544,544]{3,2,1,0:T(8,128)(2,1)}, bf16[4,4,544,544]{3,2,1,0:T(8,128)(2,1)}, u32[]{:S(2)}, u32[]{:S(2)}) %collective-permute-start.4) | collective-permute-done | bytes 9469984 | tf_op jit(solution)/shard_map/ppermute | solution.py:44
  616.9 12.9 %fusion.5 = bf16[4,4,544,544]{3,2,0,1:T(8,128)(2,1)S(1)} fusion(bf16[4,4,544,544]{3,2,1,0:T(8,128)(2,1)} %collective-permute-done.4, pred[]{:T(512)S(6)} %eq.33, bf16[4,2,4,272,544]{4,3,2,1,0:T(8,128)(2,1)} %bitcast.318, bf16[4,2,4,272,544]{4,3,2,1,0:T(8,128)(2,1)} %bitcast.314), kind=kLoop, calls=%fused_computation.18 | loop fusion | flops 61554688 | bytes 37879808 | tf_op jit(solution)/shard_map/transpose | solution.py:72
  629.9 5.7 copy.254
  636.6 8.0 fusion.50
  648.3 37.7 %reduce-scatter.10.cloned.1.call-done = bf16[1,2,128,2176]{3,2,1,0:T(8,128)(2,1)} async-done(((bf16[4,2,128,2176]{3,2,1,0:T(8,128)(2,1)}), bf16[1,2,128,2176]{3,2,1,0:T(8,128)(2,1)}) %reduce-scatter.10.cloned.1.call-update) | async-done | bytes 1114128 | tf_op jit(solution)/shard_map/reduce_scatter | solution.py:254
  690.2 6.5 pad_maximum_fusion.1
  696.7 14.5 %copy.227 = bf16[8,1088,544]{2,1,0:T(8,128)(2,1)} copy(bf16[8,1088,544]{1,2,0:T(8,128)(2,1)} %pad_maximum_fusion.1) | data formatting | bytes 18939904 | tf_op jit(solution)/shard_map/concatenate | solution.py:260
  711.3 7.5 fusion.13
  718.7 79.8 %reduce-scatter.16.cloned.1.call-done = bf16[2176,544]{1,0:T(8,128)(2,1)} async-done(((bf16[8704,544]{1,0:T(8,128)(2,1)}), bf16[2176,544]{1,0:T(8,128)(2,1)}) %reduce-scatter.16.cloned.1.call-update) | async-done | bytes 2367504
  798.6 10.5 %fusion.14 = bf16[4,4,272,544]{3,2,0,1:T(8,128)(2,1)} fusion(bf16[4,4,272,544]{3,2,1,0:T(8,128)(2,1)} %collective-permute-done.3, pred[]{:T(512)S(6)} %eq.33, bf16[4,2,4,272,544]{4,3,2,1,0:T(8,128)(2,1)} %bitcast.316), kind=kLoop, calls=%fused_computation.44 | loop fusion | flops 11837440 | bytes 18939904 | tf_op jit(solution)/shard_map/transpose | solution.py:72
  814.6 41.0 %reduce-scatter.18.cloned.1.call-done = bf16[544,544]{1,0:T(8,128)(2,1)} async-done(((bf16[2176,544]{1,0:T(8,128)(2,1)}), bf16[544,544]{1,0:T(8,128)(2,1)}) %reduce-scatter.18.cloned.1.call-update) | async-done | bytes 591888
  858.4 7.0 fusion.51
  866.3 56.6 %reduce-scatter.12.cloned.1.call-done = bf16[1088,544]{1,0:T(8,128)(2,1)} async-done(((bf16[4352,544]{1,0:T(8,128)(2,1)}), bf16[1088,544]{1,0:T(8,128)(2,1)}) %reduce-scatter.12.cloned.1.call-update) | async-done | bytes 1183760 | tf_op jit(solution)/shard_map/reduce_scatter | solution.py:75
  923.0 8.4 multiply_reduce_fusion.2
  931.4 41.1 %psum.7 = f32[4,1088]{1,0:T(4,128)S(1)} all-reduce(f32[4,1088]{1,0:T(4,128)S(1)} %pad_maximum_fusion.6), channel_id=1, replica_groups=mesh['dp'=4,'seq'=8] {'dp','seq'}, use_global_device_ids=true, to_apply=%region_23.24 | all-reduce | flops 4352 | bytes 34816 | tf_op jit(solution)/shard_map/psum | solution.py:282
  (219 shorter events, 88.9 us)
Async XLA Ops:
  7.2 420.1 %copy-start = (bf16[2,128,1088]{1,2,0:T(8,128)(2,1)S(1)}, bf16[2,128,1088]{1,2,0:T(8,128)(2,1)}, u32[]{:S(2)}) copy-start(bf16[2,128,1088]{1,2,0:T(8,128)(2,1)} %param.13) | copy-start | bytes 1671172
  7.2 163.4 %copy-start.41 = (bf16[272]{0:T(512)(128)(2,1)S(1)}, bf16[272]{0:T(512)(128)(2,1)}, u32[]{:S(2)}) copy-start(bf16[272]{0:T(512)(128)(2,1)} %param.21) | copy-start | bytes 1636
  7.2 163.4 %copy-start.42 = (bf16[272]{0:T(512)(128)(2,1)S(1)}, bf16[272]{0:T(512)(128)(2,1)}, u32[]{:S(2)}) copy-start(bf16[272]{0:T(512)(128)(2,1)} %param.20) | copy-start | bytes 1636
  7.2 163.4 %copy-start.43 = (bf16[272]{0:T(512)(128)(2,1)S(1)}, bf16[272]{0:T(512)(128)(2,1)}, u32[]{:S(2)}) copy-start(bf16[272]{0:T(512)(128)(2,1)} %param.19) | copy-start | bytes 1636
  7.2 163.4 %copy-start.44 = (bf16[272]{0:T(512)(128)(2,1)S(1)}, bf16[272]{0:T(512)(128)(2,1)}, u32[]{:S(2)}) copy-start(bf16[272]{0:T(512)(128)(2,1)} %param.18) | copy-start | bytes 1636
  7.2 171.7 %copy-start.5 = (bf16[2,128,1088]{1,2,0:T(8,128)(2,1)S(1)}, bf16[2,128,1088]{1,2,0:T(8,128)(2,1)}, u32[]{:S(2)}) copy-start(bf16[2,128,1088]{1,2,0:T(8,128)(2,1)} %param.12) | copy-start | bytes 1671172
  7.2 39.9 %all-gather.13.cloned.1.call-start = ((), (), s32[]{:S(2)}) async-start(), calls=%async_computation.9 | async-start | bytes 1740800 | tf_op jit(solution)/shard_map/all_gather | solution.py:53
  10.2 95.6 %all-gather.17.cloned.1.call-start = ((), (), s32[]{:S(2)}) async-start(), calls=%async_computation.11 | async-start | bytes 3481600 | tf_op jit(solution)/shard_map/all_gather | solution.py:53
  13.3 157.3 %all-gather.15.cloned.1.call-start = ((), (), s32[]{:S(2)}) async-start(), calls=%async_computation.10 | async-start | bytes 6963200 | tf_op jit(solution)/shard_map/all_gather | solution.py:54
  47.2 235.6 %all-gather.19.cloned.1.call-start = ((), (), s32[]{:S(2)}) async-start(), calls=%async_computation.12 | async-start | bytes 13926400 | tf_op jit(solution)/shard_map/all_gather | solution.py:54
  105.8 275.3 %all-gather.11.cloned.1.call-start = ((), (), s32[]{:S(2)}) async-start(), calls=%async_computation.5 | async-start | bytes 10027008 | tf_op jit(solution)/shard_map/all_gather | solution.py:205
  170.6 9.5 collective-permute-start
  178.9 12.2 %copy-start.23 = (f32[1088]{0:T(1024)}, f32[1088]{0:T(1024)S(1)}, u32[]{:S(2)}) copy-start(f32[1088]{0:T(1024)S(1)} %get-tuple-element.89) | copy-start | bytes 13060
  179.0 262.0 %copy-start.21 = (f32[1088]{0:T(1024)}, f32[1088]{0:T(1024)S(1)}, u32[]{:S(2)}) copy-start(f32[1088]{0:T(1024)S(1)} %get-tuple-element.86) | copy-start | bytes 13060
  179.1 12.0 %copy-start.33 = (f32[256]{0:T(256)}, f32[256]{0:T(256)S(1)}, u32[]{:S(2)}) copy-start(f32[256]{0:T(256)S(1)} %get-tuple-element.102) | copy-start | bytes 3076
  179.3 11.8 %copy-start.35 = (f32[256]{0:T(256)}, f32[256]{0:T(256)S(1)}, u32[]{:S(2)}) copy-start(f32[256]{0:T(256)S(1)} %rsqrt_bitcast_fusion) | copy-start | bytes 3076
  179.7 31.6 %copy-start.14 = (bf16[256,1088]{0,1:T(8,128)(2,1)}, bf16[256,1088]{0,1:T(8,128)(2,1)S(1)}, u32[]{:S(2)}) copy-start(bf16[256,1088]{0,1:T(8,128)(2,1)S(1)} %add_convert_fusion.2) | copy-start | bytes 1671172
  211.3 71.5 %copy-start.39 = (s32[2,1,8]{2,1,0:T(1,128)S(1)}, s32[2,1,8]{2,1,0:T(1,128)}, u32[]{:S(2)}) copy-start(s32[2,1,8]{2,1,0:T(1,128)} %param.23) | copy-start | bytes 196
  211.3 71.7 %copy-start.40 = (s32[2,1,8]{2,1,0:T(1,128)S(1)}, s32[2,1,8]{2,1,0:T(1,128)}, u32[]{:S(2)}) copy-start(s32[2,1,8]{2,1,0:T(1,128)} %param.22) | copy-start | bytes 196
  218.8 467.1 %reduce-scatter.10.cloned.1.call-start = ((), (), s32[]{:S(2)}) async-start(), calls=%async_computation.6 | async-start | bytes 5570560 | tf_op jit(solution)/shard_map/reduce_scatter | solution.py:254
  282.8 17.4 %collective-permute-start.1 = (bf16[4,4,544,544]{3,2,1,0:T(8,128)(2,1)}, bf16[4,4,544,544]{3,2,1,0:T(8,128)(2,1)}, u32[]{:S(2)}, u32[]{:S(2)}) collective-permute-start(bf16[4,4,544,544]{3,2,1,0:T(8,128)(2,1)} %bitcast.340), channel_id=1, source_target_pairs={{0,1},{1,0},{2,3},{3,2},{4,5},{5,4},{6,7},{7,6},{8,9},{9,8},{10,11... | collective-permute-start | bytes 28409864 | tf_op jit(solution)/shard_map/ppermute | solution.py:44
  412.0 28.9 %copy-start.3 = (f32[256,1088]{0,1:T(8,128)}, f32[256,1088]{0,1:T(8,128)S(1)}, u32[]{:S(2)}) copy-start(f32[256,1088]{0,1:T(8,128)S(1)} %get-tuple-element.107) | copy-start | bytes 3342340
  412.0 28.9 %copy-start.25 = (f32[256]{0:T(256)}, f32[256]{0:T(256)S(1)}, u32[]{:S(2)}) copy-start(f32[256]{0:T(256)S(1)} %broadcast_multiply_fusion.4) | copy-start | bytes 3076
  412.2 28.7 %copy-start.27 = (f32[256]{0:T(256)}, f32[256]{0:T(256)S(1)}, u32[]{:S(2)}) copy-start(f32[256]{0:T(256)S(1)} %add_rsqrt_fusion) | copy-start | bytes 3076
  424.0 13.0 %slice-start.5 = ((s8[11141120]{0:T(1024)(128)(4,1)}), s8[4194304]{0:T(1024)(128)(4,1)S(1)}, s32[]{:S(2)}) async-start(s8[11141120]{0:T(1024)(128)(4,1)} %bitcast.343), calls=%async_computation.20 | async-start | bytes 8388608
  441.9 14.2 %slice-start.3 = ((s8[4456448]{0:T(1024)(128)(4,1)}), s8[262144]{0:T(1024)(128)(4,1)S(1)}, s32[]{:S(2)}) async-start(s8[4456448]{0:T(1024)(128)(4,1)} %bitcast.329), calls=%async_computation.18 | async-start | bytes 524288
  516.9 83.0 %collective-permute-start.2 = (bf16[4,2,128,2176]{3,2,1,0:T(8,128)(2,1)}, bf16[4,2,128,2176]{3,2,1,0:T(8,128)(2,1)}, u32[]{:S(2)}, u32[]{:S(2)}) collective-permute-start(bf16[4,2,128,2176]{3,2,1,0:T(8,128)(2,1)} %select_bitcast_fusion.4), channel_id=1, source_target_pairs={{0,1},{1,0},{2,3},{3,2},{4,5},{5,4},{6,7},{7,6},{8,9},{9,8},{10,11... | collective-permute-start | bytes 13369352 | tf_op jit(solution)/shard_map/ppermute | solution.py:44
  552.0 11.5 %copy-start.17 = (bf16[256,4352]{0,1:T(8,128)(2,1)S(1)}, bf16[256,4352]{0,1:T(8,128)(2,1)}, u32[]{:S(2)}) copy-start(bf16[256,4352]{0,1:T(8,128)(2,1)} %copy-done.16) | copy-start | bytes 6684676
  583.4 16.4 %slice-start = ((s8[8912896]{0:T(1024)(128)(4,1)}), s8[4194304]{0:T(1024)(128)(4,1)S(1)}, s32[]{:S(2)}) async-start(s8[8912896]{0:T(1024)(128)(4,1)} %bitcast.321), calls=%async_computation.15 | async-start | bytes 8388608
  583.4 16.4 %slice-start.1 = ((s8[8912896]{0:T(1024)(128)(4,1)}), s8[4194304]{0:T(1024)(128)(4,1)S(1)}, s32[]{:S(2)}) async-start(s8[8912896]{0:T(1024)(128)(4,1)} %bitcast.321), calls=%async_computation.16 | async-start | bytes 8388608
  583.4 16.4 %slice-start.2 = ((s8[8912896]{0:T(1024)(128)(4,1)}), s8[524288]{0:T(1024)(128)(4,1)S(1)}, s32[]{:S(2)}) async-start(s8[8912896]{0:T(1024)(128)(4,1)} %bitcast.321), calls=%async_computation.17 | async-start | bytes 1048576
  599.5 17.4 %collective-permute-start.4 = (bf16[4,4,544,544]{3,2,1,0:T(8,128)(2,1)}, bf16[4,4,544,544]{3,2,1,0:T(8,128)(2,1)}, u32[]{:S(2)}, u32[]{:S(2)}) collective-permute-start(bf16[4,4,544,544]{3,2,1,0:T(8,128)(2,1)} %fusion.4), channel_id=1, source_target_pairs={{0,1},{1,0},{2,3},{3,2},{4,5},{5,4},{6,7},{7,6},{8,9},{9,8},{10,11... | collective-permute-start | bytes 28409864 | tf_op jit(solution)/shard_map/ppermute | solution.py:44
  604.6 193.9 %reduce-scatter.16.cloned.1.call-start = ((), (), s32[]{:S(2)}) async-start(), calls=%async_computation.13 | async-start | bytes 13926400
  635.5 220.0 %reduce-scatter.18.cloned.1.call-start = ((), (), s32[]{:S(2)}) async-start(), calls=%async_computation.14 | async-start | bytes 3481600
  645.3 42.5 %copy-start.15 = (bf16[256,1088]{0,1:T(8,128)(2,1)S(1)}, bf16[256,1088]{0,1:T(8,128)(2,1)}, u32[]{:S(2)}) copy-start(bf16[256,1088]{0,1:T(8,128)(2,1)} %copy-done.14) | copy-start | bytes 1671172
  718.7 79.9 %collective-permute-start.3 = (bf16[4,4,272,544]{3,2,1,0:T(8,128)(2,1)}, bf16[4,4,272,544]{3,2,1,0:T(8,128)(2,1)}, u32[]{:S(2)}, u32[]{:S(2)}) collective-permute-start(bf16[4,4,272,544]{3,2,1,0:T(8,128)(2,1)} %fusion.13), channel_id=1, source_target_pairs={{0,1},{1,0},{2,3},{3,2},{4,5},{5,4},{6,7},{7,6},{8,9},{9,8},{10,11... | collective-permute-start | bytes 14204936 | tf_op jit(solution)/shard_map/ppermute | solution.py:44
  798.6 124.3 %reduce-scatter.12.cloned.1.call-start = ((), (), s32[]{:S(2)}) async-start(), calls=%async_computation.7 | async-start | bytes 6963200 | tf_op jit(solution)/shard_map/reduce_scatter | solution.py:75
  814.6 42.7 %copy-start.6 = (bf16[2,128,1088]{1,2,0:T(8,128)(2,1)S(1)}, bf16[2,128,1088]{1,2,0:T(8,128)(2,1)}, u32[]{:S(2)}) copy-start(bf16[2,128,1088]{1,2,0:T(8,128)(2,1)} %param.12) | copy-start | bytes 1671172
  814.6 43.8 %copy-start.4 = (f32[256,1088]{0,1:T(8,128)S(1)}, f32[256,1088]{0,1:T(8,128)}, u32[]{:S(2)}) copy-start(f32[256,1088]{0,1:T(8,128)} %copy-done.3) | copy-start | bytes 3342340
  857.0 122.3 %reduce-scatter.14.cloned.1.call-start = ((), (), s32[]{:S(2)}) async-start(), calls=%async_computation.8 | async-start | bytes 1740800 | tf_op jit(solution)/shard_map/reduce_scatter | solution.py:76
  858.4 64.5 %copy-start.24 = (f32[1088]{0:T(1024)S(1)}, f32[1088]{0:T(1024)}, u32[]{:S(2)}) copy-start(f32[1088]{0:T(1024)} %copy-done.23) | copy-start | bytes 13060
  858.4 64.5 %copy-start.34 = (f32[256]{0:T(256)S(1)}, f32[256]{0:T(256)}, u32[]{:S(2)}) copy-start(f32[256]{0:T(256)} %copy-done.33) | copy-start | bytes 3076
  858.4 64.5 %copy-start.36 = (f32[256]{0:T(256)S(1)}, f32[256]{0:T(256)}, u32[]{:S(2)}) copy-start(f32[256]{0:T(256)} %copy-done.35) | copy-start | bytes 3076
  923.0 50.2 %copy-start.22 = (f32[1088]{0:T(1024)S(1)}, f32[1088]{0:T(1024)}, u32[]{:S(2)}) copy-start(f32[1088]{0:T(1024)} %copy-done.21) | copy-start | bytes 13060
  923.0 50.2 %copy-start.26 = (f32[256]{0:T(256)S(1)}, f32[256]{0:T(256)}, u32[]{:S(2)}) copy-start(f32[256]{0:T(256)} %copy-done.25) | copy-start | bytes 3076
  923.0 50.2 %copy-start.28 = (f32[256]{0:T(256)S(1)}, f32[256]{0:T(256)}, u32[]{:S(2)}) copy-start(f32[256]{0:T(256)} %copy-done.27) | copy-start | bytes 3076
  923.0 50.2 %copy-start.30 = (f32[256]{0:T(256)S(1)}, f32[256]{0:T(256)}, u32[]{:S(2)}) copy-start(f32[256]{0:T(256)} %copy-done.29) | copy-start | bytes 3076
  923.0 50.2 %copy-start.32 = (f32[256]{0:T(256)S(1)}, f32[256]{0:T(256)}, u32[]{:S(2)}) copy-start(f32[256]{0:T(256)} %copy-done.31) | copy-start | bytes 3076
  (20 other events, 107.2 us)
Sparse Core Ops, SparseCore 0:
  10.3 36.7 all-gather.12
  49.3 56.4 all-gather.16
  107.7 62.8 all-gather.14
  172.3 110.5 all-gather.18
  284.3 86.8 all-gather.10
  604.8 81.1 reduce-scatter.9
  689.1 109.3 reduce-scatter.15
  800.9 54.6 reduce-scatter.17
  858.9 63.9 reduce-scatter.11
  925.2 33.3 reduce-scatter.13
where the time goes:
time: 1000 us; the launch traced here: 990 us
  waiting for transfers between devices  451 us (45%)
  local copies, waits for them, and re-layouts  225 us (22%)
  other arithmetic  132 us (13%)
  matrix products  117 us (12%)
  blocking collectives  49.2 us (5%)
  between operations  15.5 us (2%)
    all_gather x2, waiting for transfers between devices, gather_stack(): held = lax.all_gather(chips, 'dp')  129 us
    unnamed x12, waiting for transfers between devices  121 us
    all_gather x2, waiting for transfers between devices, gather_stack(): chips = lax.all_gather(shard, 'seq', axis_index_groups=same_core())  92.4 us
    reduce_scatter x1, waiting for transfers between devices, scatter_stack(): held = lax.psum_scatter(held, 'dp', scatter_dimension=0, tiled=True)  56.6 us
    reshape x2, local copies, waits for them, and re-layouts, shards(): sum_down_t.reshape(n_seq, out_cols, n_dp, fold, up_cols)  41.4 us
    psum x1, blocking collectives, shards(): norm_totals = lax.psum(norm_sums, ('dp', 'seq'))  41.1 us
    dot_general x5, matrix products, batched(): lax.dot_general(left, right, (((left_dim,), (right_dim,)), ((0, 1), (0, 1...  40 us
    reduce_scatter x1, waiting for transfers between devices, shards(): lax.psum_scatter(pair_sum(grad_kv), 'seq', scatter_dimension=0, axis_inde...  37.7 us
  transfers between devices with their start and end apart: 15, of which 11 were waited for; matrix products, arithmetic and copies ran while one was open for 33% of the time, Pallas kernels for 0%

commit v1 on v0

--- a/solution.py
+++ b/solution.py
@@ -1,6 +1,10 @@
+import functools
+
 import jax
 import jax.numpy as jnp
 from jax import lax
+from jax.experimental import pallas as pl
+from jax.experimental.pallas import tpu as pltpu
 from jax.sharding import PartitionSpec as P
 
 HEADS = 17
@@ -136,7 +140,7 @@
     )
 
 
-def shards(
+def shards_plain(
     tokens,
     cotangent,
     w_qkv,
@@ -295,9 +299,610 @@
     )
 
 
+MESH = pl.DeviceIdType.MESH
+ORDERS = tuple(tuple((q + k) % 4 for k in range(4)) for q in range(4))
+TILE = 128
+LANES = (3 * TILE, 3 * TILE, 3 * TILE, 4 * TILE)
+UNITS = 5
+REM_UP, REM_QKV, REM_OUT, REM_DOWN, REM_NORM = 0, 32, 56, 64, 96
+
+
+def place_of(q, dp, seq):
+    z = seq // 2
+    bits = (dp % 2, dp // 2, (z % 2 + z // 2) % 2, z // 2)
+    return sum(bits[dim] * 2**k for k, dim in enumerate(ORDERS[q]))
+
+
+def partner(dim):
+    dp, seq = lax.axis_index("dp"), lax.axis_index("seq")
+    z, core = seq // 2, seq % 2
+    if dim == 0:
+        return (dp + 1 - 2 * (dp % 2), seq)
+    if dim == 1:
+        return (dp + 2 - 4 * (dp // 2), seq)
+    if dim == 2:
+        return (dp, (z + 1 - 2 * (z % 2)) * 2 + core)
+    return (dp, (3 - z) * 2 + core)
+
+
+def sibling():
+    dp, seq = lax.axis_index("dp"), lax.axis_index("seq")
+    return (dp, seq + 1 - 2 * (seq % 2))
+
+
+def greet(devices):
+    barrier = pltpu.get_barrier_semaphore()
+    for device in devices:
+        pl.semaphore_signal(barrier, inc=1, device_id=device, device_id_type=MESH)
+    pl.semaphore_wait(barrier, len(devices))
+
+
+def send(src, dst, send_sem, recv_sem, device):
+    copy = pltpu.make_async_remote_copy(
+        src_ref=src, dst_ref=dst, send_sem=send_sem, recv_sem=recv_sem,
+        device_id=device, device_id_type=MESH,
+    )
+    copy.start()
+    return copy
+
+
+def gather_kernel(*refs):
+    shards_in, full = refs[:4], refs[4:8]
+    own_sem, link_send, link_recv, sib_send, sib_recv = refs[8:]
+    dp, seq = lax.axis_index("dp"), lax.axis_index("seq")
+    core = seq % 2
+    greet([partner(dim) for dim in range(4)] + [sibling()])
+    at = [place_of(q, dp, seq) for q in range(4)]
+    links, sides, owns = {}, [], []
+    for q in range(4):
+        links[q] = send(
+            shards_in[q], full[q].at[core, at[q]], link_send.at[q, 0], link_recv.at[q, 0],
+            partner(ORDERS[q][0]),
+        )
+        own = pltpu.make_async_copy(shards_in[q], full[q].at[core, at[q]], own_sem.at[q])
+        own.start()
+        owns.append(own)
+        sides.append(
+            send(
+                shards_in[q], full[q].at[core, at[q]], sib_send.at[q, 0], sib_recv.at[q, 0],
+                sibling(),
+            )
+        )
+    for own in owns:
+        own.wait()
+    for stage in range(4):
+        for q in range(4):
+            links[q].wait()
+            size = 2**stage
+            if stage < 3:
+                held = full[q].at[core, pl.ds(at[q] // (2 * size) * (2 * size), 2 * size)]
+                links[q] = send(
+                    held, held, link_send.at[q, stage + 1], link_recv.at[q, stage + 1],
+                    partner(ORDERS[q][stage + 1]),
+                )
+            mine = at[q] // size
+            got = full[q].at[core, pl.ds((mine + 1 - 2 * (mine % 2)) * size, size)]
+            sides.append(
+                send(
+                    got, got, sib_send.at[q, stage + 1], sib_recv.at[q, stage + 1], sibling()
+                )
+            )
+    for side in sides:
+        side.wait()
+
+
+def gather_weights(chunks):
+    rows = chunks[0].shape[0]
+    anywhere = pl.BlockSpec(memory_space=pl.ANY)
+    dma = pltpu.SemaphoreType.DMA
+    return pl.pallas_call(
+        gather_kernel,
+        out_shape=[jax.ShapeDtypeStruct((2, 16, rows, lanes), jnp.bfloat16) for lanes in LANES],
+        in_specs=[anywhere] * 4,
+        out_specs=[anywhere] * 4,
+        scratch_shapes=[dma((4,)), dma((4, 4)), dma((4, 4)), dma((4, 5)), dma((4, 5))],
+        compiler_params=pltpu.CompilerParams(collective_id=0, has_side_effects=True),
+        name="gather_weights",
+    )(*chunks)
+
+
+def scatter_kernel(*refs):
+    parts, outs = refs[:4], refs[4:8]
+    own, acc, got3, got2, got1, got0 = (refs[8 + 4 * i : 12 + 4 * i] for i in range(6))
+    got = (got0, got1, got2, got3)
+    own_sem, link_send, link_recv, sib_send, sib_recv = refs[32:]
+    dp, seq = lax.axis_index("dp"), lax.axis_index("seq")
+    core = seq % 2
+    greet([partner(dim) for dim in range(4)] + [sibling()])
+    at = [place_of(q, dp, seq) for q in range(4)]
+    side, load = {}, {}
+    for part in range(2):
+        for q in range(4):
+            high = at[q] // 8
+            span = pl.ds(((1 - high) if part == 0 else high) * 8, 8)
+            side[q, part] = send(
+                parts[q].at[1 - core, span], acc[q].at[span],
+                sib_send.at[q, part], sib_recv.at[q, part], sibling(),
+            )
+            load[q, part] = pltpu.make_async_copy(
+                parts[q].at[core, span], own[q].at[span], own_sem.at[q, part]
+            )
+            load[q, part].start()
+
+    def add(q, base, other, other_base, count):
+        def one(b, carry):
+            acc[q][base + b] = acc[q][base + b] + other[other_base + b]
+            return carry
+
+        lax.fori_loop(0, count, one, 0)
+
+    links = {}
+    for part in range(2):
+        for q in range(4):
+            side[q, part].wait_recv()
+            load[q, part].wait()
+            high = at[q] // 8
+            base = ((1 - high) if part == 0 else high) * 8
+            add(q, base, own[q], base, 8)
+            if part == 0:
+                links[q, 3] = send(
+                    acc[q].at[pl.ds(base, 8)], got3[q], link_send.at[q, 3], link_recv.at[q, 3],
+                    partner(ORDERS[q][3]),
+                )
+    for stage in (3, 2, 1):
+        half = 2 ** (stage - 1)
+        for q in range(4):
+            links[q, stage].wait_recv()
+            base = at[q] // (2 * half) * (2 * half)
+            high = at[q] // half % 2
+            away, keep = (1 - high) * half, high * half
+            add(q, base + away, got[stage][q], away, half)
+            links[q, stage - 1] = send(
+                acc[q].at[pl.ds(base + away, half)], got[stage - 1][q],
+                link_send.at[q, stage - 1], link_recv.at[q, stage - 1],
+                partner(ORDERS[q][stage - 1]),
+            )
+            add(q, base + keep, got[stage][q], keep, half)
+    for q in range(4):
+        links[q, 0].wait_recv()
+        outs[q][...] = acc[q][at[q]] + got0[q][0]
+    for copy in list(side.values()) + list(links.values()):
+        copy.wait_send()
+
+
+def scatter_grads(parts):
+    rows = parts[0].shape[2]
+    dma = pltpu.SemaphoreType.DMA
+    bf16 = jnp.bfloat16
+    buffers = [
+        pltpu.VMEM((count, rows, lanes), bf16) for count in (16, 16, 8, 4, 2, 1) for lanes in LANES
+    ]
+    return pl.pallas_call(
+        scatter_kernel,
+        out_shape=[jax.ShapeDtypeStruct((rows, lanes), bf16) for lanes in LANES],
+        in_specs=[pl.BlockSpec(memory_space=pl.ANY)] * 4,
+        out_specs=[pl.BlockSpec(memory_space=pltpu.VMEM)] * 4,
+        scratch_shapes=buffers + [dma((4, 2)), dma((4, 4)), dma((4, 4)), dma((4, 2)), dma((4, 2))],
+        compiler_params=pltpu.CompilerParams(
+            collective_id=1, has_side_effects=True, vmem_limit_bytes=56 * 2**20
+        ),
+        name="scatter_grads",
+    )(*parts)
+
+
+def exchange_kernel(blocks, out, own_sem, send_sem, recv_sem):
+    dp, seq = lax.axis_index("dp"), lax.axis_index("seq")
+    others = [(dp, (seq + k) % 8) for k in range(1, 8)]
+    greet(others)
+    own = pltpu.make_async_copy(blocks.at[seq], out.at[seq], own_sem)
+    copies = [
+        send(blocks.at[device[1]], out.at[seq], send_sem.at[k], recv_sem.at[k], device)
+        for k, device in enumerate(others)
+    ]
+    own.start()
+    own.wait()
+    for copy in copies:
+        copy.wait()
+
+
+def exchange(blocks, which):
+    dma = pltpu.SemaphoreType.DMA
+    return pl.pallas_call(
+        exchange_kernel,
+        out_shape=jax.ShapeDtypeStruct(blocks.shape, blocks.dtype),
+        in_specs=[pl.BlockSpec(memory_space=pl.ANY)],
+        out_specs=pl.BlockSpec(memory_space=pl.ANY),
+        scratch_shapes=[dma, dma((7,)), dma((7,))],
+        compiler_params=pltpu.CompilerParams(collective_id=2 + which, has_side_effects=True),
+        name=f"exchange_{which}",
+    )(blocks)
+
+
+def spots():
+    for dp in range(4):
+        for seq in range(8):
+            yield dp, seq, seq % 2, [place_of(q, dp, seq) for q in range(4)]
+
+
+def unpack_kernel(c0, c1, c2, c3, qkv, out, up, down, norms):
+    for dp, s, core, at in spots():
+        qkv[dp, :, s * 408 : s * 408 + 384] = c0[core, at[0]]
+        mixed = c1[core, at[1]]
+        rem = mixed[:, TILE : 2 * TILE]
+        out[dp, :, s * 136 : s * 136 + 128] = mixed[:, :TILE]
+        up[dp, :, s * 544 : s * 544 + 128] = mixed[:, 2 * TILE :]
+        up[dp, :, s * 544 + 128 : s * 544 + 512] = c2[core, at[2]]
+        up[dp, :, s * 544 + 512 : s * 544 + 544] = rem[:, REM_UP : REM_UP + 32]
+        qkv[dp, :, s * 408 + 384 : s * 408 + 408] = rem[:, REM_QKV : REM_QKV + 24]
+        out[dp, :, s * 136 + 128 : s * 136 + 136] = rem[:, REM_OUT : REM_OUT + 8]
+        for i in range(4):
+            down[dp * 4 + i, :, s * 136 : s * 136 + 128] = c3[core, at[3], :, i * TILE : (i + 1) * TILE]
+            down[dp * 4 + i, :, s * 136 + 128 : s * 136 + 136] = rem[
+                :, REM_DOWN + 8 * i : REM_DOWN + 8 * i + 8
+            ]
+        if s == 0:
+            norms[dp] = rem
+
+
+def unpack_weights(chunks):
+    bf16 = jnp.bfloat16
+    rows, step = chunks[0].shape[2], 16
+
+    def spec(count, lanes):
+        return pl.BlockSpec((count, step, lanes), lambda i: (0, i, 0))
+
+    sizes = ((4, 3264), (4, 1088), (4, 4352), (16, 1088), (4, 128))
+    return pl.pallas_call(
+        unpack_kernel,
+        grid=(rows // step,),
+        out_shape=[jax.ShapeDtypeStruct((count, rows, lanes), bf16) for count, lanes in sizes],
+        in_specs=[pl.BlockSpec((2, 16, step, lanes), lambda i: (0, 0, i, 0)) for lanes in LANES],
+        out_specs=[spec(*size) for size in sizes],
+        compiler_params=pltpu.CompilerParams(vmem_limit_bytes=40 * 2**20),
+        name="unpack_weights",
+    )(*chunks)
+
+
+def pack_kernel(qkv, out, up, down, norms, c0, c1, c2, c3):
+    for dp, s, core, at in spots():
+        c0[core, at[0]] = qkv[dp, :, s * 408 : s * 408 + 384]
+        c1[core, at[1], :, :TILE] = out[dp, :, s * 136 : s * 136 + 128]
+        c1[core, at[1], :, 2 * TILE :] = up[dp, :, s * 544 : s * 544 + 128]
+        c2[core, at[2]] = up[dp, :, s * 544 + 128 : s * 544 + 512]
+        base = at[1]
+        c1[core, base, :, TILE : 2 * TILE] = norms[dp]
+        c1[core, base, :, TILE + REM_UP : TILE + REM_UP + 32] = up[dp, :, s * 544 + 512 : s * 544 + 544]
+        c1[core, base, :, TILE + REM_QKV : TILE + REM_QKV + 24] = qkv[dp, :, s * 408 + 384 : s * 408 + 408]
+        c1[core, base, :, TILE + REM_OUT : TILE + REM_OUT + 8] = out[dp, :, s * 136 + 128 : s * 136 + 136]
+        for i in range(4):
+            c3[core, at[3], :, i * TILE : (i + 1) * TILE] = down[dp * 4 + i, :, s * 136 : s * 136 + 128]
+            spot = TILE + REM_DOWN + 8 * i
+            c1[core, base, :, spot : spot + 8] = down[dp * 4 + i, :, s * 136 + 128 : s * 136 + 136]
+
+
+def pack_grads(qkv, out, up, down, norms):
+    rows, step = qkv.shape[1], 16
+
+    def spec(count, lanes):
+        return pl.BlockSpec((count, step, lanes), lambda i: (0, i, 0))
+
+    return pl.pallas_call(
+        pack_kernel,
+        grid=(rows // step,),
+        out_shape=[jax.ShapeDtypeStruct((2, 16, rows, lanes), jnp.bfloat16) for lanes in LANES],
+        in_specs=[spec(4, 3264), spec(4, 1088), spec(4, 4352), spec(16, 1088), spec(4, 128)],
+        out_specs=[pl.BlockSpec((2, 16, step, lanes), lambda i: (0, 0, i, 0)) for lanes in LANES],
+        compiler_params=pltpu.CompilerParams(vmem_limit_bytes=40 * 2**20),
+        name="pack_grads",
+    )(qkv, out, up, down, norms)
+
+
+QUERY_BLOCK = 256
+
+
+def flip(block):
+    return block.astype(jnp.float32).T.astype(jnp.bfloat16)
+
+
+def masked_scores(k_rows, q_cols, seg_k, seg_q, start, scale):
+    count, width = k_rows.shape[0], q_cols.shape[1]
+    scores = dot(k_rows, q_cols) * scale
+    key_at = lax.broadcasted_iota(jnp.int32, (count, width), 0)
+    query_at = lax.broadcasted_iota(jnp.int32, (count, width), 1) + start
+    return jnp.where((seg_k == seg_q) & (key_at <= query_at), scores, -1e30)
+
+
+def attend_kernel(scale, order, x, seg_k, seg_q, out, lse, q_t, k_t, v_t, o_t):
+    unit = pl.program_id(0)
+    slots = x.shape[0]
+    tok = x.shape[3]
+    depth = q_t.shape[0]
+    for b in range(slots):
+        at = order[unit, b]
+        for n, held in enumerate((q_t, k_t, v_t)):
+            held[:, b * tok : (b + 1) * tok] = x[at, 0, n * depth : (n + 1) * depth]
+    keys = flip(k_t[...])
+    for start in range(0, slots * tok, QUERY_BLOCK):
+        count = start + QUERY_BLOCK
+        cols = slice(start, count)
+        scores = masked_scores(
+            keys[:count], q_t[:, cols], seg_k[0, :count], seg_q[0, :, cols], start, scale
+        )
+        top = jnp.max(scores, 0, keepdims=True)
+        weights = jnp.exp(scores - top)
+        total = jnp.sum(weights, 0, keepdims=True)
+        probs = (weights * (1.0 / total)).astype(jnp.bfloat16)
+        o_t[:, cols] = dot(v_t[:, :count], probs).astype(jnp.bfloat16)
+        lse[0, :, cols] = top + jnp.log(total)
+    for b in range(slots):
+        out[order[unit, b], 0] = o_t[:, b * tok : (b + 1) * tok]
+
+
+def attend(x, order, seg_k, seg_q, scale):
+    slots, units, depth3, tok = x.shape
+    depth, length = depth3 // 3, slots * tok
+    bf16 = jnp.bfloat16
+    held = [pltpu.VMEM((depth, length), bf16)] * 4
+    return pl.pallas_call(
+        functools.partial(attend_kernel, scale),
+        grid_spec=pltpu.PrefetchScalarGridSpec(
+            num_scalar_prefetch=1,
+            grid=(units,),
+            in_specs=[
+                pl.BlockSpec((slots, 1, depth3, tok), lambda u, o: (0, u, 0, 0)),
+                pl.BlockSpec((1, length, 1), lambda u, o: (u, 0, 0)),
+                pl.BlockSpec((1, 1, length), lambda u, o: (u, 0, 0)),
+            ],
+            out_specs=[
+                pl.BlockSpec((slots, 1, depth, tok), lambda u, o: (0, u, 0, 0)),
+                pl.BlockSpec((1, 1, length), lambda u, o: (u, 0, 0)),
+            ],
+            scratch_shapes=held,
+        ),
+        out_shape=[
+            jax.ShapeDtypeStruct((slots, units, depth, tok), bf16),
+            jax.ShapeDtypeStruct((units, 1, length), jnp.float32),
+        ],
+        compiler_params=pltpu.CompilerParams(vmem_limit_bytes=40 * 2**20),
+        name="attend",
+    )(order, x, seg_k, seg_q)
+
+
+def attend_back_kernel(
+    scale, order, x, g, seg_k, seg_q, lse, out, q_t, k_t, v_t, g_t, dq_t, dk_t, dv_t
+):
+    unit = pl.program_id(0)
+    slots = x.shape[0]
+    tok = x.shape[3]
+    depth = q_t.shape[0]
+    for b in range(slots):
+        at = order[unit, b]
+        for n, held in enumerate((q_t, k_t, v_t)):
+            held[:, b * tok : (b + 1) * tok] = x[at, 0, n * depth : (n + 1) * depth]
+        g_t[:, b * tok : (b + 1) * tok] = g[at, 0]
+    keys = flip(k_t[...])
+    values = flip(v_t[...])
+    length = slots * tok
+    for start in reversed(range(0, length, QUERY_BLOCK)):
+        count = start + QUERY_BLOCK
+        cols = slice(start, count)
+        queries, grads = q_t[:, cols], g_t[:, cols]
+        scores = masked_scores(
+            keys[:count], queries, seg_k[0, :count], seg_q[0, :, cols], start, scale
+        )
+        probs = jnp.exp(scores - lse[0, :, cols])
+        grad_probs = dot(values[:count], grads)
+        row_dot = jnp.sum(probs * grad_probs, 0, keepdims=True)
+        grad_scores = (probs * (grad_probs - row_dot)).astype(jnp.bfloat16)
+        probs_low = probs.astype(jnp.bfloat16)
+        dq_t[:, cols] = dot(k_t[:, :count], grad_scores) * scale
+        dk = dot_right_t(queries, grad_scores)
+        dv = dot_right_t(grads, probs_low)
+        if count == length:
+            dk_t[...] = dk
+            dv_t[...] = dv
+        else:
+            dk_t[:, :count] += dk
+            dv_t[:, :count] += dv
+    for b in range(slots):
+        at = order[unit, b]
+        cols = slice(b * tok, (b + 1) * tok)
+        out[at, 0, :depth] = dq_t[:, cols].astype(jnp.bfloat16)
+        out[at, 0, depth : 2 * depth] = (dk_t[:, cols] * scale).astype(jnp.bfloat16)
+        out[at, 0, 2 * depth :] = dv_t[:, cols].astype(jnp.bfloat16)
+
+
+def attend_back(x, g, order, seg_k, seg_q, lse, scale):
+    slots, units, depth3, tok = x.shape
+    depth, length = depth3 // 3, slots * tok
+    bf16 = jnp.bfloat16
+    held = [pltpu.VMEM((depth, length), bf16)] * 4 + [pltpu.VMEM((depth, length), jnp.float32)] * 3
+    return pl.pallas_call(
+        functools.partial(attend_back_kernel, scale),
+        grid_spec=pltpu.PrefetchScalarGridSpec(
+            num_scalar_prefetch=1,
+            grid=(units,),
+            in_specs=[
+                pl.BlockSpec((slots, 1, depth3, tok), lambda u, o: (0, u, 0, 0)),
+                pl.BlockSpec((slots, 1, depth, tok), lambda u, o: (0, u, 0, 0)),
+                pl.BlockSpec((1, length, 1), lambda u, o: (u, 0, 0)),
+                pl.BlockSpec((1, 1, length), lambda u, o: (u, 0, 0)),
+                pl.BlockSpec((1, 1, length), lambda u, o: (u, 0, 0)),
+            ],
+            out_specs=pl.BlockSpec((slots, 1, depth3, tok), lambda u, o: (0, u, 0, 0)),
+            scratch_shapes=held,
+        ),
+        out_shape=jax.ShapeDtypeStruct(x.shape, bf16),
+        compiler_params=pltpu.CompilerParams(vmem_limit_bytes=48 * 2**20),
+        name="attend_back",
+    )(order, x, g, seg_k, seg_q, lse)
+
+
+def to_units(flat, micro_count, kinds):
+    tok = flat.shape[1] // micro_count
+    units = flat.reshape(kinds, HEADS, -1, micro_count, tok).transpose(3, 1, 0, 2, 4)
+    units = units.reshape(micro_count * HEADS, -1, tok)
+    units = jnp.pad(units, ((0, 8 * UNITS - units.shape[0]), (0, 0), (0, 0)))
+    return units.reshape(8, UNITS, -1, tok)
+
+
+def from_units(units, micro_count, kinds):
+    tok = units.shape[3]
+    held = units.reshape(8 * UNITS, -1, tok)[: micro_count * HEADS]
+    held = held.reshape(micro_count, HEADS, kinds, -1, tok).transpose(0, 4, 2, 1, 3)
+    return held.reshape(micro_count * tok, -1)
+
+
+def shards_fast(
+    tokens,
+    cotangent,
+    w_qkv,
+    w_out,
+    w_up,
+    w_down,
+    gain_one,
+    bias_one,
+    gain_two,
+    bias_two,
+    lengths,
+    slot_order,
+):
+    micro_count, tok_dev, width = tokens.shape
+    rows = micro_count * tok_dev
+    scale = (width // HEADS) ** (-0.5)
+    bf16, f32 = jnp.bfloat16, jnp.float32
+    part = w_qkv.shape[0]
+    my_slot = lax.axis_index("seq")
+
+    downs = [w_down[i * part : (i + 1) * part] for i in range(4)]
+    norms = jnp.stack([gain_one, bias_one, gain_two, bias_two], 1)
+    rem = jnp.concatenate(
+        [w_up[:, 512:], w_qkv[:, 384:], w_out[:, 128:]]
+        + [down[:, 128:] for down in downs]
+        + [norms, jnp.zeros((part, 28), bf16)],
+        1,
+    )
+    gathered = gather_weights(
+        [
+            w_qkv[:, :384],
+            jnp.concatenate([w_out[:, :128], rem, w_up[:, :128]], 1),
+            w_up[:, 128:512],
+            jnp.concatenate([down[:, :128] for down in downs], 1),
+        ]
+    )
+    full_qkv, full_out, full_up, full_down, full_norms = unpack_weights(gathered)
+    full_qkv = full_qkv.reshape(width, -1)
+    full_out = full_out.reshape(width, width)
+    full_up = full_up.reshape(width, -1)
+    full_down = full_down.reshape(-1, width)
+    norm_rows = full_norms[:, :, REM_NORM : REM_NORM + 4].reshape(width, 4).T.astype(f32)
+    g_one, b_one, g_two, b_two = norm_rows[0], norm_rows[1], norm_rows[2], norm_rows[3]
+
+    unit_ids = my_slot * UNITS + jnp.arange(UNITS, dtype=jnp.int32)
+    second = (unit_ids >= HEADS)[:, None]
+    doc_ends = jax.vmap(running_total)(lengths[:, 0])
+    places = jnp.arange(8 * tok_dev, dtype=jnp.int32)
+    segments = jax.vmap(segment_of, (None, 0))(places, doc_ends)
+    unit_segments = jnp.where(second, segments[1][None], segments[0][None])
+    seg_k, seg_q = unit_segments[:, :, None], unit_segments[:, None, :]
+    slots = jnp.arange(8, dtype=jnp.int32)
+    holders = jnp.sum(
+        jnp.where(slot_order[:, 0][:, None, :] == slots[None, :, None], slots[None, None, :], 0), 2
+    )
+    order = jnp.where(second, holders[1][None], holders[0][None])
+
+    residual = tokens.astype(f32).reshape(rows, width)
+    scaled_one, inv_one = normalize(residual)
+    normed_one = (scaled_one * g_one + b_one).astype(bf16)
+    qkv_t = lax.dot_general(
+        full_qkv, normed_one, (((0,), (1,)), ((), ())), preferred_element_type=f32
+    ).astype(bf16)
+    unit_qkv = exchange(to_units(qkv_t, micro_count, 3), 0)
+    unit_out, lse = attend(unit_qkv, order, seg_k, seg_q, scale)
+    attn_flat = from_units(exchange(unit_out, 1), micro_count, 1)
+    middle = residual + dot(attn_flat, full_out)
+    scaled_two, inv_two = normalize(middle)
+    normed_two = (scaled_two * g_two + b_two).astype(bf16)
+    hidden = dot(normed_two, full_up)
+    activated_full, gelu_back = jax.vjp(gelu_tanh, hidden)
+    activated = activated_full.astype(bf16)
+
+    grad_rows = cotangent.reshape(rows, width)
+    block_out = (middle + dot(activated, full_down)).astype(bf16)
+    grad_hidden = gelu_back(dot_right_t(grad_rows, full_down))[0].astype(bf16)
+    sum_down = dot_left_t(activated, grad_rows).astype(bf16)
+    sum_up = dot_left_t(normed_two, grad_hidden).astype(bf16)
+    grad_normed_two = dot_right_t(grad_hidden, full_up)
+    grad_middle = grad_rows.astype(f32) + norm_back(grad_normed_two, scaled_two, inv_two, g_two)
+    grad_branch = grad_middle.astype(bf16)
+    sum_proj = dot_left_t(attn_flat, grad_branch).astype(bf16)
+    grad_heads_t = dot_right_t(full_out, grad_branch).astype(bf16)
+    unit_grad = exchange(to_units(grad_heads_t, micro_count, 1), 2)
+    unit_back = attend_back(unit_qkv, unit_grad, order, seg_k, seg_q, lse, scale)
+    grad_qkv_rows = from_units(exchange(unit_back, 3), micro_count, 3)
+    sum_qkv = dot_left_t(normed_one, grad_qkv_rows).astype(bf16)
+    grad_normed_one = dot_right_t(grad_qkv_rows, full_qkv)
+    grad_input = (
+        grad_middle + norm_back(grad_normed_one, scaled_one, inv_one, g_one)
+    ).astype(bf16)
+
+    norm_sums = jnp.stack(
+        [
+            jnp.sum(grad_normed_one * scaled_one, 0),
+            jnp.sum(grad_normed_one, 0),
+            jnp.sum(grad_normed_two * scaled_two, 0),
+            jnp.sum(grad_normed_two, 0),
+        ]
+    )
+    norm_cols = jnp.pad(norm_sums.T.astype(bf16), ((0, 0), (REM_NORM, 28)))
+    sum0, sum1, sum2, sum3 = (
+        total.astype(f32)
+        for total in scatter_grads(
+            pack_grads(
+                sum_qkv.reshape(4, part, -1),
+                sum_proj.reshape(4, part, -1),
+                sum_up.reshape(4, part, -1),
+                sum_down.reshape(16, part, -1),
+                norm_cols.reshape(4, part, -1),
+            )
+        )
+    )
+    rest = sum1[:, TILE : 2 * TILE]
+    out_qkv = jnp.concatenate([sum0, rest[:, REM_QKV : REM_QKV + 24]], 1)
+    out_proj = jnp.concatenate([sum1[:, :TILE], rest[:, REM_OUT : REM_OUT + 8]], 1)
+    out_up = jnp.concatenate([sum1[:, 2 * TILE :], sum2, rest[:, REM_UP : REM_UP + 32]], 1)
+    out_down = jnp.concatenate(
+        [
+            jnp.concatenate(
+                [
+                    sum3[:, i * TILE : (i + 1) * TILE],
+                    rest[:, REM_DOWN + 8 * i : REM_DOWN + 8 * i + 8],
+                ],
+                1,
+            )
+            for i in range(4)
+        ],
+        0,
+    )
+    norm_mine = rest[:, REM_NORM : REM_NORM + 4].T
+    return (
+        block_out.reshape(tokens.shape),
+        grad_input.reshape(tokens.shape),
+        out_qkv,
+        out_proj,
+        out_up,
+        out_down,
+        norm_mine[0],
+        norm_mine[1],
+        norm_mine[2],
+        norm_mine[3],
+    )
+
+
 def solution(mesh):
+    grid = (mesh.shape["dp"], mesh.shape["seq"])
     return jax.shard_map(
-        shards,
+        shards_fast if grid == (4, 8) else shards_plain,
         mesh=mesh,
         in_specs=(
             P(None, ("dp", "seq"), None),

time: 1000 us -> 858 us (0.86)
  Pallas kernels: 0 us -> 713 us
  waiting for transfers between devices: 451 us -> 0 us
  local copies, waits for them, and re-layouts: 225 us -> 59.3 us
  other arithmetic: 132 us -> 7.13 us
  blocking collectives: 49.2 us -> 0 us
  matrix products: 117 us -> 72.5 us
  between operations: 15.5 us -> 1.76 us
    pallas_call x0 -> x10, Pallas kernels: none -> 713 us  [the longest x1 190 us: unpack_weights(): pl.pallas_call(unpack_kernel, grid=(rows // step,), out_shape=[jax.ShapeD...]
    all_gather x5 -> x0, waiting for transfers between devices: 221 us -> none  [the longest x2 129 us: gather_stack(): held = lax.all_gather(chips, 'dp')]
    unnamed x12 -> x0, waiting for transfers between devices: 121 us -> none
    reduce_scatter x3 -> x0, waiting for transfers between devices: 94.3 us -> none  [the longest x1 56.6 us: scatter_stack(): held = lax.psum_scatter(held, 'dp', scatter_dimension=0, tiled=True)]
    dot_general x12 -> x1, matrix products: 80.9 us -> 6.73 us  [shards_fast(): lax.dot_general(full_qkv, normed_one, (((0,), (1,)), ((), ())), preferred...]
    reshape x8 -> x3, local copies, waits for them, and re-layouts: 75.7 us -> 6.08 us  [the longest x2 5.24 us: to_units(): flat.reshape(kinds, HEADS, -1, micro_count, tok).transpose(3, 1, 0, 2, 4)]
    psum x1 -> x0, blocking collectives: 41.1 us -> none  [shards(): norm_totals = lax.psum(norm_sums, ('dp', 'seq'))]
    transpose x5 -> x0, other arithmetic: 40.8 us -> none  [the longest x2 23.4 us: scatter_stack(): held = pair_sum(parts).transpose(1, 0, 2, 3).reshape(-1, parts.shape[3])]
  transfers between devices with their start and end apart: 15 -> 0, of which waited for: 11 -> 0; matrix products, arithmetic and copies ran while one was open for 33% -> 0% of each run, Pallas kernels for 0% -> 0%
where the time goes in v1:
time: 858 us; the launch traced here: 853 us
  Pallas kernels  713 us (83%)
  matrix products  72.5 us (8%)
  local copies, waits for them, and re-layouts  59.3 us (7%)
    pallas_call x1, Pallas kernels, unpack_weights(): pl.pallas_call(unpack_kernel, grid=(rows // step,), out_shape=[jax.ShapeD...  190 us
    pallas_call x1, Pallas kernels, gather_weights(): pl.pallas_call(gather_kernel, out_shape=[jax.ShapeDtypeStruct((2, 16, row...  178 us
    pallas_call x1, Pallas kernels, scatter_grads(): pl.pallas_call(scatter_kernel, out_shape=[jax.ShapeDtypeStruct((rows, lan...  170 us
    pallas_call x4, Pallas kernels, exchange(): pl.pallas_call(exchange_kernel, out_shape=jax.ShapeDtypeStruct(blocks.sha...  117 us
    dot_general x4, matrix products, dot_right_t(): lax.dot_general(left, right, (((1,), (1,)), ((), ())), preferred_element_...  32.9 us
    pallas_call x1, Pallas kernels, pack_grads(): pl.pallas_call(pack_kernel, grid=(rows // step,), out_shape=[jax.ShapeDty...  28.1 us
    unnamed x84, local copies, waits for them, and re-layouts  18.7 us

profile of v1, /device:TPU:0, one launch (start us, length us, event | category | flops | bytes accessed | tf_op | source)
XLA Modules:
  0.0 853.5 jit_solution(16159256513097795240)
XLA Ops:
  0.7 1.7 slice.155.refs_0_
  2.4 0.9 slice.156
  4.3 0.9 fusion.35
  8.2 1.1 concatenate.30.refs_1_
  11.5 178.2 %gather_weights.1 = (bf16[2,16,272,384]{3,2,1,0:T(8,128)(2,1)}, bf16[2,16,272,384]{3,2,1,0:T(8,128)(2,1)}, bf16[2,16,272,384]{3,2,1,0:T(8,128)(2,1)}, bf16[2,16,272,512]{3,2,1,0:T(8,128)(2,1)}) custom-call(bf16[272,384]{1,0:T(8,128)(2,1)} %slice.155.refs_0_, bf16[272,384]{1,0:T(8,128)(2,1)} %concatenate.30.refs_1_, bf16[272,384]{1,0:T(8,128)(2,1)} %slice.165.refs_2_, ...), custom_call_target="tpu_custom_call" | custom-call | tf_op jit(solution)/shard_map/gather_weights/pallas_call | solution.py:398
  189.7 2.9 copy-done.5
  192.6 190.5 %unpack_weights.1 = (bf16[4,272,3264]{2,1,0:T(8,128)(2,1)}, bf16[4,272,1088]{2,1,0:T(8,128)(2,1)S(1)}, bf16[4,272,4352]{2,1,0:T(8,128)(2,1)}, bf16[16,272,1088]{2,1,0:T(8,128)(2,1)}, bf16[4,272,128]{2,1,0:T(8,128)(2,1)S(1)}) custom-call(bf16[2,16,272,384]{3,2,1,0:T(8,128)(2,1)S(1)} %copy-done.5, bf16[2,16,272,384]{3,2,1,0:T(8,128)(2,1)} %get-tuple-element.30.c1, ...), custom_call_target="tpu_custom_call" | custom-call | tf_op jit(solution)/shard_map/unpack_weights/pallas_call | solution.py:555
  383.1 1.5 copy-done.9
  387.5 6.7 convolution_convert_fusion.4
  394.3 3.5 reshape.357
  398.2 1.6 pad.12
  399.8 35.0 %exchange_0.1.x = bf16[8,5,192,128]{3,2,1,0:T(8,128)(2,1)} custom-call(bf16[8,5,192,128]{3,2,1,0:T(8,128)(2,1)} %bitcast.138), custom_call_target="tpu_custom_call" | custom-call | tf_op jit(solution)/shard_map/exchange_0/pallas_call | solution.py:510
  436.3 12.9 %attend.1 = (bf16[8,5,64,128]{3,2,1,0:T(8,128)(2,1)S(1)}, f32[5,1,1024]{2,1,0:T(1,128)S(1)}) custom-call(s32[5,8]{1,0:T(8,128)S(1)} %broadcast_select_fusion.2.order, bf16[8,5,192,128]{3,2,1,0:T(8,128)(2,1)S(1)} %copy-done.2, s32[5,1024,1]{2,1,0:T(8,128)S(1)} %broadcast_select_fusion.seg_k, s32[5,1,1024]{2,1,0:T(1,128)S(1)} %broadcast_select_fusion.1.seg_q), custom_call_target="tpu_custom_call" | custom-call | tf_op jit(solution)/shard_map/attend/pallas_call | solution.py:646
  450.0 24.9 %exchange_1.1 = bf16[8,5,64,128]{3,2,1,0:T(8,128)(2,1)} custom-call(bf16[8,5,64,128]{3,2,1,0:T(8,128)(2,1)} %copy-done.8), custom_call_target="tpu_custom_call" | custom-call | tf_op jit(solution)/shard_map/exchange_1/pallas_call | solution.py:510
  474.9 1.1 slice.201
  476.7 1.2 fusion.40
  478.2 6.3 fusion.33
  484.5 2.1 copy-done.19
  486.6 8.3 fusion.14
  495.7 22.7 %fusion.3 = bf16[256,4352]{1,0:T(8,128)(2,1)S(1)} fusion(f32[256,4352]{1,0:T(8,128)} %copy-done.19, bf16[4352,1088]{1,0:T(8,128)(2,1)} %bitcast.165, bf16[2,128,1088]{1,2,0:T(8,128)(2,1)S(1)} %copy-done), kind=kOutput, calls=%fused_computation.13 | convolution fusion | flops 2451046400 | bytes 16711680 | tf_op jit(solution)/shard_map/dot_general | solution.py:91
  518.4 3.0 multiply_reduce_fusion
  521.9 1.0 copy-done.14
  522.8 1.7 convolution_convert_fusion.5
  524.6 1.7 reshape.368
  526.5 0.9 pad.13
  527.4 17.8 %exchange_2.1.g = bf16[8,5,64,128]{3,2,1,0:T(8,128)(2,1)} custom-call(bf16[8,5,64,128]{3,2,1,0:T(8,128)(2,1)} %bitcast.149), custom_call_target="tpu_custom_call" | custom-call | tf_op jit(solution)/shard_map/exchange_2/pallas_call | solution.py:510
  545.2 1.1 copy-done.7
  546.3 16.3 %attend_back.1.blocks = bf16[8,5,192,128]{3,2,1,0:T(8,128)(2,1)S(1)} custom-call(s32[5,8]{1,0:T(8,128)S(1)} %broadcast_select_fusion.2.order, bf16[8,5,192,128]{3,2,1,0:T(8,128)(2,1)S(1)} %copy-done.3, bf16[8,5,64,128]{3,2,1,0:T(8,128)(2,1)S(1)} %copy-done.7, s32[5,1024,1]{2,1,0:T(8,128)} %copy-done.1, s32[5,1,1024]{2,1,0:T(1,128)S(1)} %broadcast_select_fusion.1.seg_q, ...), custom_call_target="tpu_custom_call" | custom-call | tf_op jit(solution)/shard_map/attend_back/pallas_call | solution.py:720
  562.6 1.3 copy-done.4
  564.0 38.9 %exchange_3.1 = bf16[8,5,192,128]{3,2,1,0:T(8,128)(2,1)} custom-call(bf16[8,5,192,128]{3,2,1,0:T(8,128)(2,1)} %copy-done.4), custom_call_target="tpu_custom_call" | custom-call | tf_op jit(solution)/shard_map/exchange_3/pallas_call | solution.py:510
  602.9 1.6 slice.204
  604.5 1.7 copy.120
  606.2 5.5 multiply_reduce_fusion.1
  611.8 1.2 copy_bitcast_fusion
  613.0 5.2 convolution_convert_fusion.2
  618.3 0.9 convolution_convert_fusion.3
  619.5 5.5 convolution_convert_fusion.1
  625.0 5.5 convolution_convert_fusion
  630.4 13.9 %copy.121 = bf16[4352,1088]{1,0:T(8,128)(2,1)} copy(bf16[4352,1088]{0,1:T(8,128)(2,1)} %convolution_convert_fusion) | data formatting | bytes 18939904 | tf_op jit(solution)/shard_map/convert_element_type | solution.py:833
  644.8 28.1 %pack_grads.1 = (bf16[2,16,272,384]{3,2,1,0:T(8,128)(2,1)S(1)}, bf16[2,16,272,384]{3,2,1,0:T(8,128)(2,1)}, bf16[2,16,272,384]{3,2,1,0:T(8,128)(2,1)}, bf16[2,16,272,512]{3,2,1,0:T(8,128)(2,1)}) custom-call(bf16[4,272,3264]{2,1,0:T(8,128)(2,1)} %bitcast.132, bf16[4,272,1088]{2,1,0:T(8,128)(2,1)S(1)} %bitcast.127, bf16[4,272,4352]{2,1,0:T(8,128)(2,1)} %bitcast.131, ...), custom_call_target="tpu_custom_call" | custom-call | tf_op jit(solution)/shard_map/pack_grads/pallas_call | solution.py:589
  673.0 2.7 copy-done.6
  675.7 170.2 %scatter_grads.1 = (bf16[272,384]{1,0:T(8,128)(2,1)}, bf16[272,384]{1,0:T(8,128)(2,1)}, bf16[272,384]{1,0:T(8,128)(2,1)}, bf16[272,512]{1,0:T(8,128)(2,1)}) custom-call(bf16[2,16,272,384]{3,2,1,0:T(8,128)(2,1)} %copy-done.6, bf16[2,16,272,384]{3,2,1,0:T(8,128)(2,1)} %get-tuple-element.41.refs_1_, bf16[2,16,272,384]{3,2,1,0:T(8,128)(2,1)} %get-tuple-element.42.refs_2_, ...), custom_call_target="tpu_custom_call" | custom-call | tf_op jit(solution)/shard_map/scatter_grads/pallas_call | solution.py:480
  845.9 1.0 slice.205
  847.0 1.0 convert_element_type.104
  847.9 0.9 pad_maximum_fusion.1
  849.9 0.9 pad_maximum_fusion
  850.9 1.2 copy.126
  852.2 1.0 slice_reduce_fusion
  (144 shorter events, 15.8 us)
Async XLA Ops:
  0.6 495.1 %copy-start = (bf16[2,128,1088]{1,2,0:T(8,128)(2,1)S(1)}, bf16[2,128,1088]{1,2,0:T(8,128)(2,1)}, u32[]{:S(2)}) copy-start(bf16[2,128,1088]{1,2,0:T(8,128)(2,1)} %param.13) | copy-start | bytes 1671172
  0.7 7.5 slice-start.7
  0.7 7.5 slice-start.5
  0.7 7.5 slice-start.6
  0.7 8.7 %copy-start.28 = (bf16[272,544]{1,0:T(8,128)(2,1)S(1)}, bf16[272,544]{1,0:T(8,128)(2,1)}, u32[]{:S(2)}) copy-start(bf16[272,544]{1,0:T(8,128)(2,1)} %param.16) | copy-start | bytes 887812
  0.7 7.4 copy-start.30
  2.4 7.6 copy-start.27
  189.7 2.9 copy-start.5
  192.6 192.0 %copy-start.32 = (s32[2,1,8]{2,1,0:T(1,128)S(1)}, s32[2,1,8]{2,1,0:T(1,128)}, u32[]{:S(2)}) copy-start(s32[2,1,8]{2,1,0:T(1,128)} %param.23) | copy-start | bytes 196
  383.1 1.5 copy-start.9
  384.6 1.1 copy-start.16
  386.7 0.8 copy-start.20
  399.8 35.0 %copy-start.31 = (s32[2,1,8]{2,1,0:T(1,128)S(1)}, s32[2,1,8]{2,1,0:T(1,128)}, u32[]{:S(2)}) copy-start(s32[2,1,8]{2,1,0:T(1,128)} %param.22) | copy-start | bytes 196
  434.7 1.5 copy-start.2
  435.4 13.8 %copy-start.1 = (s32[5,1024,1]{2,1,0:T(8,128)}, s32[5,1024,1]{2,1,0:T(8,128)S(1)}, u32[]{:S(2)}) copy-start(s32[5,1024,1]{2,1,0:T(8,128)S(1)} %broadcast_select_fusion.seg_k) | copy-start | bytes 61444
  449.2 0.8 copy-start.8
  450.0 26.6 %copy-start.10 = (bf16[4,272,1088]{2,1,0:T(8,128)(2,1)S(1)}, bf16[4,272,1088]{2,1,0:T(8,128)(2,1)}, u32[]{:S(2)}) copy-start(bf16[4,272,1088]{2,1,0:T(8,128)(2,1)} %copy-done.9) | copy-start | bytes 7102468
  474.9 1.8 copy-start.17
  476.7 1.3 copy-start.24
  477.9 43.5 %copy-start.11 = (f32[256,1088]{0,1:T(8,128)}, f32[256,1088]{0,1:T(8,128)S(1)}, u32[]{:S(2)}) copy-start(f32[256,1088]{0,1:T(8,128)S(1)} %get-tuple-element.132) | copy-start | bytes 3342340
  484.4 2.1 copy-start.19
  486.6 31.8 %slice-start = ((s8[9469952]{0:T(1024)(128)(4,1)}), s8[4194304]{0:T(1024)(128)(4,1)S(1)}, s32[]{:S(2)}) async-start(s8[9469952]{0:T(1024)(128)(4,1)} %bitcast.135), calls=%async_computation | async-start | bytes 8388608
  494.9 23.5 %slice-start.1 = ((s8[9469952]{0:T(1024)(128)(4,1)}), s8[4194304]{0:T(1024)(128)(4,1)S(1)}, s32[]{:S(2)}) async-start(s8[9469952]{0:T(1024)(128)(4,1)} %bitcast.135), calls=%async_computation.1 | async-start | bytes 8388608
  495.7 22.7 %slice-start.2 = ((s8[9469952]{0:T(1024)(128)(4,1)}), s8[1081344]{0:T(1024)(128)(4,1)S(1)}, s32[]{:S(2)}) async-start(s8[9469952]{0:T(1024)(128)(4,1)} %bitcast.135), calls=%async_computation.2 | async-start | bytes 2162688
  518.4 3.0 copy-start.22
  521.8 1.0 copy-start.14
  526.3 18.9 %copy-start.3 = (bf16[8,5,192,128]{3,2,1,0:T(8,128)(2,1)S(1)}, bf16[8,5,192,128]{3,2,1,0:T(8,128)(2,1)}, u32[]{:S(2)}) copy-start(bf16[8,5,192,128]{3,2,1,0:T(8,128)(2,1)} %exchange_0.1.x) | copy-start | bytes 5898244
  545.2 1.1 copy-start.7
  562.6 1.4 copy-start.4
  604.4 1.7 copy-start.18
  606.2 5.6 copy-start.15
  611.8 1.2 copy-start.21
  613.0 5.2 copy-start.25
  613.0 6.2 copy-start.23
  618.3 1.2 copy-start.12
  618.3 6.7 slice-start.3
  619.5 5.5 slice-start.4
  673.0 2.7 copy-start.6
  845.9 2.9 copy-start.13
  848.8 1.1 copy-start.29
  849.0 1.8 copy-start.26

commit v2 on v1

--- a/solution.py
+++ b/solution.py
@@ -300,7 +300,11 @@
 
 
 MESH = pl.DeviceIdType.MESH
-ORDERS = tuple(tuple((q + k) % 4 for k in range(4)) for q in range(4))
+ORDERS = ((2, 0, 3, 1), (2, 1, 3, 0), (3, 0, 2, 1), (3, 1, 2, 0))
+ROW_CUTS = ((0, 64), (64, 64), (128, 64), (192, 80))
+CHUNKS = tuple((q, r) for pair in ((0, 1), (2, 3)) for r in range(4) for q in pair)
+GATHER_LAGS = (0, 1, 2, 3, 5)
+SCATTER_LAGS = (0, 2, 3, 4, 6)
 TILE = 128
 LANES = (3 * TILE, 3 * TILE, 3 * TILE, 4 * TILE)
 UNITS = 5
@@ -353,40 +357,45 @@
     core = seq % 2
     greet([partner(dim) for dim in range(4)] + [sibling()])
     at = [place_of(q, dp, seq) for q in range(4)]
-    links, sides, owns = {}, [], []
-    for q in range(4):
-        links[q] = send(
-            shards_in[q], full[q].at[core, at[q]], link_send.at[q, 0], link_recv.at[q, 0],
-            partner(ORDERS[q][0]),
+    owns, links, sides = {}, {}, []
+
+    def step(chunk, stage):
+        q, r = CHUNKS[chunk]
+        span = pl.ds(*ROW_CUTS[r])
+        size = 2**stage
+        if stage == 0:
+            fresh, target = shards_in[q].at[span], full[q].at[core, at[q], span]
+            links[chunk] = send(
+                fresh, target, link_send.at[chunk, 0], link_recv.at[chunk, 0],
+                partner(ORDERS[q][0]),
+            )
+            owns[chunk] = pltpu.make_async_copy(fresh, target, own_sem.at[chunk])
+            owns[chunk].start()
+            sides.append(
+                send(fresh, target, sib_send.at[chunk, 0], sib_recv.at[chunk, 0], sibling())
+            )
+            return
+        links[chunk].wait()
+        if stage == 1:
+            owns[chunk].wait()
+        if stage < 4:
+            held = full[q].at[core, pl.ds(at[q] // size * size, size), span]
+            links[chunk] = send(
+                held, held, link_send.at[chunk, stage], link_recv.at[chunk, stage],
+                partner(ORDERS[q][stage]),
+            )
+        half = size // 2
+        mine = at[q] // half
+        got = full[q].at[core, pl.ds((mine + 1 - 2 * (mine % 2)) * half, half), span]
+        sides.append(
+            send(got, got, sib_send.at[chunk, stage], sib_recv.at[chunk, stage], sibling())
         )
-        own = pltpu.make_async_copy(shards_in[q], full[q].at[core, at[q]], own_sem.at[q])
-        own.start()
-        owns.append(own)
-        sides.append(
-            send(
-                shards_in[q], full[q].at[core, at[q]], sib_send.at[q, 0], sib_recv.at[q, 0],
-                sibling(),
-            )
-        )
-    for own in owns:
-        own.wait()
-    for stage in range(4):
-        for q in range(4):
-            links[q].wait()
-            size = 2**stage
-            if stage < 3:
-                held = full[q].at[core, pl.ds(at[q] // (2 * size) * (2 * size), 2 * size)]
-                links[q] = send(
-                    held, held, link_send.at[q, stage + 1], link_recv.at[q, stage + 1],
-                    partner(ORDERS[q][stage + 1]),
-                )
-            mine = at[q] // size
-            got = full[q].at[core, pl.ds((mine + 1 - 2 * (mine % 2)) * size, size)]
-            sides.append(
-                send(
-                    got, got, sib_send.at[q, stage + 1], sib_recv.at[q, stage + 1], sibling()
-                )
-            )
+
+    for turn in range(len(CHUNKS) + GATHER_LAGS[4]):
+        for stage in (4, 3, 2, 1, 0):
+            lag = GATHER_LAGS[stage]
+            if 0 <= turn - lag < len(CHUNKS):
+                step(turn - lag, stage)
     for side in sides:
         side.wait()
 
@@ -400,7 +409,7 @@
         out_shape=[jax.ShapeDtypeStruct((2, 16, rows, lanes), jnp.bfloat16) for lanes in LANES],
         in_specs=[anywhere] * 4,
         out_specs=[anywhere] * 4,
-        scratch_shapes=[dma((4,)), dma((4, 4)), dma((4, 4)), dma((4, 5)), dma((4, 5))],
+        scratch_shapes=[dma((16,)), dma((16, 4)), dma((16, 4)), dma((16, 5)), dma((16, 5))],
         compiler_params=pltpu.CompilerParams(collective_id=0, has_side_effects=True),
         name="gather_weights",
     )(*chunks)
@@ -415,57 +424,61 @@
     core = seq % 2
     greet([partner(dim) for dim in range(4)] + [sibling()])
     at = [place_of(q, dp, seq) for q in range(4)]
-    side, load = {}, {}
-    for part in range(2):
-        for q in range(4):
-            high = at[q] // 8
-            span = pl.ds(((1 - high) if part == 0 else high) * 8, 8)
-            side[q, part] = send(
-                parts[q].at[1 - core, span], acc[q].at[span],
-                sib_send.at[q, part], sib_recv.at[q, part], sibling(),
-            )
-            load[q, part] = pltpu.make_async_copy(
-                parts[q].at[core, span], own[q].at[span], own_sem.at[q, part]
-            )
-            load[q, part].start()
-
-    def add(q, base, other, other_base, count):
+    side, load, links = {}, {}, {}
+    for chunk, (q, r) in enumerate(CHUNKS):
+        rows = pl.ds(*ROW_CUTS[r])
+        side[chunk] = send(
+            parts[q].at[1 - core, :, rows], acc[q].at[:, rows],
+            sib_send.at[chunk], sib_recv.at[chunk], sibling(),
+        )
+        load[chunk] = pltpu.make_async_copy(
+            parts[q].at[core, :, rows], own[q].at[:, rows], own_sem.at[chunk]
+        )
+        load[chunk].start()
+
+    def add(chunk, base, other, other_base, count):
+        q, r = CHUNKS[chunk]
+        rows = pl.ds(*ROW_CUTS[r])
+
         def one(b, carry):
-            acc[q][base + b] = acc[q][base + b] + other[other_base + b]
+            acc[q][base + b, rows] = acc[q][base + b, rows] + other[other_base + b, rows]
             return carry
 
         lax.fori_loop(0, count, one, 0)
 
-    links = {}
-    for part in range(2):
-        for q in range(4):
-            side[q, part].wait_recv()
-            load[q, part].wait()
-            high = at[q] // 8
-            base = ((1 - high) if part == 0 else high) * 8
-            add(q, base, own[q], base, 8)
-            if part == 0:
-                links[q, 3] = send(
-                    acc[q].at[pl.ds(base, 8)], got3[q], link_send.at[q, 3], link_recv.at[q, 3],
-                    partner(ORDERS[q][3]),
-                )
-    for stage in (3, 2, 1):
-        half = 2 ** (stage - 1)
-        for q in range(4):
-            links[q, stage].wait_recv()
-            base = at[q] // (2 * half) * (2 * half)
-            high = at[q] // half % 2
-            away, keep = (1 - high) * half, high * half
-            add(q, base + away, got[stage][q], away, half)
-            links[q, stage - 1] = send(
-                acc[q].at[pl.ds(base + away, half)], got[stage - 1][q],
-                link_send.at[q, stage - 1], link_recv.at[q, stage - 1],
-                partner(ORDERS[q][stage - 1]),
-            )
-            add(q, base + keep, got[stage][q], keep, half)
-    for q in range(4):
-        links[q, 0].wait_recv()
-        outs[q][...] = acc[q][at[q]] + got0[q][0]
+    def step(chunk, stage):
+        q, r = CHUNKS[chunk]
+        rows = pl.ds(*ROW_CUTS[r])
+        half = 2**stage
+        base = at[q] // (2 * half) * (2 * half)
+        high = at[q] // half % 2
+        away, keep = (1 - high) * half, high * half
+        if stage == 3:
+            side[chunk].wait_recv()
+            load[chunk].wait()
+            other = own[q]
+        else:
+            links[chunk, stage + 1].wait_recv()
+            other = got[stage + 1][q]
+        add(chunk, base + away, other, away, half)
+        links[chunk, stage] = send(
+            acc[q].at[pl.ds(base + away, half), rows], got[stage][q].at[:, rows],
+            link_send.at[chunk, stage], link_recv.at[chunk, stage], partner(ORDERS[q][stage]),
+        )
+        add(chunk, base + keep, other, keep, half)
+
+    for turn in range(len(CHUNKS) + SCATTER_LAGS[4]):
+        for stage in (-1, 0, 1, 2, 3):
+            lag = SCATTER_LAGS[3 - stage]
+            chunk = turn - lag
+            if 0 <= chunk < len(CHUNKS):
+                if stage >= 0:
+                    step(chunk, stage)
+                    continue
+                q, r = CHUNKS[chunk]
+                rows = pl.ds(*ROW_CUTS[r])
+                links[chunk, 0].wait_recv()
+                outs[q][rows] = acc[q][at[q], rows] + got0[q][0, rows]
     for copy in list(side.values()) + list(links.values()):
         copy.wait_send()
 
@@ -482,7 +495,7 @@
         out_shape=[jax.ShapeDtypeStruct((rows, lanes), bf16) for lanes in LANES],
         in_specs=[pl.BlockSpec(memory_space=pl.ANY)] * 4,
         out_specs=[pl.BlockSpec(memory_space=pltpu.VMEM)] * 4,
-        scratch_shapes=buffers + [dma((4, 2)), dma((4, 4)), dma((4, 4)), dma((4, 2)), dma((4, 2))],
+        scratch_shapes=buffers + [dma((16,)), dma((16, 4)), dma((16, 4)), dma((16,)), dma((16,))],
         compiler_params=pltpu.CompilerParams(
             collective_id=1, has_side_effects=True, vmem_limit_bytes=56 * 2**20
         ),
@@ -525,23 +538,29 @@
 
 
 def unpack_kernel(c0, c1, c2, c3, qkv, out, up, down, norms):
-    for dp, s, core, at in spots():
-        qkv[dp, :, s * 408 : s * 408 + 384] = c0[core, at[0]]
-        mixed = c1[core, at[1]]
-        rem = mixed[:, TILE : 2 * TILE]
-        out[dp, :, s * 136 : s * 136 + 128] = mixed[:, :TILE]
-        up[dp, :, s * 544 : s * 544 + 128] = mixed[:, 2 * TILE :]
-        up[dp, :, s * 544 + 128 : s * 544 + 512] = c2[core, at[2]]
-        up[dp, :, s * 544 + 512 : s * 544 + 544] = rem[:, REM_UP : REM_UP + 32]
-        qkv[dp, :, s * 408 + 384 : s * 408 + 408] = rem[:, REM_QKV : REM_QKV + 24]
-        out[dp, :, s * 136 + 128 : s * 136 + 136] = rem[:, REM_OUT : REM_OUT + 8]
+    for dp in range(4):
+        pieces = [[] for _ in range(7)]
+        for s in range(8):
+            at = [place_of(q, dp, s) for q in range(4)]
+            core = s % 2
+            rem = c1[core, at[1], :, TILE : 2 * TILE]
+            if s == 0:
+                norms[dp] = rem
+            pieces[0] += [c0[core, at[0]], rem[:, REM_QKV : REM_QKV + 24]]
+            pieces[1] += [c1[core, at[1], :, :TILE], rem[:, REM_OUT : REM_OUT + 8]]
+            pieces[2] += [
+                c1[core, at[1], :, 2 * TILE :], c2[core, at[2]], rem[:, REM_UP : REM_UP + 32]
+            ]
+            for i in range(4):
+                pieces[3 + i] += [
+                    c3[core, at[3], :, i * TILE : (i + 1) * TILE],
+                    rem[:, REM_DOWN + 8 * i : REM_DOWN + 8 * i + 8],
+                ]
+        qkv[dp] = jnp.concatenate(pieces[0], 1)
+        out[dp] = jnp.concatenate(pieces[1], 1)
+        up[dp] = jnp.concatenate(pieces[2], 1)
         for i in range(4):
-            down[dp * 4 + i, :, s * 136 : s * 136 + 128] = c3[core, at[3], :, i * TILE : (i + 1) * TILE]
-            down[dp * 4 + i, :, s * 136 + 128 : s * 136 + 136] = rem[
-                :, REM_DOWN + 8 * i : REM_DOWN + 8 * i + 8
-            ]
-        if s == 0:
-            norms[dp] = rem
+            down[dp * 4 + i] = jnp.concatenate(pieces[3 + i], 1)
 
 
 def unpack_weights(chunks):

time: 858 us -> 696 us (0.81)
  Pallas kernels: 713 us -> 551 us
    pallas_call x1, Pallas kernels: 190 us -> 27.2 us  [unpack_weights(): pl.pallas_call(unpack_kernel, grid=(rows // step,), out_shape=[jax.ShapeD...]
    pallas_call x1, Pallas kernels: 170 us -> 180 us  [scatter_grads(): pl.pallas_call(scatter_kernel, out_shape=[jax.ShapeDtypeStruct((rows, lan...]
where the time goes in v2:
time: 696 us; the launch traced here: 691 us
  Pallas kernels  551 us (79%)
  matrix products  72.5 us (10%)
  local copies, waits for them, and re-layouts  59.3 us (9%)
  other arithmetic  7.13 us (1%)
    pallas_call x1, Pallas kernels, scatter_grads(): pl.pallas_call(scatter_kernel, out_shape=[jax.ShapeDtypeStruct((rows, lan...  180 us
    pallas_call x1, Pallas kernels, gather_weights(): pl.pallas_call(gather_kernel, out_shape=[jax.ShapeDtypeStruct((2, 16, row...  170 us
    pallas_call x4, Pallas kernels, exchange(): pl.pallas_call(exchange_kernel, out_shape=jax.ShapeDtypeStruct(blocks.sha...  116 us
    dot_general x4, matrix products, dot_right_t(): lax.dot_general(left, right, (((1,), (1,)), ((), ())), preferred_element_...  32.9 us
    pallas_call x1, Pallas kernels, pack_grads(): pl.pallas_call(pack_kernel, grid=(rows // step,), out_shape=[jax.ShapeDty...  28.1 us
    pallas_call x1, Pallas kernels, unpack_weights(): pl.pallas_call(unpack_kernel, grid=(rows // step,), out_shape=[jax.ShapeD...  27.2 us
    unnamed x84, local copies, waits for them, and re-layouts  18.7 us
    dot_general x4, matrix products, dot_left_t(): lax.dot_general(left, right, (((0,), (0,)), ((), ())), preferred_element_...  17.1 us

profile of v2, /device:TPU:0, one launch (start us, length us, event | category | flops | bytes accessed | tf_op | source)
XLA Modules:
  0.0 691.2 jit_solution(15612079819028315370)
XLA Ops:
  0.7 1.7 slice.155.refs_0_
  2.4 0.9 slice.156
  4.3 0.9 fusion.35
  8.2 1.1 concatenate.30.refs_1_
  11.5 170.0 %gather_weights.1 = (bf16[2,16,272,384]{3,2,1,0:T(8,128)(2,1)}, bf16[2,16,272,384]{3,2,1,0:T(8,128)(2,1)}, bf16[2,16,272,384]{3,2,1,0:T(8,128)(2,1)}, bf16[2,16,272,512]{3,2,1,0:T(8,128)(2,1)}) custom-call(bf16[272,384]{1,0:T(8,128)(2,1)} %slice.155.refs_0_, bf16[272,384]{1,0:T(8,128)(2,1)} %concatenate.30.refs_1_, bf16[272,384]{1,0:T(8,128)(2,1)} %slice.165.refs_2_, ...), custom_call_target="tpu_custom_call" | custom-call | tf_op jit(solution)/shard_map/gather_weights/pallas_call | solution.py:407
  181.5 2.9 copy-done.5
  184.4 27.2 %unpack_weights.1 = (bf16[4,272,3264]{2,1,0:T(8,128)(2,1)}, bf16[4,272,1088]{2,1,0:T(8,128)(2,1)S(1)}, bf16[4,272,4352]{2,1,0:T(8,128)(2,1)}, bf16[16,272,1088]{2,1,0:T(8,128)(2,1)}, bf16[4,272,128]{2,1,0:T(8,128)(2,1)S(1)}) custom-call(bf16[2,16,272,384]{3,2,1,0:T(8,128)(2,1)S(1)} %copy-done.5, bf16[2,16,272,384]{3,2,1,0:T(8,128)(2,1)} %get-tuple-element.30.c1, ...), custom_call_target="tpu_custom_call" | custom-call | tf_op jit(solution)/shard_map/unpack_weights/pallas_call | solution.py:574
  211.6 1.5 copy-done.9
  216.0 6.7 convolution_convert_fusion.4
  222.7 3.5 reshape.357
  226.7 1.6 pad.12
  228.3 33.8 %exchange_0.1.x = bf16[8,5,192,128]{3,2,1,0:T(8,128)(2,1)} custom-call(bf16[8,5,192,128]{3,2,1,0:T(8,128)(2,1)} %bitcast.138), custom_call_target="tpu_custom_call" | custom-call | tf_op jit(solution)/shard_map/exchange_0/pallas_call | solution.py:523
  263.6 12.9 %attend.1 = (bf16[8,5,64,128]{3,2,1,0:T(8,128)(2,1)S(1)}, f32[5,1,1024]{2,1,0:T(1,128)S(1)}) custom-call(s32[5,8]{1,0:T(8,128)S(1)} %broadcast_select_fusion.2.order, bf16[8,5,192,128]{3,2,1,0:T(8,128)(2,1)S(1)} %copy-done.2, s32[5,1024,1]{2,1,0:T(8,128)S(1)} %broadcast_select_fusion.seg_k, s32[5,1,1024]{2,1,0:T(1,128)S(1)} %broadcast_select_fusion.1.seg_q), custom_call_target="tpu_custom_call" | custom-call | tf_op jit(solution)/shard_map/attend/pallas_call | solution.py:665
  277.4 25.2 %exchange_1.1 = bf16[8,5,64,128]{3,2,1,0:T(8,128)(2,1)} custom-call(bf16[8,5,64,128]{3,2,1,0:T(8,128)(2,1)} %copy-done.8), custom_call_target="tpu_custom_call" | custom-call | tf_op jit(solution)/shard_map/exchange_1/pallas_call | solution.py:523
  302.6 1.1 slice.201
  304.3 1.2 fusion.40
  305.8 6.3 fusion.33
  312.1 2.1 copy-done.19
  314.2 8.3 %fusion.14 = bf16[136,2,8,128]{3,2,1,0:T(8,128)(2,1)S(1)} fusion(f32[256,1088]{0,1:T(8,128)S(1)} %get-tuple-element.132, bf16[4352,1088]{1,0:T(8,128)(2,1)} %bitcast.164, f32[256,4352]{1,0:T(8,128)S(1)} %fusion.33), kind=kOutput, calls=%fused_computation.32 | convolution fusion | flops 2434891776 | bytes 15597568 | tf_op jit(solution)/shard_map/dot_general | solution.py:87
  323.4 22.7 %fusion.3 = bf16[256,4352]{1,0:T(8,128)(2,1)S(1)} fusion(f32[256,4352]{1,0:T(8,128)} %copy-done.19, bf16[4352,1088]{1,0:T(8,128)(2,1)} %bitcast.165, bf16[2,128,1088]{1,2,0:T(8,128)(2,1)S(1)} %copy-done), kind=kOutput, calls=%fused_computation.13 | convolution fusion | flops 2451046400 | bytes 16711680 | tf_op jit(solution)/shard_map/dot_general | solution.py:91
  346.1 3.0 multiply_reduce_fusion
  349.5 1.0 copy-done.14
  350.5 1.7 convolution_convert_fusion.5
  352.2 1.7 reshape.368
  354.1 0.9 pad.13
  355.0 17.8 %exchange_2.1.g = bf16[8,5,64,128]{3,2,1,0:T(8,128)(2,1)} custom-call(bf16[8,5,64,128]{3,2,1,0:T(8,128)(2,1)} %bitcast.149), custom_call_target="tpu_custom_call" | custom-call | tf_op jit(solution)/shard_map/exchange_2/pallas_call | solution.py:523
  372.9 1.1 copy-done.7
  374.0 16.3 %attend_back.1.blocks = bf16[8,5,192,128]{3,2,1,0:T(8,128)(2,1)S(1)} custom-call(s32[5,8]{1,0:T(8,128)S(1)} %broadcast_select_fusion.2.order, bf16[8,5,192,128]{3,2,1,0:T(8,128)(2,1)S(1)} %copy-done.3, bf16[8,5,64,128]{3,2,1,0:T(8,128)(2,1)S(1)} %copy-done.7, s32[5,1024,1]{2,1,0:T(8,128)} %copy-done.1, s32[5,1,1024]{2,1,0:T(1,128)S(1)} %broadcast_select_fusion.1.seg_q, ...), custom_call_target="tpu_custom_call" | custom-call | tf_op jit(solution)/shard_map/attend_back/pallas_call | solution.py:739
  390.3 1.3 copy-done.4
  391.6 38.9 %exchange_3.1 = bf16[8,5,192,128]{3,2,1,0:T(8,128)(2,1)} custom-call(bf16[8,5,192,128]{3,2,1,0:T(8,128)(2,1)} %copy-done.4), custom_call_target="tpu_custom_call" | custom-call | tf_op jit(solution)/shard_map/exchange_3/pallas_call | solution.py:523
  430.6 1.6 slice.204
  432.1 1.7 copy.120
  433.9 5.5 multiply_reduce_fusion.1
  439.4 1.2 copy_bitcast_fusion
  440.7 5.2 convolution_convert_fusion.2
  445.9 0.9 convolution_convert_fusion.3
  447.2 5.5 convolution_convert_fusion.1
  452.6 5.5 convolution_convert_fusion
  458.1 13.9 %copy.121 = bf16[4352,1088]{1,0:T(8,128)(2,1)} copy(bf16[4352,1088]{0,1:T(8,128)(2,1)} %convolution_convert_fusion) | data formatting | bytes 18939904 | tf_op jit(solution)/shard_map/convert_element_type | solution.py:852
  472.5 28.1 %pack_grads.1 = (bf16[2,16,272,384]{3,2,1,0:T(8,128)(2,1)S(1)}, bf16[2,16,272,384]{3,2,1,0:T(8,128)(2,1)}, bf16[2,16,272,384]{3,2,1,0:T(8,128)(2,1)}, bf16[2,16,272,512]{3,2,1,0:T(8,128)(2,1)}) custom-call(bf16[4,272,3264]{2,1,0:T(8,128)(2,1)} %bitcast.132, bf16[4,272,1088]{2,1,0:T(8,128)(2,1)S(1)} %bitcast.127, bf16[4,272,4352]{2,1,0:T(8,128)(2,1)} %bitcast.131, ...), custom_call_target="tpu_custom_call" | custom-call | tf_op jit(solution)/shard_map/pack_grads/pallas_call | solution.py:608
  500.6 2.7 copy-done.6
  503.4 180.3 %scatter_grads.1 = (bf16[272,384]{1,0:T(8,128)(2,1)}, bf16[272,384]{1,0:T(8,128)(2,1)}, bf16[272,384]{1,0:T(8,128)(2,1)}, bf16[272,512]{1,0:T(8,128)(2,1)}) custom-call(bf16[2,16,272,384]{3,2,1,0:T(8,128)(2,1)} %copy-done.6, bf16[2,16,272,384]{3,2,1,0:T(8,128)(2,1)} %get-tuple-element.41.refs_1_, bf16[2,16,272,384]{3,2,1,0:T(8,128)(2,1)} %get-tuple-element.42.refs_2_, ...), custom_call_target="tpu_custom_call" | custom-call | tf_op jit(solution)/shard_map/scatter_grads/pallas_call | solution.py:493
  683.7 1.0 slice.205
  684.7 1.0 convert_element_type.104
  685.7 0.9 pad_maximum_fusion.1
  687.7 0.9 pad_maximum_fusion
  688.7 1.2 copy.126
  690.0 1.0 slice_reduce_fusion
  (144 shorter events, 15.8 us)
Async XLA Ops:
  0.6 322.7 %copy-start = (bf16[2,128,1088]{1,2,0:T(8,128)(2,1)S(1)}, bf16[2,128,1088]{1,2,0:T(8,128)(2,1)}, u32[]{:S(2)}) copy-start(bf16[2,128,1088]{1,2,0:T(8,128)(2,1)} %param.13) | copy-start | bytes 1671172
  0.7 7.5 %slice-start.7 = ((bf16[272,408]{1,0:T(8,128)(2,1)}), bf16[272,24]{1,0:T(8,128)(2,1)S(1)}, s32[]{:S(2)}) async-start(bf16[272,408]{1,0:T(8,128)(2,1)} %param.14), calls=%async_computation.7 | async-start | bytes 139264 | tf_op jit(solution)/shard_map/slice | solution.py:799
  0.7 7.5 %slice-start.5 = ((bf16[272,544]{1,0:T(8,128)(2,1)}), bf16[272,32]{1,0:T(8,128)(2,1)S(1)}, s32[]{:S(2)}) async-start(bf16[272,544]{1,0:T(8,128)(2,1)} %param.16), calls=%async_computation.5 | async-start | bytes 139264 | tf_op jit(solution)/shard_map/slice | solution.py:799
  0.7 7.5 %slice-start.6 = ((bf16[272,544]{1,0:T(8,128)(2,1)}), bf16[272,128]{1,0:T(8,128)(2,1)S(1)}, s32[]{:S(2)}) async-start(bf16[272,544]{1,0:T(8,128)(2,1)} %param.16), calls=%async_computation.6 | async-start | bytes 139264 | tf_op jit(solution)/shard_map/slice | solution.py:807
  0.7 8.7 %copy-start.28 = (bf16[272,544]{1,0:T(8,128)(2,1)S(1)}, bf16[272,544]{1,0:T(8,128)(2,1)}, u32[]{:S(2)}) copy-start(bf16[272,544]{1,0:T(8,128)(2,1)} %param.16) | copy-start | bytes 887812
  0.7 7.4 %copy-start.30 = (bf16[272]{0:T(512)(128)(2,1)S(1)}, bf16[272]{0:T(512)(128)(2,1)}, u32[]{:S(2)}) copy-start(bf16[272]{0:T(512)(128)(2,1)} %param.21) | copy-start | bytes 1636
  2.4 7.6 %copy-start.27 = (bf16[1088,136]{0,1:T(8,128)(2,1)S(1)}, bf16[1088,136]{0,1:T(8,128)(2,1)}, u32[]{:S(2)}) copy-start(bf16[1088,136]{0,1:T(8,128)(2,1)} %param.17) | copy-start | bytes 887812
  181.5 2.9 copy-start.5
  184.4 28.7 %copy-start.32 = (s32[2,1,8]{2,1,0:T(1,128)S(1)}, s32[2,1,8]{2,1,0:T(1,128)}, u32[]{:S(2)}) copy-start(s32[2,1,8]{2,1,0:T(1,128)} %param.23) | copy-start | bytes 196
  211.6 1.5 copy-start.9
  213.1 1.1 copy-start.16
  215.2 0.8 copy-start.20
  228.3 33.8 %copy-start.31 = (s32[2,1,8]{2,1,0:T(1,128)S(1)}, s32[2,1,8]{2,1,0:T(1,128)}, u32[]{:S(2)}) copy-start(s32[2,1,8]{2,1,0:T(1,128)} %param.22) | copy-start | bytes 196
  262.0 1.5 copy-start.2
  262.7 13.8 %copy-start.1 = (s32[5,1024,1]{2,1,0:T(8,128)}, s32[5,1024,1]{2,1,0:T(8,128)S(1)}, u32[]{:S(2)}) copy-start(s32[5,1024,1]{2,1,0:T(8,128)S(1)} %broadcast_select_fusion.seg_k) | copy-start | bytes 61444
  276.5 0.8 copy-start.8
  277.3 27.0 %copy-start.10 = (bf16[4,272,1088]{2,1,0:T(8,128)(2,1)S(1)}, bf16[4,272,1088]{2,1,0:T(8,128)(2,1)}, u32[]{:S(2)}) copy-start(bf16[4,272,1088]{2,1,0:T(8,128)(2,1)} %copy-done.9) | copy-start | bytes 7102468
  302.6 1.8 copy-start.17
  304.3 1.3 copy-start.24
  305.6 43.5 %copy-start.11 = (f32[256,1088]{0,1:T(8,128)}, f32[256,1088]{0,1:T(8,128)S(1)}, u32[]{:S(2)}) copy-start(f32[256,1088]{0,1:T(8,128)S(1)} %get-tuple-element.132) | copy-start | bytes 3342340
  312.1 2.1 copy-start.19
  314.2 31.8 %slice-start = ((s8[9469952]{0:T(1024)(128)(4,1)}), s8[4194304]{0:T(1024)(128)(4,1)S(1)}, s32[]{:S(2)}) async-start(s8[9469952]{0:T(1024)(128)(4,1)} %bitcast.135), calls=%async_computation | async-start | bytes 8388608
  322.5 23.5 %slice-start.1 = ((s8[9469952]{0:T(1024)(128)(4,1)}), s8[4194304]{0:T(1024)(128)(4,1)S(1)}, s32[]{:S(2)}) async-start(s8[9469952]{0:T(1024)(128)(4,1)} %bitcast.135), calls=%async_computation.1 | async-start | bytes 8388608
  323.4 22.7 %slice-start.2 = ((s8[9469952]{0:T(1024)(128)(4,1)}), s8[1081344]{0:T(1024)(128)(4,1)S(1)}, s32[]{:S(2)}) async-start(s8[9469952]{0:T(1024)(128)(4,1)} %bitcast.135), calls=%async_computation.2 | async-start | bytes 2162688
  346.1 3.0 copy-start.22
  349.5 1.0 copy-start.14
  354.0 18.9 %copy-start.3 = (bf16[8,5,192,128]{3,2,1,0:T(8,128)(2,1)S(1)}, bf16[8,5,192,128]{3,2,1,0:T(8,128)(2,1)}, u32[]{:S(2)}) copy-start(bf16[8,5,192,128]{3,2,1,0:T(8,128)(2,1)} %exchange_0.1.x) | copy-start | bytes 5898244
  372.9 1.1 copy-start.7
  390.3 1.4 copy-start.4
  432.1 1.7 copy-start.18
  433.9 5.6 copy-start.15
  439.4 1.2 copy-start.21
  440.7 5.2 copy-start.25
  440.7 6.2 copy-start.23
  445.9 1.2 copy-start.12
  445.9 6.7 slice-start.3
  447.2 5.5 slice-start.4
  500.6 2.7 copy-start.6
  683.7 2.9 copy-start.13
  686.6 1.1 copy-start.29
  686.7 1.8 copy-start.26

commit v3 on v2

--- a/solution.py
+++ b/solution.py
@@ -303,8 +303,9 @@
 ORDERS = ((2, 0, 3, 1), (2, 1, 3, 0), (3, 0, 2, 1), (3, 1, 2, 0))
 ROW_CUTS = ((0, 64), (64, 64), (128, 64), (192, 80))
 CHUNKS = tuple((q, r) for pair in ((0, 1), (2, 3)) for r in range(4) for q in pair)
-GATHER_LAGS = (0, 1, 2, 3, 5)
-SCATTER_LAGS = (0, 2, 3, 4, 6)
+GATHER_LAGS = (0, 2, 4, 6, 9)
+SCATTER_LAGS = (0, 3, 5, 7, 9)
+AHEAD = 4
 TILE = 128
 LANES = (3 * TILE, 3 * TILE, 3 * TILE, 4 * TILE)
 UNITS = 5
@@ -425,7 +426,9 @@
     greet([partner(dim) for dim in range(4)] + [sibling()])
     at = [place_of(q, dp, seq) for q in range(4)]
     side, load, links = {}, {}, {}
-    for chunk, (q, r) in enumerate(CHUNKS):
+
+    def begin(chunk):
+        q, r = CHUNKS[chunk]
         rows = pl.ds(*ROW_CUTS[r])
         side[chunk] = send(
             parts[q].at[1 - core, :, rows], acc[q].at[:, rows],
@@ -435,6 +438,9 @@
             parts[q].at[core, :, rows], own[q].at[:, rows], own_sem.at[chunk]
         )
         load[chunk].start()
+
+    for chunk in range(AHEAD):
+        begin(chunk)
 
     def add(chunk, base, other, other_base, count):
         q, r = CHUNKS[chunk]
@@ -468,6 +474,8 @@
         add(chunk, base + keep, other, keep, half)
 
     for turn in range(len(CHUNKS) + SCATTER_LAGS[4]):
+        if turn + AHEAD < len(CHUNKS):
+            begin(turn + AHEAD)
         for stage in (-1, 0, 1, 2, 3):
             lag = SCATTER_LAGS[3 - stage]
             chunk = turn - lag
@@ -621,6 +629,32 @@
 
 def flip(block):
     return block.astype(jnp.float32).T.astype(jnp.bfloat16)
+
+
+def outer_kernel(left, right, out):
+    out[...] = dot(flip(left[...]), right[...]).astype(out.dtype)
+
+
+def outer(left, right):
+    rows, width = left.shape
+    step = 2 * TILE
+    return pl.pallas_call(
+        outer_kernel,
+        grid=(width // step,),
+        out_shape=jax.ShapeDtypeStruct((width, right.shape[1]), jnp.bfloat16),
+        in_specs=[
+            pl.BlockSpec((rows, step), lambda i: (0, i)),
+            pl.BlockSpec(right.shape, lambda i: (0, 0)),
+        ],
+        out_specs=pl.BlockSpec((step, right.shape[1]), lambda i: (i, 0)),
+        compiler_params=pltpu.CompilerParams(vmem_limit_bytes=24 * 2**20),
+        cost_estimate=pl.CostEstimate(
+            flops=2 * rows * width * right.shape[1],
+            bytes_accessed=2 * width * (right.shape[1] + rows),
+            transcendentals=0,
+        ),
+        name="outer",
+    )(left, right)
 
 
 def masked_scores(k_rows, q_cols, seg_k, seg_q, start, scale):
@@ -849,7 +883,7 @@
     grad_rows = cotangent.reshape(rows, width)
     block_out = (middle + dot(activated, full_down)).astype(bf16)
     grad_hidden = gelu_back(dot_right_t(grad_rows, full_down))[0].astype(bf16)
-    sum_down = dot_left_t(activated, grad_rows).astype(bf16)
+    sum_down = outer(activated, grad_rows)
     sum_up = dot_left_t(normed_two, grad_hidden).astype(bf16)
     grad_normed_two = dot_right_t(grad_hidden, full_up)
     grad_middle = grad_rows.astype(f32) + norm_back(grad_normed_two, scaled_two, inv_two, g_two)

time: 696 us -> 668 us (0.960)
  Pallas kernels: 551 us -> 536 us
  matrix products: 72.5 us -> 60.6 us
  local copies, waits for them, and re-layouts: 59.3 us -> 50.3 us
    pallas_call x1, Pallas kernels: 180 us -> 165 us  [scatter_grads(): pl.pallas_call(scatter_kernel, out_shape=[jax.ShapeDtypeStruct((rows, lan...]
    pallas_call x1, Pallas kernels: 170 us -> 157 us  [gather_weights(): pl.pallas_call(gather_kernel, out_shape=[jax.ShapeDtypeStruct((2, 16, row...]
    convert_element_type x1, local copies, waits for them, and re-layouts: 13.9 us -> 2.38 us  [shards_fast(): residual = tokens.astype(f32).reshape(rows, width)]
    unnamed x84 -> x99, local copies, waits for them, and re-layouts: 18.7 us -> 26.4 us
    dot_general x4, matrix products: 32.9 us -> 25.4 us  [dot_right_t(): lax.dot_general(left, right, (((1,), (1,)), ((), ())), preferred_element_...]
    pallas_call x0 -> x1, Pallas kernels: none -> 6.96 us  [outer(): pl.pallas_call(outer_kernel, grid=(width // step,), out_shape=jax.ShapeDt...]
    dot_general x4 -> x3, matrix products: 17.1 us -> 14.2 us  [dot_left_t(): lax.dot_general(left, right, (((0,), (0,)), ((), ())), preferred_element_...]
where the time goes in v3:
time: 668 us; the launch traced here: 659 us
  Pallas kernels  536 us (80%)
  matrix products  60.6 us (9%)
  local copies, waits for them, and re-layouts  50.3 us (8%)
  other arithmetic  10.2 us (2%)
    pallas_call x1, Pallas kernels, scatter_grads(): pl.pallas_call(scatter_kernel, out_shape=[jax.ShapeDtypeStruct((rows, lan...  165 us
    pallas_call x1, Pallas kernels, gather_weights(): pl.pallas_call(gather_kernel, out_shape=[jax.ShapeDtypeStruct((2, 16, row...  157 us
    pallas_call x4, Pallas kernels, exchange(): pl.pallas_call(exchange_kernel, out_shape=jax.ShapeDtypeStruct(blocks.sha...  122 us
    pallas_call x1, Pallas kernels, pack_grads(): pl.pallas_call(pack_kernel, grid=(rows // step,), out_shape=[jax.ShapeDty...  28.1 us
    pallas_call x1, Pallas kernels, unpack_weights(): pl.pallas_call(unpack_kernel, grid=(rows // step,), out_shape=[jax.ShapeD...  27.2 us
    unnamed x99, local copies, waits for them, and re-layouts  26.4 us
    dot_general x4, matrix products, dot_right_t(): lax.dot_general(left, right, (((1,), (1,)), ((), ())), preferred_element_...  25.4 us
    pallas_call x1, Pallas kernels, attend_back(): pl.pallas_call(functools.partial(attend_back_kernel, scale), grid_spec=pl...  16.4 us

profile of v3, /device:TPU:0, one launch (start us, length us, event | category | flops | bytes accessed | tf_op | source)
XLA Modules:
  0.0 659.1 jit_solution(3089513575747693460)
XLA Ops:
  0.8 2.4 copy.113
  5.2 1.1 concatenate.30.refs_1_
  8.5 157.1 %gather_weights.1 = (bf16[2,16,272,384]{3,2,1,0:T(8,128)(2,1)}, bf16[2,16,272,384]{3,2,1,0:T(8,128)(2,1)}, bf16[2,16,272,384]{3,2,1,0:T(8,128)(2,1)}, bf16[2,16,272,512]{3,2,1,0:T(8,128)(2,1)}) custom-call(bf16[272,384]{1,0:T(8,128)(2,1)} %slice.155.refs_0_, bf16[272,384]{1,0:T(8,128)(2,1)} %concatenate.30.refs_1_, bf16[272,384]{1,0:T(8,128)(2,1)} %slice.165.refs_2_, ...), custom_call_target="tpu_custom_call" | custom-call | tf_op jit(solution)/shard_map/gather_weights/pallas_call | solution.py:408
  165.6 2.9 copy-done.7
  168.5 27.2 %unpack_weights.1 = (bf16[4,272,3264]{2,1,0:T(8,128)(2,1)}, bf16[4,272,1088]{2,1,0:T(8,128)(2,1)S(1)}, bf16[4,272,4352]{2,1,0:T(8,128)(2,1)}, bf16[16,272,1088]{2,1,0:T(8,128)(2,1)}, bf16[4,272,128]{2,1,0:T(8,128)(2,1)S(1)}) custom-call(bf16[2,16,272,384]{3,2,1,0:T(8,128)(2,1)S(1)} %copy-done.7, bf16[2,16,272,384]{3,2,1,0:T(8,128)(2,1)} %get-tuple-element.30.c1, ...), custom_call_target="tpu_custom_call" | custom-call | tf_op jit(solution)/shard_map/unpack_weights/pallas_call | solution.py:582
  195.6 1.5 copy-done.4
  200.0 5.5 convolution_convert_fusion.3
  206.4 1.6 pad.12
  208.0 40.8 %exchange_0.1.x = bf16[8,5,192,128]{3,2,1,0:T(8,128)(2,1)} custom-call(bf16[8,5,192,128]{3,2,1,0:T(8,128)(2,1)} %bitcast.108), custom_call_target="tpu_custom_call" | custom-call | tf_op jit(solution)/shard_map/exchange_0/pallas_call | solution.py:531
  250.4 12.8 %attend.1 = (bf16[8,5,64,128]{3,2,1,0:T(8,128)(2,1)S(1)}, f32[5,1,1024]{2,1,0:T(1,128)S(1)}) custom-call(s32[5,8]{1,0:T(8,128)S(1)} %broadcast_select_fusion.2.order, bf16[8,5,192,128]{3,2,1,0:T(8,128)(2,1)S(1)} %copy-done.2, s32[5,1024,1]{2,1,0:T(8,128)S(1)} %broadcast_select_fusion.seg_k, s32[5,1,1024]{2,1,0:T(1,128)S(1)} %broadcast_select_fusion.1.seg_q), custom_call_target="tpu_custom_call" | custom-call | tf_op jit(solution)/shard_map/attend/pallas_call | solution.py:699
  264.0 24.9 %exchange_1.1 = bf16[8,5,64,128]{3,2,1,0:T(8,128)(2,1)} custom-call(bf16[8,5,64,128]{3,2,1,0:T(8,128)(2,1)} %copy-done.12), custom_call_target="tpu_custom_call" | custom-call | tf_op jit(solution)/shard_map/exchange_1/pallas_call | solution.py:531
  288.9 1.1 slice.201
  290.6 2.6 fusion.28
  293.5 9.9 %multiply_convert_fusion = (bf16[256,4352]{1,0:T(8,128)(2,1)S(1)}, f32[256,4352]{1,0:T(8,128)}) fusion(bf16[1088,4352]{1,0:T(8,128)(2,1)} %bitcast.137, f32[256,1088]{1,0:T(8,128)S(1)} %get-tuple-element.130, f32[1088]{0:T(1024)S(1)} %get-tuple-element.99, f32[1088]{0:T(1024)S(1)} %get-tuple-element.98, f32[256]{0:T(256)S(1)} %add_rsqrt_fusion, ...), kind=kOutput, calls=%fused_computation.15 | convolution fusion | flops 2435727360 | bytes 17279488 | tf_op jit(solution)/shard_map/dot_general | solution.py:87
  303.5 3.0 fusion.6
  306.5 1.1 copy.143
  307.6 1.3 copy.134
  308.9 8.7 %fusion.3 = bf16[256,4352]{1,0:T(8,128)(2,1)S(1)} fusion(f32[256,4352]{1,0:T(8,128)} %get-tuple-element.132, bf16[4352,1088]{1,0:T(8,128)(2,1)} %bitcast.133, bf16[256,1088]{1,0:T(8,128)(2,1)S(1)} %bitcast.102), kind=kOutput, calls=%fused_computation.12 | convolution fusion | flops 2451046400 | bytes 16711680 | tf_op jit(solution)/shard_map/dot_general | solution.py:91
  317.7 8.2 %fusion.29 = (bf16[1088]{0:T(1024)(128)(2,1)S(1)}, f32[256,1088]{0,1:T(8,128)}) fusion(bf16[256,4352]{1,0:T(8,128)(2,1)S(1)} %fusion.3, bf16[1088,4352]{1,0:T(8,128)(2,1)} %bitcast.138), kind=kOutput, calls=%fused_computation.93 | convolution fusion | flops 2424585216 | bytes 12814464 | tf_op jit(solution)/shard_map/dot_general | solution.py:91
  325.9 2.7 copy.136
  328.5 2.3 multiply_reduce_fusion
  331.4 1.0 copy-done.17
  332.4 1.7 convolution_convert_fusion.4
  334.1 1.7 reshape.368
  336.0 0.9 pad.13
  336.9 17.8 %exchange_2.1.g = bf16[8,5,64,128]{3,2,1,0:T(8,128)(2,1)} custom-call(bf16[8,5,64,128]{3,2,1,0:T(8,128)(2,1)} %bitcast.119), custom_call_target="tpu_custom_call" | custom-call | tf_op jit(solution)/shard_map/exchange_2/pallas_call | solution.py:531
  354.8 1.1 copy-done.9
  355.9 16.4 %attend_back.1.blocks = bf16[8,5,192,128]{3,2,1,0:T(8,128)(2,1)S(1)} custom-call(s32[5,8]{1,0:T(8,128)S(1)} %broadcast_select_fusion.2.order, bf16[8,5,192,128]{3,2,1,0:T(8,128)(2,1)S(1)} %copy-done.3, bf16[8,5,64,128]{3,2,1,0:T(8,128)(2,1)S(1)} %copy-done.9, s32[5,1024,1]{2,1,0:T(8,128)} %copy-done.1, s32[5,1,1024]{2,1,0:T(1,128)S(1)} %broadcast_select_fusion.1.seg_q, ...), custom_call_target="tpu_custom_call" | custom-call | tf_op jit(solution)/shard_map/attend_back/pallas_call | solution.py:773
  372.3 1.3 copy-done.6
  373.6 38.9 %exchange_3.1 = bf16[8,5,192,128]{3,2,1,0:T(8,128)(2,1)} custom-call(bf16[8,5,192,128]{3,2,1,0:T(8,128)(2,1)} %copy-done.6), custom_call_target="tpu_custom_call" | custom-call | tf_op jit(solution)/shard_map/exchange_3/pallas_call | solution.py:531
  412.5 1.6 slice.204
  414.1 1.7 copy.138
  415.8 6.8 %fusion.30 = (bf16[1088]{0:T(1024)(128)(2,1)S(1)}, f32[256,1088]{0,1:T(8,128)}) fusion(bf16[1088,3264]{1,0:T(8,128)(2,1)} %bitcast.140, bf16[408,8,2,128]{3,2,1,0:T(2,128)(2,1)S(1)} %bitcast.110), kind=kOutput, calls=%fused_computation.94 | convolution fusion | flops 1818508288 | bytes 9889920 | tf_op jit(solution)/shard_map/dot_general | solution.py:91
  422.6 1.7 copy.139
  425.6 1.3 add_convert_fusion
  426.8 2.2 copy.144
  429.0 6.8 %convolution_convert_fusion.1 = bf16[1088,3264]{1,0:T(8,128)(2,1)} fusion(bf16[256,1088]{1,0:T(8,128)(2,1)S(1)} %bitcast.118, bf16[408,8,2,128]{3,2,1,0:T(2,128)(2,1)} %bitcast.111), kind=kOutput, calls=%fused_computation.1 | convolution fusion | flops 1821782016 | bytes 9330688 | tf_op jit(solution)/shard_map/dot_general | solution.py:95
  437.8 6.5 convolution_convert_fusion
  444.4 7.0 %outer.1 = bf16[4352,1088]{1,0:T(8,128)(2,1)S(1)} custom-call(bf16[256,4352]{1,0:T(8,128)(2,1)S(1)} %copy-done.11, bf16[256,1088]{1,0:T(8,128)(2,1)S(1)} %bitcast.103), custom_call_target="tpu_custom_call" | custom-call | flops 2424307712 | bytes 11698176 | tf_op jit(solution)/shard_map/outer/pallas_call | solution.py:641
  451.3 3.8 copy-done
  455.6 28.1 %pack_grads.1 = (bf16[2,16,272,384]{3,2,1,0:T(8,128)(2,1)S(1)}, bf16[2,16,272,384]{3,2,1,0:T(8,128)(2,1)}, bf16[2,16,272,384]{3,2,1,0:T(8,128)(2,1)}, bf16[2,16,272,512]{3,2,1,0:T(8,128)(2,1)}) custom-call(bf16[4,272,3264]{2,1,0:T(8,128)(2,1)} %bitcast.106, bf16[4,272,1088]{2,1,0:T(8,128)(2,1)S(1)} %bitcast.101, bf16[4,272,4352]{2,1,0:T(8,128)(2,1)} %bitcast.105, ...), custom_call_target="tpu_custom_call" | custom-call | tf_op jit(solution)/shard_map/pack_grads/pallas_call | solution.py:616
  483.7 2.7 copy-done.8
  486.4 165.1 %scatter_grads.1 = (bf16[272,384]{1,0:T(8,128)(2,1)}, bf16[272,384]{1,0:T(8,128)(2,1)}, bf16[272,384]{1,0:T(8,128)(2,1)}, bf16[272,512]{1,0:T(8,128)(2,1)}) custom-call(bf16[2,16,272,384]{3,2,1,0:T(8,128)(2,1)} %copy-done.8, bf16[2,16,272,384]{3,2,1,0:T(8,128)(2,1)} %get-tuple-element.41.refs_1_, bf16[2,16,272,384]{3,2,1,0:T(8,128)(2,1)} %get-tuple-element.42.refs_2_, ...), custom_call_target="tpu_custom_call" | custom-call | tf_op jit(solution)/shard_map/scatter_grads/pallas_call | solution.py:501
  651.5 1.0 slice.205
  652.5 1.0 convert_element_type.100
  655.5 0.9 pad_maximum_fusion
  656.5 1.2 copy.146
  657.8 1.0 slice_reduce_fusion
  (163 shorter events, 17.5 us)
Async XLA Ops:
  0.6 2.5 copy-start.33
  0.7 4.5 slice-start.4
  0.7 3.2 slice-start
  0.7 3.3 slice-start.1
  0.7 4.5 slice-start.2
  0.7 4.5 slice-start.3
  0.7 3.4 copy-start.31
  0.7 4.0 copy-start.35
  0.7 4.1 copy-start.36
  0.7 4.2 copy-start.37
  0.8 4.3 copy-start.38
  3.1 3.2 copy-start.32
  165.6 2.9 copy-start.7
  168.5 28.7 %copy-start.40 = (s32[2,1,8]{2,1,0:T(1,128)S(1)}, s32[2,1,8]{2,1,0:T(1,128)}, u32[]{:S(2)}) copy-start(s32[2,1,8]{2,1,0:T(1,128)} %param.23) | copy-start | bytes 196
  195.6 1.5 copy-start.4
  197.1 1.1 copy-start.22
  208.0 40.9 %copy-start.39 = (s32[2,1,8]{2,1,0:T(1,128)S(1)}, s32[2,1,8]{2,1,0:T(1,128)}, u32[]{:S(2)}) copy-start(s32[2,1,8]{2,1,0:T(1,128)} %param.22) | copy-start | bytes 196
  248.8 1.5 copy-start.2
  249.5 13.7 %copy-start.1 = (s32[5,1024,1]{2,1,0:T(8,128)}, s32[5,1024,1]{2,1,0:T(8,128)S(1)}, u32[]{:S(2)}) copy-start(s32[5,1024,1]{2,1,0:T(8,128)S(1)} %broadcast_select_fusion.seg_k) | copy-start | bytes 61444
  263.2 0.8 copy-start.12
  264.0 26.6 %copy-start.5 = (bf16[4,272,1088]{2,1,0:T(8,128)(2,1)S(1)}, bf16[4,272,1088]{2,1,0:T(8,128)(2,1)}, u32[]{:S(2)}) copy-start(bf16[4,272,1088]{2,1,0:T(8,128)(2,1)} %copy-done.4) | copy-start | bytes 7102468
  290.6 2.6 copy-start.24
  293.2 10.2 %copy-start.13 = (f32[256,1088]{1,0:T(8,128)}, f32[256,1088]{1,0:T(8,128)S(1)}, u32[]{:S(2)}) copy-start(f32[256,1088]{1,0:T(8,128)S(1)} %get-tuple-element.130) | copy-start | bytes 3342340
  293.2 10.2 %slice-start.5 = ((s8[10027008]{0:T(1024)(128)(4,1)}), s8[4194304]{0:T(1024)(128)(4,1)S(1)}, s32[]{:S(2)}) async-start(s8[10027008]{0:T(1024)(128)(4,1)} %bitcast.134), calls=%async_computation.5 | async-start | bytes 8388608
  293.5 9.9 %slice-start.6 = ((s8[10027008]{0:T(1024)(128)(4,1)}), s8[4194304]{0:T(1024)(128)(4,1)S(1)}, s32[]{:S(2)}) async-start(s8[10027008]{0:T(1024)(128)(4,1)} %bitcast.134), calls=%async_computation.6 | async-start | bytes 8388608
  293.5 9.9 %slice-start.7 = ((s8[10027008]{0:T(1024)(128)(4,1)}), s8[1638400]{0:T(1024)(128)(4,1)S(1)}, s32[]{:S(2)}) async-start(s8[10027008]{0:T(1024)(128)(4,1)} %bitcast.134), calls=%async_computation.7 | async-start | bytes 3276800
  303.4 3.1 copy-start.10
  317.7 8.2 %copy-start.28 = (bf16[256,4352]{1,0:T(8,128)(2,1)}, bf16[256,4352]{1,0:T(8,128)(2,1)S(1)}, u32[]{:S(2)}) copy-start(bf16[256,4352]{1,0:T(8,128)(2,1)S(1)} %fusion.3) | copy-start | bytes 6684676
  328.5 2.3 copy-start.14
  328.5 2.3 copy-start.20
  331.4 1.0 copy-start.17
  335.9 18.9 %copy-start.3 = (bf16[8,5,192,128]{3,2,1,0:T(8,128)(2,1)S(1)}, bf16[8,5,192,128]{3,2,1,0:T(8,128)(2,1)}, u32[]{:S(2)}) copy-start(bf16[8,5,192,128]{3,2,1,0:T(8,128)(2,1)} %exchange_0.1.x) | copy-start | bytes 5898244
  354.8 1.1 copy-start.9
  372.3 1.3 copy-start.6
  415.8 6.8 %copy-start.23 = (bf16[2,128,3,17,64]{1,0,4,3,2:T(2,128)(2,1)}, bf16[2,128,3,17,64]{1,0,4,3,2:T(2,128)(2,1)S(1)}, u32[]{:S(2)}) copy-start(bf16[2,128,3,17,64]{1,0,4,3,2:T(2,128)(2,1)S(1)} %copy.138) | copy-start | bytes 5013508
  422.6 1.7 copy-start.16
  424.3 1.3 copy-start.18
  426.8 2.2 copy-start.27
  429.0 6.8 %copy-start.19 = (f32[256,1088]{1,0:T(8,128)S(1)}, f32[256,1088]{1,0:T(8,128)}, u32[]{:S(2)}) copy-start(f32[256,1088]{1,0:T(8,128)} %copy-done.17) | copy-start | bytes 3342340
  429.0 6.8 %copy-start.25 = (bf16[2,128,1,17,64]{1,0,4,3,2:T(2,128)(2,1)S(1)}, bf16[2,128,1,17,64]{1,0,4,3,2:T(2,128)(2,1)}, u32[]{:S(2)}) copy-start(bf16[2,128,1,17,64]{1,0,4,3,2:T(2,128)(2,1)} %copy-done.24) | copy-start | bytes 1671172
  435.8 1.3 copy-start.15
  435.8 2.0 copy-start.29
  437.8 6.5 copy-start.11
  451.3 3.8 copy-start
  483.7 2.7 copy-start.8
  651.5 2.9 copy-start.21
  654.4 1.1 copy-start.34
  654.6 1.8 copy-start.30
  (1 other events, 0.8 us)

commit v4 on v3

--- a/solution.py
+++ b/solution.py
@@ -300,7 +300,8 @@
 
 
 MESH = pl.DeviceIdType.MESH
-ORDERS = ((2, 0, 3, 1), (2, 1, 3, 0), (3, 0, 2, 1), (3, 1, 2, 0))
+GATHER_ORDERS = ((2, 3, 0, 1), (2, 3, 1, 0), (2, 3, 0, 1), (2, 3, 1, 0))
+SCATTER_ORDERS = ((2, 3, 0, 1), (2, 3, 1, 0), (0, 2, 3, 1), (1, 3, 2, 0))
 ROW_CUTS = ((0, 64), (64, 64), (128, 64), (192, 80))
 CHUNKS = tuple((q, r) for pair in ((0, 1), (2, 3)) for r in range(4) for q in pair)
 GATHER_LAGS = (0, 2, 4, 6, 9)
@@ -312,10 +313,10 @@
 REM_UP, REM_QKV, REM_OUT, REM_DOWN, REM_NORM = 0, 32, 56, 64, 96
 
 
-def place_of(q, dp, seq):
+def place_of(order, dp, seq):
     z = seq // 2
     bits = (dp % 2, dp // 2, (z % 2 + z // 2) % 2, z // 2)
-    return sum(bits[dim] * 2**k for k, dim in enumerate(ORDERS[q]))
+    return sum(bits[dim] * 2**k for k, dim in enumerate(order))
 
 
 def partner(dim):
@@ -357,7 +358,7 @@
     dp, seq = lax.axis_index("dp"), lax.axis_index("seq")
     core = seq % 2
     greet([partner(dim) for dim in range(4)] + [sibling()])
-    at = [place_of(q, dp, seq) for q in range(4)]
+    at = [place_of(GATHER_ORDERS[q], dp, seq) for q in range(4)]
     owns, links, sides = {}, {}, []
 
     def step(chunk, stage):
@@ -368,7 +369,7 @@
             fresh, target = shards_in[q].at[span], full[q].at[core, at[q], span]
             links[chunk] = send(
                 fresh, target, link_send.at[chunk, 0], link_recv.at[chunk, 0],
-                partner(ORDERS[q][0]),
+                partner(GATHER_ORDERS[q][0]),
             )
             owns[chunk] = pltpu.make_async_copy(fresh, target, own_sem.at[chunk])
             owns[chunk].start()
@@ -383,7 +384,7 @@
             held = full[q].at[core, pl.ds(at[q] // size * size, size), span]
             links[chunk] = send(
                 held, held, link_send.at[chunk, stage], link_recv.at[chunk, stage],
-                partner(ORDERS[q][stage]),
+                partner(GATHER_ORDERS[q][stage]),
             )
         half = size // 2
         mine = at[q] // half
@@ -424,7 +425,7 @@
     dp, seq = lax.axis_index("dp"), lax.axis_index("seq")
     core = seq % 2
     greet([partner(dim) for dim in range(4)] + [sibling()])
-    at = [place_of(q, dp, seq) for q in range(4)]
+    at = [place_of(SCATTER_ORDERS[q], dp, seq) for q in range(4)]
     side, load, links = {}, {}, {}
 
     def begin(chunk):
@@ -469,7 +470,7 @@
         add(chunk, base + away, other, away, half)
         links[chunk, stage] = send(
             acc[q].at[pl.ds(base + away, half), rows], got[stage][q].at[:, rows],
-            link_send.at[chunk, stage], link_recv.at[chunk, stage], partner(ORDERS[q][stage]),
+            link_send.at[chunk, stage], link_recv.at[chunk, stage], partner(SCATTER_ORDERS[q][stage]),
         )
         add(chunk, base + keep, other, keep, half)
 
@@ -542,14 +543,14 @@
 def spots():
     for dp in range(4):
         for seq in range(8):
-            yield dp, seq, seq % 2, [place_of(q, dp, seq) for q in range(4)]
+            yield dp, seq, seq % 2, [place_of(SCATTER_ORDERS[q], dp, seq) for q in range(4)]
 
 
 def unpack_kernel(c0, c1, c2, c3, qkv, out, up, down, norms):
     for dp in range(4):
         pieces = [[] for _ in range(7)]
         for s in range(8):
-            at = [place_of(q, dp, s) for q in range(4)]
+            at = [place_of(GATHER_ORDERS[q], dp, s) for q in range(4)]
             core = s % 2
             rem = c1[core, at[1], :, TILE : 2 * TILE]
             if s == 0:

time: 668 us -> 640 us (0.958)
  Pallas kernels: 536 us -> 507 us
    pallas_call x1, Pallas kernels: 157 us -> 139 us  [gather_weights(): pl.pallas_call(gather_kernel, out_shape=[jax.ShapeDtypeStruct((2, 16, row...]
    pallas_call x1, Pallas kernels: 165 us -> 153 us  [scatter_grads(): pl.pallas_call(scatter_kernel, out_shape=[jax.ShapeDtypeStruct((rows, lan...]
where the time goes in v4:
time: 640 us; the launch traced here: 630 us
  Pallas kernels  507 us (79%)
  matrix products  60.6 us (9%)
  local copies, waits for them, and re-layouts  50.3 us (8%)
  other arithmetic  10.2 us (2%)
    pallas_call x1, Pallas kernels, scatter_grads(): pl.pallas_call(scatter_kernel, out_shape=[jax.ShapeDtypeStruct((rows, lan...  153 us
    pallas_call x1, Pallas kernels, gather_weights(): pl.pallas_call(gather_kernel, out_shape=[jax.ShapeDtypeStruct((2, 16, row...  139 us
    pallas_call x4, Pallas kernels, exchange(): pl.pallas_call(exchange_kernel, out_shape=jax.ShapeDtypeStruct(blocks.sha...  123 us
    pallas_call x1, Pallas kernels, pack_grads(): pl.pallas_call(pack_kernel, grid=(rows // step,), out_shape=[jax.ShapeDty...  28.1 us
    pallas_call x1, Pallas kernels, unpack_weights(): pl.pallas_call(unpack_kernel, grid=(rows // step,), out_shape=[jax.ShapeD...  27.2 us
    unnamed x99, local copies, waits for them, and re-layouts  26.4 us
    dot_general x4, matrix products, dot_right_t(): lax.dot_general(left, right, (((1,), (1,)), ((), ())), preferred_element_...  25.4 us
    pallas_call x1, Pallas kernels, attend_back(): pl.pallas_call(functools.partial(attend_back_kernel, scale), grid_spec=pl...  16.4 us

profile of v4, /device:TPU:0, one launch (start us, length us, event | category | flops | bytes accessed | tf_op | source)
XLA Modules:
  0.0 629.7 jit_solution(15851357384887238540)
XLA Ops:
  0.8 2.4 copy.113
  5.2 1.1 concatenate.30.refs_1_
  8.5 139.4 %gather_weights.1 = (bf16[2,16,272,384]{3,2,1,0:T(8,128)(2,1)}, bf16[2,16,272,384]{3,2,1,0:T(8,128)(2,1)}, bf16[2,16,272,384]{3,2,1,0:T(8,128)(2,1)}, bf16[2,16,272,512]{3,2,1,0:T(8,128)(2,1)}) custom-call(bf16[272,384]{1,0:T(8,128)(2,1)} %slice.155.refs_0_, bf16[272,384]{1,0:T(8,128)(2,1)} %concatenate.30.refs_1_, bf16[272,384]{1,0:T(8,128)(2,1)} %slice.165.refs_2_, ...), custom_call_target="tpu_custom_call" | custom-call | tf_op jit(solution)/shard_map/gather_weights/pallas_call | solution.py:409
  147.9 2.9 copy-done.7
  150.8 27.2 %unpack_weights.1 = (bf16[4,272,3264]{2,1,0:T(8,128)(2,1)}, bf16[4,272,1088]{2,1,0:T(8,128)(2,1)S(1)}, bf16[4,272,4352]{2,1,0:T(8,128)(2,1)}, bf16[16,272,1088]{2,1,0:T(8,128)(2,1)}, bf16[4,272,128]{2,1,0:T(8,128)(2,1)S(1)}) custom-call(bf16[2,16,272,384]{3,2,1,0:T(8,128)(2,1)S(1)} %copy-done.7, bf16[2,16,272,384]{3,2,1,0:T(8,128)(2,1)} %get-tuple-element.30.c1, ...), custom_call_target="tpu_custom_call" | custom-call | tf_op jit(solution)/shard_map/unpack_weights/pallas_call | solution.py:583
  178.0 1.5 copy-done.4
  182.3 5.5 convolution_convert_fusion.3
  188.7 1.6 pad.12
  190.3 41.7 %exchange_0.1.x = bf16[8,5,192,128]{3,2,1,0:T(8,128)(2,1)} custom-call(bf16[8,5,192,128]{3,2,1,0:T(8,128)(2,1)} %bitcast.108), custom_call_target="tpu_custom_call" | custom-call | tf_op jit(solution)/shard_map/exchange_0/pallas_call | solution.py:532
  233.5 12.8 %attend.1 = (bf16[8,5,64,128]{3,2,1,0:T(8,128)(2,1)S(1)}, f32[5,1,1024]{2,1,0:T(1,128)S(1)}) custom-call(s32[5,8]{1,0:T(8,128)S(1)} %broadcast_select_fusion.2.order, bf16[8,5,192,128]{3,2,1,0:T(8,128)(2,1)S(1)} %copy-done.2, s32[5,1024,1]{2,1,0:T(8,128)S(1)} %broadcast_select_fusion.seg_k, s32[5,1,1024]{2,1,0:T(1,128)S(1)} %broadcast_select_fusion.1.seg_q), custom_call_target="tpu_custom_call" | custom-call | tf_op jit(solution)/shard_map/attend/pallas_call | solution.py:700
  247.2 24.9 %exchange_1.1 = bf16[8,5,64,128]{3,2,1,0:T(8,128)(2,1)} custom-call(bf16[8,5,64,128]{3,2,1,0:T(8,128)(2,1)} %copy-done.12), custom_call_target="tpu_custom_call" | custom-call | tf_op jit(solution)/shard_map/exchange_1/pallas_call | solution.py:532
  272.1 1.1 slice.201
  273.8 2.6 fusion.28
  276.7 9.9 %multiply_convert_fusion = (bf16[256,4352]{1,0:T(8,128)(2,1)S(1)}, f32[256,4352]{1,0:T(8,128)}) fusion(bf16[1088,4352]{1,0:T(8,128)(2,1)} %bitcast.137, f32[256,1088]{1,0:T(8,128)S(1)} %get-tuple-element.130, f32[1088]{0:T(1024)S(1)} %get-tuple-element.99, f32[1088]{0:T(1024)S(1)} %get-tuple-element.98, f32[256]{0:T(256)S(1)} %add_rsqrt_fusion, ...), kind=kOutput, calls=%fused_computation.15 | convolution fusion | flops 2435727360 | bytes 17279488 | tf_op jit(solution)/shard_map/dot_general | solution.py:87
  286.6 3.1 fusion.6
  289.7 1.1 copy.143
  290.8 1.3 copy.134
  292.1 8.7 %fusion.3 = bf16[256,4352]{1,0:T(8,128)(2,1)S(1)} fusion(f32[256,4352]{1,0:T(8,128)} %get-tuple-element.132, bf16[4352,1088]{1,0:T(8,128)(2,1)} %bitcast.133, bf16[256,1088]{1,0:T(8,128)(2,1)S(1)} %bitcast.102), kind=kOutput, calls=%fused_computation.12 | convolution fusion | flops 2451046400 | bytes 16711680 | tf_op jit(solution)/shard_map/dot_general | solution.py:91
  300.9 8.2 %fusion.29 = (bf16[1088]{0:T(1024)(128)(2,1)S(1)}, f32[256,1088]{0,1:T(8,128)}) fusion(bf16[256,4352]{1,0:T(8,128)(2,1)S(1)} %fusion.3, bf16[1088,4352]{1,0:T(8,128)(2,1)} %bitcast.138), kind=kOutput, calls=%fused_computation.93 | convolution fusion | flops 2424585216 | bytes 12814464 | tf_op jit(solution)/shard_map/dot_general | solution.py:91
  309.0 2.7 copy.136
  311.7 2.3 multiply_reduce_fusion
  314.5 1.0 copy-done.17
  315.6 1.7 convolution_convert_fusion.4
  317.3 1.7 reshape.368
  319.2 0.9 pad.13
  320.1 17.8 %exchange_2.1.g = bf16[8,5,64,128]{3,2,1,0:T(8,128)(2,1)} custom-call(bf16[8,5,64,128]{3,2,1,0:T(8,128)(2,1)} %bitcast.119), custom_call_target="tpu_custom_call" | custom-call | tf_op jit(solution)/shard_map/exchange_2/pallas_call | solution.py:532
  338.0 1.1 copy-done.9
  339.1 16.4 %attend_back.1.blocks = bf16[8,5,192,128]{3,2,1,0:T(8,128)(2,1)S(1)} custom-call(s32[5,8]{1,0:T(8,128)S(1)} %broadcast_select_fusion.2.order, bf16[8,5,192,128]{3,2,1,0:T(8,128)(2,1)S(1)} %copy-done.3, bf16[8,5,64,128]{3,2,1,0:T(8,128)(2,1)S(1)} %copy-done.9, s32[5,1024,1]{2,1,0:T(8,128)} %copy-done.1, s32[5,1,1024]{2,1,0:T(1,128)S(1)} %broadcast_select_fusion.1.seg_q, ...), custom_call_target="tpu_custom_call" | custom-call | tf_op jit(solution)/shard_map/attend_back/pallas_call | solution.py:774
  355.5 1.3 copy-done.6
  356.8 38.9 %exchange_3.1 = bf16[8,5,192,128]{3,2,1,0:T(8,128)(2,1)} custom-call(bf16[8,5,192,128]{3,2,1,0:T(8,128)(2,1)} %copy-done.6), custom_call_target="tpu_custom_call" | custom-call | tf_op jit(solution)/shard_map/exchange_3/pallas_call | solution.py:532
  395.7 1.6 slice.204
  397.3 1.7 copy.138
  399.0 6.8 %fusion.30 = (bf16[1088]{0:T(1024)(128)(2,1)S(1)}, f32[256,1088]{0,1:T(8,128)}) fusion(bf16[1088,3264]{1,0:T(8,128)(2,1)} %bitcast.140, bf16[408,8,2,128]{3,2,1,0:T(2,128)(2,1)S(1)} %bitcast.110), kind=kOutput, calls=%fused_computation.94 | convolution fusion | flops 1818508288 | bytes 9889920 | tf_op jit(solution)/shard_map/dot_general | solution.py:91
  405.8 1.7 copy.139
  408.7 1.3 add_convert_fusion
  410.0 2.2 copy.144
  412.2 6.8 %convolution_convert_fusion.1 = bf16[1088,3264]{1,0:T(8,128)(2,1)} fusion(bf16[256,1088]{1,0:T(8,128)(2,1)S(1)} %bitcast.118, bf16[408,8,2,128]{3,2,1,0:T(2,128)(2,1)} %bitcast.111), kind=kOutput, calls=%fused_computation.1 | convolution fusion | flops 1821782016 | bytes 9330688 | tf_op jit(solution)/shard_map/dot_general | solution.py:95
  421.0 6.5 %convolution_convert_fusion = bf16[1088,4352]{1,0:T(8,128)(2,1)} fusion(bf16[256,4352]{1,0:T(8,128)(2,1)S(1)} %copy-done.29, f32[256,1088]{1,0:T(8,128)S(1)} %copy-done.15, f32[1088]{0:T(1024)S(1)} %get-tuple-element.99, f32[1088]{0:T(1024)S(1)} %get-tuple-element.98, f32[256]{0:T(256)S(1)} %add_rsqrt_fusion, f32[256]{0:T(256)S(1)} %broadcast_multiply_fusion.4), kind=kOutput, calls=%fused_computation | convolution fusion | flops 2430435328 | bytes 12823040 | tf_op jit(solution)/shard_map/dot_general | solution.py:95
  427.5 7.0 %outer.1 = bf16[4352,1088]{1,0:T(8,128)(2,1)S(1)} custom-call(bf16[256,4352]{1,0:T(8,128)(2,1)S(1)} %copy-done.11, bf16[256,1088]{1,0:T(8,128)(2,1)S(1)} %bitcast.103), custom_call_target="tpu_custom_call" | custom-call | flops 2424307712 | bytes 11698176 | tf_op jit(solution)/shard_map/outer/pallas_call | solution.py:642
  434.5 3.8 copy-done
  438.8 28.1 %pack_grads.1 = (bf16[2,16,272,384]{3,2,1,0:T(8,128)(2,1)S(1)}, bf16[2,16,272,384]{3,2,1,0:T(8,128)(2,1)}, bf16[2,16,272,384]{3,2,1,0:T(8,128)(2,1)}, bf16[2,16,272,512]{3,2,1,0:T(8,128)(2,1)}) custom-call(bf16[4,272,3264]{2,1,0:T(8,128)(2,1)} %bitcast.106, bf16[4,272,1088]{2,1,0:T(8,128)(2,1)S(1)} %bitcast.101, bf16[4,272,4352]{2,1,0:T(8,128)(2,1)} %bitcast.105, ...), custom_call_target="tpu_custom_call" | custom-call | tf_op jit(solution)/shard_map/pack_grads/pallas_call | solution.py:617
  466.9 2.7 copy-done.8
  469.6 152.5 %scatter_grads.1 = (bf16[272,384]{1,0:T(8,128)(2,1)}, bf16[272,384]{1,0:T(8,128)(2,1)}, bf16[272,384]{1,0:T(8,128)(2,1)}, bf16[272,512]{1,0:T(8,128)(2,1)}) custom-call(bf16[2,16,272,384]{3,2,1,0:T(8,128)(2,1)} %copy-done.8, bf16[2,16,272,384]{3,2,1,0:T(8,128)(2,1)} %get-tuple-element.41.refs_1_, bf16[2,16,272,384]{3,2,1,0:T(8,128)(2,1)} %get-tuple-element.42.refs_2_, ...), custom_call_target="tpu_custom_call" | custom-call | tf_op jit(solution)/shard_map/scatter_grads/pallas_call | solution.py:502
  622.1 1.0 slice.205
  623.2 1.0 convert_element_type.100
  626.1 0.9 pad_maximum_fusion
  627.1 1.2 copy.146
  628.4 1.0 slice_reduce_fusion
  (163 shorter events, 17.5 us)
Async XLA Ops:
  0.6 2.5 copy-start.33
  0.7 4.5 slice-start.4
  0.7 3.2 slice-start
  0.7 3.3 slice-start.1
  0.7 4.5 slice-start.2
  0.7 4.5 slice-start.3
  0.7 3.4 copy-start.31
  0.7 4.0 copy-start.35
  0.7 4.1 copy-start.36
  0.7 4.2 copy-start.37
  0.8 4.3 copy-start.38
  3.1 3.2 copy-start.32
  147.9 2.9 copy-start.7
  150.8 28.7 %copy-start.40 = (s32[2,1,8]{2,1,0:T(1,128)S(1)}, s32[2,1,8]{2,1,0:T(1,128)}, u32[]{:S(2)}) copy-start(s32[2,1,8]{2,1,0:T(1,128)} %param.23) | copy-start | bytes 196
  178.0 1.5 copy-start.4
  179.4 1.1 copy-start.22
  190.3 41.7 %copy-start.39 = (s32[2,1,8]{2,1,0:T(1,128)S(1)}, s32[2,1,8]{2,1,0:T(1,128)}, u32[]{:S(2)}) copy-start(s32[2,1,8]{2,1,0:T(1,128)} %param.22) | copy-start | bytes 196
  232.0 1.5 copy-start.2
  232.7 13.7 %copy-start.1 = (s32[5,1024,1]{2,1,0:T(8,128)}, s32[5,1024,1]{2,1,0:T(8,128)S(1)}, u32[]{:S(2)}) copy-start(s32[5,1024,1]{2,1,0:T(8,128)S(1)} %broadcast_select_fusion.seg_k) | copy-start | bytes 61444
  246.4 0.8 copy-start.12
  247.2 26.6 %copy-start.5 = (bf16[4,272,1088]{2,1,0:T(8,128)(2,1)S(1)}, bf16[4,272,1088]{2,1,0:T(8,128)(2,1)}, u32[]{:S(2)}) copy-start(bf16[4,272,1088]{2,1,0:T(8,128)(2,1)} %copy-done.4) | copy-start | bytes 7102468
  273.8 2.6 copy-start.24
  276.4 10.2 %copy-start.13 = (f32[256,1088]{1,0:T(8,128)}, f32[256,1088]{1,0:T(8,128)S(1)}, u32[]{:S(2)}) copy-start(f32[256,1088]{1,0:T(8,128)S(1)} %get-tuple-element.130) | copy-start | bytes 3342340
  276.4 10.2 %slice-start.5 = ((s8[10027008]{0:T(1024)(128)(4,1)}), s8[4194304]{0:T(1024)(128)(4,1)S(1)}, s32[]{:S(2)}) async-start(s8[10027008]{0:T(1024)(128)(4,1)} %bitcast.134), calls=%async_computation.5 | async-start | bytes 8388608
  276.7 9.9 %slice-start.6 = ((s8[10027008]{0:T(1024)(128)(4,1)}), s8[4194304]{0:T(1024)(128)(4,1)S(1)}, s32[]{:S(2)}) async-start(s8[10027008]{0:T(1024)(128)(4,1)} %bitcast.134), calls=%async_computation.6 | async-start | bytes 8388608
  276.7 9.9 %slice-start.7 = ((s8[10027008]{0:T(1024)(128)(4,1)}), s8[1638400]{0:T(1024)(128)(4,1)S(1)}, s32[]{:S(2)}) async-start(s8[10027008]{0:T(1024)(128)(4,1)} %bitcast.134), calls=%async_computation.7 | async-start | bytes 3276800
  286.6 3.1 copy-start.10
  300.8 8.2 %copy-start.28 = (bf16[256,4352]{1,0:T(8,128)(2,1)}, bf16[256,4352]{1,0:T(8,128)(2,1)S(1)}, u32[]{:S(2)}) copy-start(bf16[256,4352]{1,0:T(8,128)(2,1)S(1)} %fusion.3) | copy-start | bytes 6684676
  311.7 2.3 copy-start.14
  311.7 2.3 copy-start.20
  314.5 1.0 copy-start.17
  319.0 18.9 %copy-start.3 = (bf16[8,5,192,128]{3,2,1,0:T(8,128)(2,1)S(1)}, bf16[8,5,192,128]{3,2,1,0:T(8,128)(2,1)}, u32[]{:S(2)}) copy-start(bf16[8,5,192,128]{3,2,1,0:T(8,128)(2,1)} %exchange_0.1.x) | copy-start | bytes 5898244
  338.0 1.1 copy-start.9
  355.5 1.3 copy-start.6
  399.0 6.8 %copy-start.23 = (bf16[2,128,3,17,64]{1,0,4,3,2:T(2,128)(2,1)}, bf16[2,128,3,17,64]{1,0,4,3,2:T(2,128)(2,1)S(1)}, u32[]{:S(2)}) copy-start(bf16[2,128,3,17,64]{1,0,4,3,2:T(2,128)(2,1)S(1)} %copy.138) | copy-start | bytes 5013508
  405.8 1.7 copy-start.16
  407.5 1.3 copy-start.18
  410.0 2.2 copy-start.27
  412.2 6.8 %copy-start.19 = (f32[256,1088]{1,0:T(8,128)S(1)}, f32[256,1088]{1,0:T(8,128)}, u32[]{:S(2)}) copy-start(f32[256,1088]{1,0:T(8,128)} %copy-done.17) | copy-start | bytes 3342340
  412.2 6.8 %copy-start.25 = (bf16[2,128,1,17,64]{1,0,4,3,2:T(2,128)(2,1)S(1)}, bf16[2,128,1,17,64]{1,0,4,3,2:T(2,128)(2,1)}, u32[]{:S(2)}) copy-start(bf16[2,128,1,17,64]{1,0,4,3,2:T(2,128)(2,1)} %copy-done.24) | copy-start | bytes 1671172
  419.0 1.3 copy-start.15
  419.0 2.0 copy-start.29
  421.0 6.5 %copy-start.11 = (bf16[256,4352]{1,0:T(8,128)(2,1)S(1)}, bf16[256,4352]{1,0:T(8,128)(2,1)}, u32[]{:S(2)}) copy-start(bf16[256,4352]{1,0:T(8,128)(2,1)} %copy-done.10) | copy-start | bytes 6684676
  434.5 3.8 copy-start
  466.9 2.7 copy-start.8
  622.1 2.9 copy-start.21
  625.0 1.1 copy-start.34
  625.2 1.8 copy-start.30
  (1 other events, 0.8 us)

commit v5 on v4

--- a/solution.py
+++ b/solution.py
@@ -300,8 +300,8 @@
 
 
 MESH = pl.DeviceIdType.MESH
-GATHER_ORDERS = ((2, 3, 0, 1), (2, 3, 1, 0), (2, 3, 0, 1), (2, 3, 1, 0))
-SCATTER_ORDERS = ((2, 3, 0, 1), (2, 3, 1, 0), (0, 2, 3, 1), (1, 3, 2, 0))
+GATHER_ORDERS = ((2, 3, 0, 1), (2, 3, 1, 0), (0, 2, 3, 1), (3, 2, 1, 0))
+SCATTER_ORDERS = GATHER_ORDERS
 ROW_CUTS = ((0, 64), (64, 64), (128, 64), (192, 80))
 CHUNKS = tuple((q, r) for pair in ((0, 1), (2, 3)) for r in range(4) for q in pair)
 GATHER_LAGS = (0, 2, 4, 6, 9)
@@ -310,6 +310,7 @@
 TILE = 128
 LANES = (3 * TILE, 3 * TILE, 3 * TILE, 4 * TILE)
 UNITS = 5
+IDLE = 7
 REM_UP, REM_QKV, REM_OUT, REM_DOWN, REM_NORM = 0, 32, 56, 64, 96
 
 
@@ -512,25 +513,31 @@
     )(*parts)
 
 
-def exchange_kernel(blocks, out, own_sem, send_sem, recv_sem):
+def exchange_kernel(to_owners, blocks, out, own_sem, send_sem, recv_sem):
     dp, seq = lax.axis_index("dp"), lax.axis_index("seq")
     others = [(dp, (seq + k) % 8) for k in range(1, 8)]
     greet(others)
     own = pltpu.make_async_copy(blocks.at[seq], out.at[seq], own_sem)
     copies = [
-        send(blocks.at[device[1]], out.at[seq], send_sem.at[k], recv_sem.at[k], device)
+        pltpu.make_async_remote_copy(
+            src_ref=blocks.at[device[1]], dst_ref=out.at[seq], send_sem=send_sem.at[k],
+            recv_sem=recv_sem.at[k], device_id=device, device_id_type=MESH,
+        )
         for k, device in enumerate(others)
     ]
+    for k, copy in enumerate(copies):
+        pl.when((others[k][1] if to_owners else seq) != IDLE)(copy.start)
     own.start()
     own.wait()
-    for copy in copies:
-        copy.wait()
+    for k, copy in enumerate(copies):
+        pl.when((others[k][1] if to_owners else seq) != IDLE)(copy.wait_send)
+        pl.when((seq if to_owners else (seq + 7 - k) % 8) != IDLE)(copy.wait_recv)
 
 
 def exchange(blocks, which):
     dma = pltpu.SemaphoreType.DMA
     return pl.pallas_call(
-        exchange_kernel,
+        functools.partial(exchange_kernel, which % 2 == 0),
         out_shape=jax.ShapeDtypeStruct(blocks.shape, blocks.dtype),
         in_specs=[pl.BlockSpec(memory_space=pl.ANY)],
         out_specs=pl.BlockSpec(memory_space=pl.ANY),

time: 640 us -> 626 us (0.978)
  Pallas kernels: 507 us -> 493 us
    pallas_call x1, Pallas kernels: 153 us -> 145 us  [scatter_grads(): pl.pallas_call(scatter_kernel, out_shape=[jax.ShapeDtypeStruct((rows, lan...]
where the time goes in v5:
time: 626 us; the launch traced here: 616 us
  Pallas kernels  493 us (79%)
  matrix products  60.6 us (10%)
  local copies, waits for them, and re-layouts  50.3 us (8%)
  other arithmetic  10.2 us (2%)
    pallas_call x1, Pallas kernels, scatter_grads(): pl.pallas_call(scatter_kernel, out_shape=[jax.ShapeDtypeStruct((rows, lan...  145 us
    pallas_call x1, Pallas kernels, gather_weights(): pl.pallas_call(gather_kernel, out_shape=[jax.ShapeDtypeStruct((2, 16, row...  138 us
    pallas_call x4, Pallas kernels, exchange(): pl.pallas_call(functools.partial(exchange_kernel, which % 2 == 0), out_sh...  119 us
    pallas_call x1, Pallas kernels, pack_grads(): pl.pallas_call(pack_kernel, grid=(rows // step,), out_shape=[jax.ShapeDty...  27.9 us
    pallas_call x1, Pallas kernels, unpack_weights(): pl.pallas_call(unpack_kernel, grid=(rows // step,), out_shape=[jax.ShapeD...  27.2 us
    unnamed x99, local copies, waits for them, and re-layouts  26.4 us
    dot_general x4, matrix products, dot_right_t(): lax.dot_general(left, right, (((1,), (1,)), ((), ())), preferred_element_...  25.4 us
    pallas_call x1, Pallas kernels, attend_back(): pl.pallas_call(functools.partial(attend_back_kernel, scale), grid_spec=pl...  16.2 us

profile of v5, /device:TPU:0, one launch (start us, length us, event | category | flops | bytes accessed | tf_op | source)
XLA Modules:
  0.0 615.5 jit_solution(4375818941526648180)
XLA Ops:
  0.8 2.4 copy.113
  5.2 1.1 concatenate.30.refs_1_
  8.5 137.6 %gather_weights.1 = (bf16[2,16,272,384]{3,2,1,0:T(8,128)(2,1)}, bf16[2,16,272,384]{3,2,1,0:T(8,128)(2,1)}, bf16[2,16,272,384]{3,2,1,0:T(8,128)(2,1)}, bf16[2,16,272,512]{3,2,1,0:T(8,128)(2,1)}) custom-call(bf16[272,384]{1,0:T(8,128)(2,1)} %slice.155.refs_0_, bf16[272,384]{1,0:T(8,128)(2,1)} %concatenate.30.refs_1_, bf16[272,384]{1,0:T(8,128)(2,1)} %slice.165.refs_2_, ...), custom_call_target="tpu_custom_call" | custom-call | tf_op jit(solution)/shard_map/gather_weights/pallas_call | solution.py:410
  146.0 2.9 copy-done.7
  148.9 27.2 %unpack_weights.1 = (bf16[4,272,3264]{2,1,0:T(8,128)(2,1)}, bf16[4,272,1088]{2,1,0:T(8,128)(2,1)S(1)}, bf16[4,272,4352]{2,1,0:T(8,128)(2,1)}, bf16[16,272,1088]{2,1,0:T(8,128)(2,1)}, bf16[4,272,128]{2,1,0:T(8,128)(2,1)S(1)}) custom-call(bf16[2,16,272,384]{3,2,1,0:T(8,128)(2,1)S(1)} %copy-done.7, bf16[2,16,272,384]{3,2,1,0:T(8,128)(2,1)} %get-tuple-element.30.c1, ...), custom_call_target="tpu_custom_call" | custom-call | tf_op jit(solution)/shard_map/unpack_weights/pallas_call | solution.py:590
  176.1 1.5 copy-done.4
  180.5 5.5 convolution_convert_fusion.3
  186.9 1.6 pad.12
  188.5 37.7 %exchange_0.1.x = bf16[8,5,192,128]{3,2,1,0:T(8,128)(2,1)} custom-call(bf16[8,5,192,128]{3,2,1,0:T(8,128)(2,1)} %bitcast.108), custom_call_target="tpu_custom_call" | custom-call | tf_op jit(solution)/shard_map/exchange_0/pallas_call | solution.py:539
  227.7 12.6 %attend.1 = (bf16[8,5,64,128]{3,2,1,0:T(8,128)(2,1)S(1)}, f32[5,1,1024]{2,1,0:T(1,128)S(1)}) custom-call(s32[5,8]{1,0:T(8,128)S(1)} %broadcast_select_fusion.2.order, bf16[8,5,192,128]{3,2,1,0:T(8,128)(2,1)S(1)} %copy-done.2, s32[5,1024,1]{2,1,0:T(8,128)S(1)} %broadcast_select_fusion.seg_k, s32[5,1,1024]{2,1,0:T(1,128)S(1)} %broadcast_select_fusion.1.seg_q), custom_call_target="tpu_custom_call" | custom-call | tf_op jit(solution)/shard_map/attend/pallas_call | solution.py:707
  241.1 26.9 %exchange_1.1 = bf16[8,5,64,128]{3,2,1,0:T(8,128)(2,1)} custom-call(bf16[8,5,64,128]{3,2,1,0:T(8,128)(2,1)} %copy-done.12), custom_call_target="tpu_custom_call" | custom-call | tf_op jit(solution)/shard_map/exchange_1/pallas_call | solution.py:539
  268.0 1.1 slice.201
  269.7 2.6 fusion.28
  272.7 9.9 %multiply_convert_fusion = (bf16[256,4352]{1,0:T(8,128)(2,1)S(1)}, f32[256,4352]{1,0:T(8,128)}) fusion(bf16[1088,4352]{1,0:T(8,128)(2,1)} %bitcast.137, f32[256,1088]{1,0:T(8,128)S(1)} %get-tuple-element.130, f32[1088]{0:T(1024)S(1)} %get-tuple-element.99, f32[1088]{0:T(1024)S(1)} %get-tuple-element.98, f32[256]{0:T(256)S(1)} %add_rsqrt_fusion, ...), kind=kOutput, calls=%fused_computation.15 | convolution fusion | flops 2435727360 | bytes 17279488 | tf_op jit(solution)/shard_map/dot_general | solution.py:87
  282.6 3.1 fusion.6
  285.6 1.1 copy.143
  286.7 1.3 copy.134
  288.0 8.7 %fusion.3 = bf16[256,4352]{1,0:T(8,128)(2,1)S(1)} fusion(f32[256,4352]{1,0:T(8,128)} %get-tuple-element.132, bf16[4352,1088]{1,0:T(8,128)(2,1)} %bitcast.133, bf16[256,1088]{1,0:T(8,128)(2,1)S(1)} %bitcast.102), kind=kOutput, calls=%fused_computation.12 | convolution fusion | flops 2451046400 | bytes 16711680 | tf_op jit(solution)/shard_map/dot_general | solution.py:91
  296.8 8.2 %fusion.29 = (bf16[1088]{0:T(1024)(128)(2,1)S(1)}, f32[256,1088]{0,1:T(8,128)}) fusion(bf16[256,4352]{1,0:T(8,128)(2,1)S(1)} %fusion.3, bf16[1088,4352]{1,0:T(8,128)(2,1)} %bitcast.138), kind=kOutput, calls=%fused_computation.93 | convolution fusion | flops 2424585216 | bytes 12814464 | tf_op jit(solution)/shard_map/dot_general | solution.py:91
  305.0 2.7 copy.136
  307.6 2.3 multiply_reduce_fusion
  310.5 1.0 copy-done.17
  311.5 1.7 convolution_convert_fusion.4
  313.2 1.7 reshape.368
  315.1 0.9 pad.13
  316.0 16.5 %exchange_2.1.g = bf16[8,5,64,128]{3,2,1,0:T(8,128)(2,1)} custom-call(bf16[8,5,64,128]{3,2,1,0:T(8,128)(2,1)} %bitcast.119), custom_call_target="tpu_custom_call" | custom-call | tf_op jit(solution)/shard_map/exchange_2/pallas_call | solution.py:539
  332.6 1.1 copy-done.9
  333.7 16.2 %attend_back.1.blocks = bf16[8,5,192,128]{3,2,1,0:T(8,128)(2,1)S(1)} custom-call(s32[5,8]{1,0:T(8,128)S(1)} %broadcast_select_fusion.2.order, bf16[8,5,192,128]{3,2,1,0:T(8,128)(2,1)S(1)} %copy-done.3, bf16[8,5,64,128]{3,2,1,0:T(8,128)(2,1)S(1)} %copy-done.9, s32[5,1024,1]{2,1,0:T(8,128)} %copy-done.1, s32[5,1,1024]{2,1,0:T(1,128)S(1)} %broadcast_select_fusion.1.seg_q, ...), custom_call_target="tpu_custom_call" | custom-call | tf_op jit(solution)/shard_map/attend_back/pallas_call | solution.py:781
  349.9 1.3 copy-done.6
  351.2 37.8 %exchange_3.1 = bf16[8,5,192,128]{3,2,1,0:T(8,128)(2,1)} custom-call(bf16[8,5,192,128]{3,2,1,0:T(8,128)(2,1)} %copy-done.6), custom_call_target="tpu_custom_call" | custom-call | tf_op jit(solution)/shard_map/exchange_3/pallas_call | solution.py:539
  389.1 1.6 slice.204
  390.6 1.7 copy.138
  392.4 6.8 %fusion.30 = (bf16[1088]{0:T(1024)(128)(2,1)S(1)}, f32[256,1088]{0,1:T(8,128)}) fusion(bf16[1088,3264]{1,0:T(8,128)(2,1)} %bitcast.140, bf16[408,8,2,128]{3,2,1,0:T(2,128)(2,1)S(1)} %bitcast.110), kind=kOutput, calls=%fused_computation.94 | convolution fusion | flops 1818508288 | bytes 9889920 | tf_op jit(solution)/shard_map/dot_general | solution.py:91
  399.1 1.7 copy.139
  402.1 1.3 add_convert_fusion
  403.4 2.2 copy.144
  405.6 6.8 %convolution_convert_fusion.1 = bf16[1088,3264]{1,0:T(8,128)(2,1)} fusion(bf16[256,1088]{1,0:T(8,128)(2,1)S(1)} %bitcast.118, bf16[408,8,2,128]{3,2,1,0:T(2,128)(2,1)} %bitcast.111), kind=kOutput, calls=%fused_computation.1 | convolution fusion | flops 1821782016 | bytes 9330688 | tf_op jit(solution)/shard_map/dot_general | solution.py:95
  414.4 6.5 %convolution_convert_fusion = bf16[1088,4352]{1,0:T(8,128)(2,1)} fusion(bf16[256,4352]{1,0:T(8,128)(2,1)S(1)} %copy-done.29, f32[256,1088]{1,0:T(8,128)S(1)} %copy-done.15, f32[1088]{0:T(1024)S(1)} %get-tuple-element.99, f32[1088]{0:T(1024)S(1)} %get-tuple-element.98, f32[256]{0:T(256)S(1)} %add_rsqrt_fusion, f32[256]{0:T(256)S(1)} %broadcast_multiply_fusion.4), kind=kOutput, calls=%fused_computation | convolution fusion | flops 2430435328 | bytes 12823040 | tf_op jit(solution)/shard_map/dot_general | solution.py:95
  420.9 7.2 %outer.1 = bf16[4352,1088]{1,0:T(8,128)(2,1)S(1)} custom-call(bf16[256,4352]{1,0:T(8,128)(2,1)S(1)} %copy-done.11, bf16[256,1088]{1,0:T(8,128)(2,1)S(1)} %bitcast.103), custom_call_target="tpu_custom_call" | custom-call | flops 2424307712 | bytes 11698176 | tf_op jit(solution)/shard_map/outer/pallas_call | solution.py:649
  428.1 3.8 copy-done
  432.3 27.9 %pack_grads.1 = (bf16[2,16,272,384]{3,2,1,0:T(8,128)(2,1)S(1)}, bf16[2,16,272,384]{3,2,1,0:T(8,128)(2,1)}, bf16[2,16,272,384]{3,2,1,0:T(8,128)(2,1)}, bf16[2,16,272,512]{3,2,1,0:T(8,128)(2,1)}) custom-call(bf16[4,272,3264]{2,1,0:T(8,128)(2,1)} %bitcast.106, bf16[4,272,1088]{2,1,0:T(8,128)(2,1)S(1)} %bitcast.101, bf16[4,272,4352]{2,1,0:T(8,128)(2,1)} %bitcast.105, ...), custom_call_target="tpu_custom_call" | custom-call | tf_op jit(solution)/shard_map/pack_grads/pallas_call | solution.py:624
  460.2 2.7 copy-done.8
  462.9 145.0 %scatter_grads.1 = (bf16[272,384]{1,0:T(8,128)(2,1)}, bf16[272,384]{1,0:T(8,128)(2,1)}, bf16[272,384]{1,0:T(8,128)(2,1)}, bf16[272,512]{1,0:T(8,128)(2,1)}) custom-call(bf16[2,16,272,384]{3,2,1,0:T(8,128)(2,1)} %copy-done.8, bf16[2,16,272,384]{3,2,1,0:T(8,128)(2,1)} %get-tuple-element.41.refs_1_, bf16[2,16,272,384]{3,2,1,0:T(8,128)(2,1)} %get-tuple-element.42.refs_2_, ...), custom_call_target="tpu_custom_call" | custom-call | tf_op jit(solution)/shard_map/scatter_grads/pallas_call | solution.py:503
  608.0 1.0 slice.205
  609.0 1.0 convert_element_type.100
  612.0 0.9 pad_maximum_fusion
  613.0 1.2 copy.146
  614.3 1.0 slice_reduce_fusion
  (163 shorter events, 17.5 us)
Async XLA Ops:
  0.6 2.5 copy-start.33
  0.7 4.5 slice-start.4
  0.7 3.2 slice-start
  0.7 3.3 slice-start.1
  0.7 4.5 slice-start.2
  0.7 4.5 slice-start.3
  0.7 3.4 copy-start.31
  0.7 4.0 copy-start.35
  0.7 4.1 copy-start.36
  0.7 4.2 copy-start.37
  0.8 4.3 copy-start.38
  3.1 3.2 copy-start.32
  146.0 2.9 copy-start.7
  148.9 28.7 %copy-start.40 = (s32[2,1,8]{2,1,0:T(1,128)S(1)}, s32[2,1,8]{2,1,0:T(1,128)}, u32[]{:S(2)}) copy-start(s32[2,1,8]{2,1,0:T(1,128)} %param.23) | copy-start | bytes 196
  176.1 1.5 copy-start.4
  177.6 1.1 copy-start.22
  188.4 37.7 %copy-start.39 = (s32[2,1,8]{2,1,0:T(1,128)S(1)}, s32[2,1,8]{2,1,0:T(1,128)}, u32[]{:S(2)}) copy-start(s32[2,1,8]{2,1,0:T(1,128)} %param.22) | copy-start | bytes 196
  226.1 1.5 copy-start.2
  226.8 13.5 %copy-start.1 = (s32[5,1024,1]{2,1,0:T(8,128)}, s32[5,1024,1]{2,1,0:T(8,128)S(1)}, u32[]{:S(2)}) copy-start(s32[5,1024,1]{2,1,0:T(8,128)S(1)} %broadcast_select_fusion.seg_k) | copy-start | bytes 61444
  240.3 0.8 copy-start.12
  241.1 28.6 %copy-start.5 = (bf16[4,272,1088]{2,1,0:T(8,128)(2,1)S(1)}, bf16[4,272,1088]{2,1,0:T(8,128)(2,1)}, u32[]{:S(2)}) copy-start(bf16[4,272,1088]{2,1,0:T(8,128)(2,1)} %copy-done.4) | copy-start | bytes 7102468
  269.7 2.6 copy-start.24
  272.3 10.2 %copy-start.13 = (f32[256,1088]{1,0:T(8,128)}, f32[256,1088]{1,0:T(8,128)S(1)}, u32[]{:S(2)}) copy-start(f32[256,1088]{1,0:T(8,128)S(1)} %get-tuple-element.130) | copy-start | bytes 3342340
  272.4 10.2 %slice-start.5 = ((s8[10027008]{0:T(1024)(128)(4,1)}), s8[4194304]{0:T(1024)(128)(4,1)S(1)}, s32[]{:S(2)}) async-start(s8[10027008]{0:T(1024)(128)(4,1)} %bitcast.134), calls=%async_computation.5 | async-start | bytes 8388608
  272.6 9.9 %slice-start.6 = ((s8[10027008]{0:T(1024)(128)(4,1)}), s8[4194304]{0:T(1024)(128)(4,1)S(1)}, s32[]{:S(2)}) async-start(s8[10027008]{0:T(1024)(128)(4,1)} %bitcast.134), calls=%async_computation.6 | async-start | bytes 8388608
  272.6 9.9 %slice-start.7 = ((s8[10027008]{0:T(1024)(128)(4,1)}), s8[1638400]{0:T(1024)(128)(4,1)S(1)}, s32[]{:S(2)}) async-start(s8[10027008]{0:T(1024)(128)(4,1)} %bitcast.134), calls=%async_computation.7 | async-start | bytes 3276800
  282.5 3.1 copy-start.10
  296.8 8.2 %copy-start.28 = (bf16[256,4352]{1,0:T(8,128)(2,1)}, bf16[256,4352]{1,0:T(8,128)(2,1)S(1)}, u32[]{:S(2)}) copy-start(bf16[256,4352]{1,0:T(8,128)(2,1)S(1)} %fusion.3) | copy-start | bytes 6684676
  307.6 2.3 copy-start.14
  307.6 2.3 copy-start.20
  310.5 1.0 copy-start.17
  315.0 17.6 %copy-start.3 = (bf16[8,5,192,128]{3,2,1,0:T(8,128)(2,1)S(1)}, bf16[8,5,192,128]{3,2,1,0:T(8,128)(2,1)}, u32[]{:S(2)}) copy-start(bf16[8,5,192,128]{3,2,1,0:T(8,128)(2,1)} %exchange_0.1.x) | copy-start | bytes 5898244
  332.6 1.1 copy-start.9
  349.9 1.3 copy-start.6
  392.4 6.8 %copy-start.23 = (bf16[2,128,3,17,64]{1,0,4,3,2:T(2,128)(2,1)}, bf16[2,128,3,17,64]{1,0,4,3,2:T(2,128)(2,1)S(1)}, u32[]{:S(2)}) copy-start(bf16[2,128,3,17,64]{1,0,4,3,2:T(2,128)(2,1)S(1)} %copy.138) | copy-start | bytes 5013508
  399.1 1.7 copy-start.16
  400.9 1.3 copy-start.18
  403.4 2.2 copy-start.27
  405.6 6.8 %copy-start.19 = (f32[256,1088]{1,0:T(8,128)S(1)}, f32[256,1088]{1,0:T(8,128)}, u32[]{:S(2)}) copy-start(f32[256,1088]{1,0:T(8,128)} %copy-done.17) | copy-start | bytes 3342340
  405.6 6.8 %copy-start.25 = (bf16[2,128,1,17,64]{1,0,4,3,2:T(2,128)(2,1)S(1)}, bf16[2,128,1,17,64]{1,0,4,3,2:T(2,128)(2,1)}, u32[]{:S(2)}) copy-start(bf16[2,128,1,17,64]{1,0,4,3,2:T(2,128)(2,1)} %copy-done.24) | copy-start | bytes 1671172
  412.4 1.3 copy-start.15
  412.4 2.0 copy-start.29
  414.4 6.5 %copy-start.11 = (bf16[256,4352]{1,0:T(8,128)(2,1)S(1)}, bf16[256,4352]{1,0:T(8,128)(2,1)}, u32[]{:S(2)}) copy-start(bf16[256,4352]{1,0:T(8,128)(2,1)} %copy-done.10) | copy-start | bytes 6684676
  428.1 3.8 copy-start
  460.2 2.7 copy-start.8
  608.0 2.9 copy-start.21
  610.8 1.1 copy-start.34
  611.0 1.8 copy-start.30
  (1 other events, 0.8 us)

commit v6 on v5

--- a/solution.py
+++ b/solution.py
@@ -302,8 +302,9 @@
 MESH = pl.DeviceIdType.MESH
 GATHER_ORDERS = ((2, 3, 0, 1), (2, 3, 1, 0), (0, 2, 3, 1), (3, 2, 1, 0))
 SCATTER_ORDERS = GATHER_ORDERS
-ROW_CUTS = ((0, 64), (64, 64), (128, 64), (192, 80))
-CHUNKS = tuple((q, r) for pair in ((0, 1), (2, 3)) for r in range(4) for q in pair)
+ROW_CUTS = ((0, 96), (96, 80), (176, 64), (240, 32))
+GATHER_CHUNKS = tuple((q, r) for r in range(4) for q in range(4))
+SCATTER_CHUNKS = tuple((q, r) for r in reversed(range(4)) for q in range(4))
 GATHER_LAGS = (0, 2, 4, 6, 9)
 SCATTER_LAGS = (0, 3, 5, 7, 9)
 AHEAD = 4
@@ -363,7 +364,7 @@
     owns, links, sides = {}, {}, []
 
     def step(chunk, stage):
-        q, r = CHUNKS[chunk]
+        q, r = GATHER_CHUNKS[chunk]
         span = pl.ds(*ROW_CUTS[r])
         size = 2**stage
         if stage == 0:
@@ -394,10 +395,10 @@
             send(got, got, sib_send.at[chunk, stage], sib_recv.at[chunk, stage], sibling())
         )
 
-    for turn in range(len(CHUNKS) + GATHER_LAGS[4]):
+    for turn in range(len(GATHER_CHUNKS) + GATHER_LAGS[4]):
         for stage in (4, 3, 2, 1, 0):
             lag = GATHER_LAGS[stage]
-            if 0 <= turn - lag < len(CHUNKS):
+            if 0 <= turn - lag < len(GATHER_CHUNKS):
                 step(turn - lag, stage)
     for side in sides:
         side.wait()
@@ -430,7 +431,7 @@
     side, load, links = {}, {}, {}
 
     def begin(chunk):
-        q, r = CHUNKS[chunk]
+        q, r = SCATTER_CHUNKS[chunk]
         rows = pl.ds(*ROW_CUTS[r])
         side[chunk] = send(
             parts[q].at[1 - core, :, rows], acc[q].at[:, rows],
@@ -445,7 +446,7 @@
         begin(chunk)
 
     def add(chunk, base, other, other_base, count):
-        q, r = CHUNKS[chunk]
+        q, r = SCATTER_CHUNKS[chunk]
         rows = pl.ds(*ROW_CUTS[r])
 
         def one(b, carry):
@@ -455,7 +456,7 @@
         lax.fori_loop(0, count, one, 0)
 
     def step(chunk, stage):
-        q, r = CHUNKS[chunk]
+        q, r = SCATTER_CHUNKS[chunk]
         rows = pl.ds(*ROW_CUTS[r])
         half = 2**stage
         base = at[q] // (2 * half) * (2 * half)
@@ -475,17 +476,17 @@
         )
         add(chunk, base + keep, other, keep, half)
 
-    for turn in range(len(CHUNKS) + SCATTER_LAGS[4]):
-        if turn + AHEAD < len(CHUNKS):
+    for turn in range(len(SCATTER_CHUNKS) + SCATTER_LAGS[4]):
+        if turn + AHEAD < len(SCATTER_CHUNKS):
             begin(turn + AHEAD)
         for stage in (-1, 0, 1, 2, 3):
             lag = SCATTER_LAGS[3 - stage]
             chunk = turn - lag
-            if 0 <= chunk < len(CHUNKS):
+            if 0 <= chunk < len(SCATTER_CHUNKS):
                 if stage >= 0:
                     step(chunk, stage)
                     continue
-                q, r = CHUNKS[chunk]
+                q, r = SCATTER_CHUNKS[chunk]
                 rows = pl.ds(*ROW_CUTS[r])
                 links[chunk, 0].wait_recv()
                 outs[q][rows] = acc[q][at[q], rows] + got0[q][0, rows]

time: 626 us -> 638 us (1.019)
  Pallas kernels: 493 us -> 505 us
    pallas_call x1, Pallas kernels: 145 us -> 155 us  [scatter_grads(): pl.pallas_call(scatter_kernel, out_shape=[jax.ShapeDtypeStruct((rows, lan...]
    pallas_call x1, Pallas kernels: 138 us -> 145 us  [gather_weights(): pl.pallas_call(gather_kernel, out_shape=[jax.ShapeDtypeStruct((2, 16, row...]
where the time goes in v6:
time: 638 us; the launch traced here: 628 us
  Pallas kernels  505 us (79%)
  matrix products  60.6 us (9%)
  local copies, waits for them, and re-layouts  50.3 us (8%)
  other arithmetic  10.2 us (2%)
    pallas_call x1, Pallas kernels, scatter_grads(): pl.pallas_call(scatter_kernel, out_shape=[jax.ShapeDtypeStruct((rows, lan...  155 us
    pallas_call x1, Pallas kernels, gather_weights(): pl.pallas_call(gather_kernel, out_shape=[jax.ShapeDtypeStruct((2, 16, row...  145 us
    pallas_call x4, Pallas kernels, exchange(): pl.pallas_call(functools.partial(exchange_kernel, which % 2 == 0), out_sh...  114 us
    pallas_call x1, Pallas kernels, pack_grads(): pl.pallas_call(pack_kernel, grid=(rows // step,), out_shape=[jax.ShapeDty...  27.9 us
    pallas_call x1, Pallas kernels, unpack_weights(): pl.pallas_call(unpack_kernel, grid=(rows // step,), out_shape=[jax.ShapeD...  27.2 us
    unnamed x99, local copies, waits for them, and re-layouts  26.4 us
    dot_general x4, matrix products, dot_right_t(): lax.dot_general(left, right, (((1,), (1,)), ((), ())), preferred_element_...  25.4 us
    pallas_call x1, Pallas kernels, attend_back(): pl.pallas_call(functools.partial(attend_back_kernel, scale), grid_spec=pl...  16.2 us

profile of v6, /device:TPU:0, one launch (start us, length us, event | category | flops | bytes accessed | tf_op | source)
XLA Modules:
  0.0 628.3 jit_solution(17757216278280399278)
XLA Ops:
  0.8 2.4 copy.113
  5.2 1.1 concatenate.30.refs_1_
  8.5 145.5 %gather_weights.1 = (bf16[2,16,272,384]{3,2,1,0:T(8,128)(2,1)}, bf16[2,16,272,384]{3,2,1,0:T(8,128)(2,1)}, bf16[2,16,272,384]{3,2,1,0:T(8,128)(2,1)}, bf16[2,16,272,512]{3,2,1,0:T(8,128)(2,1)}) custom-call(bf16[272,384]{1,0:T(8,128)(2,1)} %slice.155.refs_0_, bf16[272,384]{1,0:T(8,128)(2,1)} %concatenate.30.refs_1_, bf16[272,384]{1,0:T(8,128)(2,1)} %slice.165.refs_2_, ...), custom_call_target="tpu_custom_call" | custom-call | tf_op jit(solution)/shard_map/gather_weights/pallas_call | solution.py:411
  154.0 2.9 copy-done.7
  156.8 27.2 %unpack_weights.1 = (bf16[4,272,3264]{2,1,0:T(8,128)(2,1)}, bf16[4,272,1088]{2,1,0:T(8,128)(2,1)S(1)}, bf16[4,272,4352]{2,1,0:T(8,128)(2,1)}, bf16[16,272,1088]{2,1,0:T(8,128)(2,1)}, bf16[4,272,128]{2,1,0:T(8,128)(2,1)S(1)}) custom-call(bf16[2,16,272,384]{3,2,1,0:T(8,128)(2,1)S(1)} %copy-done.7, bf16[2,16,272,384]{3,2,1,0:T(8,128)(2,1)} %get-tuple-element.30.c1, ...), custom_call_target="tpu_custom_call" | custom-call | tf_op jit(solution)/shard_map/unpack_weights/pallas_call | solution.py:591
  184.0 1.5 copy-done.4
  188.4 5.5 convolution_convert_fusion.3
  194.8 1.6 pad.12
  196.4 32.9 %exchange_0.1.x = bf16[8,5,192,128]{3,2,1,0:T(8,128)(2,1)} custom-call(bf16[8,5,192,128]{3,2,1,0:T(8,128)(2,1)} %bitcast.108), custom_call_target="tpu_custom_call" | custom-call | tf_op jit(solution)/shard_map/exchange_0/pallas_call | solution.py:540
  230.8 12.6 %attend.1 = (bf16[8,5,64,128]{3,2,1,0:T(8,128)(2,1)S(1)}, f32[5,1,1024]{2,1,0:T(1,128)S(1)}) custom-call(s32[5,8]{1,0:T(8,128)S(1)} %broadcast_select_fusion.2.order, bf16[8,5,192,128]{3,2,1,0:T(8,128)(2,1)S(1)} %copy-done.2, s32[5,1024,1]{2,1,0:T(8,128)S(1)} %broadcast_select_fusion.seg_k, s32[5,1,1024]{2,1,0:T(1,128)S(1)} %broadcast_select_fusion.1.seg_q), custom_call_target="tpu_custom_call" | custom-call | tf_op jit(solution)/shard_map/attend/pallas_call | solution.py:708
  244.2 26.9 %exchange_1.1 = bf16[8,5,64,128]{3,2,1,0:T(8,128)(2,1)} custom-call(bf16[8,5,64,128]{3,2,1,0:T(8,128)(2,1)} %copy-done.12), custom_call_target="tpu_custom_call" | custom-call | tf_op jit(solution)/shard_map/exchange_1/pallas_call | solution.py:540
  271.1 1.1 slice.201
  272.8 2.6 fusion.28
  275.7 9.9 %multiply_convert_fusion = (bf16[256,4352]{1,0:T(8,128)(2,1)S(1)}, f32[256,4352]{1,0:T(8,128)}) fusion(bf16[1088,4352]{1,0:T(8,128)(2,1)} %bitcast.137, f32[256,1088]{1,0:T(8,128)S(1)} %get-tuple-element.130, f32[1088]{0:T(1024)S(1)} %get-tuple-element.99, f32[1088]{0:T(1024)S(1)} %get-tuple-element.98, f32[256]{0:T(256)S(1)} %add_rsqrt_fusion, ...), kind=kOutput, calls=%fused_computation.15 | convolution fusion | flops 2435727360 | bytes 17279488 | tf_op jit(solution)/shard_map/dot_general | solution.py:87
  285.6 3.0 fusion.6
  288.7 1.1 copy.143
  289.8 1.3 copy.134
  291.1 8.7 %fusion.3 = bf16[256,4352]{1,0:T(8,128)(2,1)S(1)} fusion(f32[256,4352]{1,0:T(8,128)} %get-tuple-element.132, bf16[4352,1088]{1,0:T(8,128)(2,1)} %bitcast.133, bf16[256,1088]{1,0:T(8,128)(2,1)S(1)} %bitcast.102), kind=kOutput, calls=%fused_computation.12 | convolution fusion | flops 2451046400 | bytes 16711680 | tf_op jit(solution)/shard_map/dot_general | solution.py:91
  299.9 8.2 %fusion.29 = (bf16[1088]{0:T(1024)(128)(2,1)S(1)}, f32[256,1088]{0,1:T(8,128)}) fusion(bf16[256,4352]{1,0:T(8,128)(2,1)S(1)} %fusion.3, bf16[1088,4352]{1,0:T(8,128)(2,1)} %bitcast.138), kind=kOutput, calls=%fused_computation.93 | convolution fusion | flops 2424585216 | bytes 12814464 | tf_op jit(solution)/shard_map/dot_general | solution.py:91
  308.0 2.7 copy.136
  310.7 2.3 multiply_reduce_fusion
  313.5 1.0 copy-done.17
  314.6 1.7 convolution_convert_fusion.4
  316.3 1.7 reshape.368
  318.2 0.9 pad.13
  319.1 16.5 %exchange_2.1.g = bf16[8,5,64,128]{3,2,1,0:T(8,128)(2,1)} custom-call(bf16[8,5,64,128]{3,2,1,0:T(8,128)(2,1)} %bitcast.119), custom_call_target="tpu_custom_call" | custom-call | tf_op jit(solution)/shard_map/exchange_2/pallas_call | solution.py:540
  335.7 1.1 copy-done.9
  336.7 16.2 %attend_back.1.blocks = bf16[8,5,192,128]{3,2,1,0:T(8,128)(2,1)S(1)} custom-call(s32[5,8]{1,0:T(8,128)S(1)} %broadcast_select_fusion.2.order, bf16[8,5,192,128]{3,2,1,0:T(8,128)(2,1)S(1)} %copy-done.3, bf16[8,5,64,128]{3,2,1,0:T(8,128)(2,1)S(1)} %copy-done.9, s32[5,1024,1]{2,1,0:T(8,128)} %copy-done.1, s32[5,1,1024]{2,1,0:T(1,128)S(1)} %broadcast_select_fusion.1.seg_q, ...), custom_call_target="tpu_custom_call" | custom-call | tf_op jit(solution)/shard_map/attend_back/pallas_call | solution.py:782
  353.0 1.3 copy-done.6
  354.3 37.8 %exchange_3.1 = bf16[8,5,192,128]{3,2,1,0:T(8,128)(2,1)} custom-call(bf16[8,5,192,128]{3,2,1,0:T(8,128)(2,1)} %copy-done.6), custom_call_target="tpu_custom_call" | custom-call | tf_op jit(solution)/shard_map/exchange_3/pallas_call | solution.py:540
  392.1 1.6 slice.204
  393.7 1.7 copy.138
  395.4 6.7 %fusion.30 = (bf16[1088]{0:T(1024)(128)(2,1)S(1)}, f32[256,1088]{0,1:T(8,128)}) fusion(bf16[1088,3264]{1,0:T(8,128)(2,1)} %bitcast.140, bf16[408,8,2,128]{3,2,1,0:T(2,128)(2,1)S(1)} %bitcast.110), kind=kOutput, calls=%fused_computation.94 | convolution fusion | flops 1818508288 | bytes 9889920 | tf_op jit(solution)/shard_map/dot_general | solution.py:91
  402.2 1.7 copy.139
  405.2 1.3 add_convert_fusion
  406.4 2.2 copy.144
  408.6 6.8 %convolution_convert_fusion.1 = bf16[1088,3264]{1,0:T(8,128)(2,1)} fusion(bf16[256,1088]{1,0:T(8,128)(2,1)S(1)} %bitcast.118, bf16[408,8,2,128]{3,2,1,0:T(2,128)(2,1)} %bitcast.111), kind=kOutput, calls=%fused_computation.1 | convolution fusion | flops 1821782016 | bytes 9330688 | tf_op jit(solution)/shard_map/dot_general | solution.py:95
  417.4 6.5 %convolution_convert_fusion = bf16[1088,4352]{1,0:T(8,128)(2,1)} fusion(bf16[256,4352]{1,0:T(8,128)(2,1)S(1)} %copy-done.29, f32[256,1088]{1,0:T(8,128)S(1)} %copy-done.15, f32[1088]{0:T(1024)S(1)} %get-tuple-element.99, f32[1088]{0:T(1024)S(1)} %get-tuple-element.98, f32[256]{0:T(256)S(1)} %add_rsqrt_fusion, f32[256]{0:T(256)S(1)} %broadcast_multiply_fusion.4), kind=kOutput, calls=%fused_computation | convolution fusion | flops 2430435328 | bytes 12823040 | tf_op jit(solution)/shard_map/dot_general | solution.py:95
  424.0 7.2 %outer.1 = bf16[4352,1088]{1,0:T(8,128)(2,1)S(1)} custom-call(bf16[256,4352]{1,0:T(8,128)(2,1)S(1)} %copy-done.11, bf16[256,1088]{1,0:T(8,128)(2,1)S(1)} %bitcast.103), custom_call_target="tpu_custom_call" | custom-call | flops 2424307712 | bytes 11698176 | tf_op jit(solution)/shard_map/outer/pallas_call | solution.py:650
  431.1 3.8 copy-done
  435.4 27.9 %pack_grads.1 = (bf16[2,16,272,384]{3,2,1,0:T(8,128)(2,1)S(1)}, bf16[2,16,272,384]{3,2,1,0:T(8,128)(2,1)}, bf16[2,16,272,384]{3,2,1,0:T(8,128)(2,1)}, bf16[2,16,272,512]{3,2,1,0:T(8,128)(2,1)}) custom-call(bf16[4,272,3264]{2,1,0:T(8,128)(2,1)} %bitcast.106, bf16[4,272,1088]{2,1,0:T(8,128)(2,1)S(1)} %bitcast.101, bf16[4,272,4352]{2,1,0:T(8,128)(2,1)} %bitcast.105, ...), custom_call_target="tpu_custom_call" | custom-call | tf_op jit(solution)/shard_map/pack_grads/pallas_call | solution.py:625
  463.3 2.7 copy-done.8
  466.0 154.7 %scatter_grads.1 = (bf16[272,384]{1,0:T(8,128)(2,1)}, bf16[272,384]{1,0:T(8,128)(2,1)}, bf16[272,384]{1,0:T(8,128)(2,1)}, bf16[272,512]{1,0:T(8,128)(2,1)}) custom-call(bf16[2,16,272,384]{3,2,1,0:T(8,128)(2,1)} %copy-done.8, bf16[2,16,272,384]{3,2,1,0:T(8,128)(2,1)} %get-tuple-element.41.refs_1_, bf16[2,16,272,384]{3,2,1,0:T(8,128)(2,1)} %get-tuple-element.42.refs_2_, ...), custom_call_target="tpu_custom_call" | custom-call | tf_op jit(solution)/shard_map/scatter_grads/pallas_call | solution.py:504
  620.8 1.0 slice.205
  621.8 1.0 convert_element_type.100
  624.7 0.9 pad_maximum_fusion
  625.8 1.2 copy.146
  627.1 1.0 slice_reduce_fusion
  (163 shorter events, 17.5 us)
Async XLA Ops:
  0.6 2.5 copy-start.33
  0.7 4.5 slice-start.4
  0.7 3.2 slice-start
  0.7 3.3 slice-start.1
  0.7 4.5 slice-start.2
  0.7 4.5 slice-start.3
  0.7 3.4 copy-start.31
  0.7 4.0 copy-start.35
  0.7 4.1 copy-start.36
  0.7 4.2 copy-start.37
  0.8 4.3 copy-start.38
  3.1 3.2 copy-start.32
  153.9 2.9 copy-start.7
  156.8 28.7 %copy-start.40 = (s32[2,1,8]{2,1,0:T(1,128)S(1)}, s32[2,1,8]{2,1,0:T(1,128)}, u32[]{:S(2)}) copy-start(s32[2,1,8]{2,1,0:T(1,128)} %param.23) | copy-start | bytes 196
  184.0 1.5 copy-start.4
  185.5 1.1 copy-start.22
  196.4 32.9 %copy-start.39 = (s32[2,1,8]{2,1,0:T(1,128)S(1)}, s32[2,1,8]{2,1,0:T(1,128)}, u32[]{:S(2)}) copy-start(s32[2,1,8]{2,1,0:T(1,128)} %param.22) | copy-start | bytes 196
  229.2 1.5 copy-start.2
  229.9 13.5 %copy-start.1 = (s32[5,1024,1]{2,1,0:T(8,128)}, s32[5,1024,1]{2,1,0:T(8,128)S(1)}, u32[]{:S(2)}) copy-start(s32[5,1024,1]{2,1,0:T(8,128)S(1)} %broadcast_select_fusion.seg_k) | copy-start | bytes 61444
  243.4 0.8 copy-start.12
  244.2 28.6 %copy-start.5 = (bf16[4,272,1088]{2,1,0:T(8,128)(2,1)S(1)}, bf16[4,272,1088]{2,1,0:T(8,128)(2,1)}, u32[]{:S(2)}) copy-start(bf16[4,272,1088]{2,1,0:T(8,128)(2,1)} %copy-done.4) | copy-start | bytes 7102468
  272.8 2.6 copy-start.24
  275.4 10.2 %copy-start.13 = (f32[256,1088]{1,0:T(8,128)}, f32[256,1088]{1,0:T(8,128)S(1)}, u32[]{:S(2)}) copy-start(f32[256,1088]{1,0:T(8,128)S(1)} %get-tuple-element.130) | copy-start | bytes 3342340
  275.4 10.2 %slice-start.5 = ((s8[10027008]{0:T(1024)(128)(4,1)}), s8[4194304]{0:T(1024)(128)(4,1)S(1)}, s32[]{:S(2)}) async-start(s8[10027008]{0:T(1024)(128)(4,1)} %bitcast.134), calls=%async_computation.5 | async-start | bytes 8388608
  275.7 9.9 %slice-start.6 = ((s8[10027008]{0:T(1024)(128)(4,1)}), s8[4194304]{0:T(1024)(128)(4,1)S(1)}, s32[]{:S(2)}) async-start(s8[10027008]{0:T(1024)(128)(4,1)} %bitcast.134), calls=%async_computation.6 | async-start | bytes 8388608
  275.7 9.9 %slice-start.7 = ((s8[10027008]{0:T(1024)(128)(4,1)}), s8[1638400]{0:T(1024)(128)(4,1)S(1)}, s32[]{:S(2)}) async-start(s8[10027008]{0:T(1024)(128)(4,1)} %bitcast.134), calls=%async_computation.7 | async-start | bytes 3276800
  285.6 3.1 copy-start.10
  299.8 8.2 %copy-start.28 = (bf16[256,4352]{1,0:T(8,128)(2,1)}, bf16[256,4352]{1,0:T(8,128)(2,1)S(1)}, u32[]{:S(2)}) copy-start(bf16[256,4352]{1,0:T(8,128)(2,1)S(1)} %fusion.3) | copy-start | bytes 6684676
  310.7 2.3 copy-start.14
  310.7 2.3 copy-start.20
  313.5 1.0 copy-start.17
  318.1 17.6 %copy-start.3 = (bf16[8,5,192,128]{3,2,1,0:T(8,128)(2,1)S(1)}, bf16[8,5,192,128]{3,2,1,0:T(8,128)(2,1)}, u32[]{:S(2)}) copy-start(bf16[8,5,192,128]{3,2,1,0:T(8,128)(2,1)} %exchange_0.1.x) | copy-start | bytes 5898244
  335.7 1.1 copy-start.9
  353.0 1.3 copy-start.6
  395.4 6.8 %copy-start.23 = (bf16[2,128,3,17,64]{1,0,4,3,2:T(2,128)(2,1)}, bf16[2,128,3,17,64]{1,0,4,3,2:T(2,128)(2,1)S(1)}, u32[]{:S(2)}) copy-start(bf16[2,128,3,17,64]{1,0,4,3,2:T(2,128)(2,1)S(1)} %copy.138) | copy-start | bytes 5013508
  402.2 1.7 copy-start.16
  403.9 1.3 copy-start.18
  406.4 2.2 copy-start.27
  408.6 6.8 %copy-start.19 = (f32[256,1088]{1,0:T(8,128)S(1)}, f32[256,1088]{1,0:T(8,128)}, u32[]{:S(2)}) copy-start(f32[256,1088]{1,0:T(8,128)} %copy-done.17) | copy-start | bytes 3342340
  408.6 6.8 %copy-start.25 = (bf16[2,128,1,17,64]{1,0,4,3,2:T(2,128)(2,1)S(1)}, bf16[2,128,1,17,64]{1,0,4,3,2:T(2,128)(2,1)}, u32[]{:S(2)}) copy-start(bf16[2,128,1,17,64]{1,0,4,3,2:T(2,128)(2,1)} %copy-done.24) | copy-start | bytes 1671172
  415.4 1.3 copy-start.15
  415.4 2.0 copy-start.29
  417.4 6.5 %copy-start.11 = (bf16[256,4352]{1,0:T(8,128)(2,1)S(1)}, bf16[256,4352]{1,0:T(8,128)(2,1)}, u32[]{:S(2)}) copy-start(bf16[256,4352]{1,0:T(8,128)(2,1)} %copy-done.10) | copy-start | bytes 6684676
  431.1 3.8 copy-start
  463.3 2.7 copy-start.8
  620.8 2.9 copy-start.21
  623.6 1.1 copy-start.34
  623.8 1.8 copy-start.30
  (1 other events, 0.8 us)
